TPU v7x, 32 devices: a whole 2x2x4 slice. The times are simulated.
32 devices in a mesh: seq: 16 (over z, y, x), head: 2 (over core).
Axes of the slice: x: 2, y: 2, z: 4, core: 2. Of those that a mesh axis runs over, the one named last changes fastest.
Arguments:
- queries: bfloat16 [4096, 4096], P('seq', 'head'), may hold values from -6 to 6
- key_rows: bfloat16 [4096, 4096], P('seq', 'head'), may hold values from -6 to 6
- value_rows: bfloat16 [4096, 4096], P('seq', 'head'), may hold values from -180 to 180
- window: int32 [64, 12], P('seq'), may hold values from 0 to 63, as said below
- random_blocks: int32 [64, 3], P('seq'), may hold values from 0 to 63, as said below
- global_blocks: int32 [2], replicated, may hold values from 0 to 63, as said below
- norm_gain: float32 [4096], P('head'), may hold values from 0.25 to 1.75
Outputs:
- normed: bfloat16 [4096, 4096], P('seq', 'head')
Inputs may be any that keep to these rules, and one draw needn't show every extreme that they name: `window`: row b names 12 distinct blocks, each with (id - b) mod 64 within 8 of 0 either way around the circle; b itself, b - 8 and b + 8 (mod 64) are always among them. `random_blocks`: shard s holds blocks s * 4 to s * 4 + 3. The 12 entries of the rows of one device name each shard at most 1 times; one shard is named exactly 1 times by the rows of every device. `global_blocks`: distinct blocks; one of them is the last block of the sequence, 63.
All inputs are finite; a program needn't handle non-finite values.
Results may differ from a plain program's by a relative error of at most 0.0045.
Values may be sent and summed in bfloat16 or wider, within the bound.
No kernel may reach another device: no remote copies, remote signals or barrier semaphores. Data moves between devices by JAX's collectives and lax.ppermute only.
A program may use at most 128 MiB of HBM per device.

v0:
```python
from functools import partial

import jax
import jax.numpy as jnp
from jax import lax
from jax.sharding import PartitionSpec as P

HD = 128
D = 4096
BLK = 64


def from_behind(shard, axis, by):
    peers = lax.axis_size(axis)
    return lax.ppermute(shard, axis, [(i, (i + by) % peers) for i in range(peers)])


def source_part(query_set, key_set, value_set, head_count):
    item_count, row_count, row_width = query_set.shape
    head_size = row_width // head_count
    query_heads = query_set.reshape(item_count, row_count, head_count, head_size)
    key_heads = key_set.reshape(item_count, key_set.shape[1], head_count, head_size)
    value_heads = value_set.reshape(item_count, value_set.shape[1], head_count, head_size)
    scores = jnp.einsum(
        "nqhd,nkhd->nhqk", query_heads, key_heads, preferred_element_type=jnp.float32
    ) * head_size ** (-0.5)
    maxima = jnp.max(scores, axis=-1)
    lifted = jnp.exp(scores - maxima[..., None])
    totals = jnp.sum(lifted, axis=-1)
    weights = lifted.astype(jnp.bfloat16)
    summed = jnp.einsum("nhqk,nkhd->nqhd", weights, value_heads, preferred_element_type=jnp.float32)
    return (maxima, totals, summed.reshape(item_count, row_count, row_width))


def merge_sources(maxima, totals, partial_sums, head_count):
    overall = jnp.max(maxima, axis=0)
    factor = jnp.exp(maxima - overall[None])
    denominator = jnp.sum(factor * totals, axis=0)
    item_count, row_count, row_width = partial_sums.shape
    split_sums = partial_sums.reshape(item_count, row_count, head_count, row_width // head_count)
    weighted = jnp.sum(split_sums * jnp.transpose(factor, (0, 2, 1))[..., None], axis=0)
    return (weighted / jnp.transpose(denominator)[..., None]).reshape(row_count, row_width)


def body(queries, key_rows, value_rows, window, random_blocks, global_blocks, norm_gain):
    per_device = window.shape[0]
    row_width = queries.shape[1]
    head_count = row_width // HD
    shards = lax.axis_size("seq")
    position = lax.axis_index("seq")
    stacked = jnp.stack([key_rows, value_rows])
    stacked_blocks = stacked.reshape(2, per_device, BLK, row_width)
    query_blocks = queries.reshape(per_device, BLK, row_width)
    fetched = {}
    for offset in (2, 1, -1, -2):
        fetched[offset] = from_behind(stacked, "seq", offset)
    beside_all = [fetched[2], fetched[1], stacked, fetched[-1], fetched[-2]]
    glob_owner = global_blocks // per_device
    glob_within = global_blocks % per_device
    own_copies = jnp.take(stacked_blocks, glob_within, axis=1).astype(jnp.float32)
    holder = (glob_owner == position)[None, :, None, None]
    masked = jnp.where(holder, own_copies, 0.0)
    global_kv = lax.psum(masked, "seq").astype(jnp.bfloat16)
    window_pool = jnp.stack(beside_all, axis=1).reshape(2, 5 * per_device, BLK, row_width)
    key_pool = jnp.concatenate([window_pool, global_kv], axis=1)
    local_index = (window // per_device - position + 2) % shards * per_device + window % per_device
    glob_index = 5 * per_device + jnp.arange(global_blocks.shape[0], dtype=jnp.int32)
    near_index = jnp.concatenate(
        [local_index, jnp.broadcast_to(glob_index[None, :], (per_device, glob_index.shape[0]))],
        axis=1,
    )

    def near_block(items):
        one_query, one_index = items
        near_keys = jnp.take(key_pool[0], one_index, axis=0).reshape(1, -1, row_width)
        near_values = jnp.take(key_pool[1], one_index, axis=0).reshape(1, -1, row_width)
        return source_part(one_query[None], near_keys, near_values, head_count)

    near_max, near_total, near_sum = lax.map(near_block, (query_blocks, near_index))
    rand_count = random_blocks.shape[1]
    flat_ids = random_blocks.reshape(-1)
    entry_count = flat_ids.shape[0]
    slot_count = -(-entry_count // shards)
    owner_of = flat_ids // per_device
    within_of = flat_ids % per_device
    matches = (owner_of[:, None] == jnp.arange(shards, dtype=jnp.int32)[None, :]).astype(jnp.int32)
    earlier = jnp.cumsum(matches, axis=0) - matches
    rank_of = jnp.sum(earlier * matches, axis=1)
    slot_ids = jnp.arange(slot_count, dtype=jnp.int32)
    placed = (matches[:, :, None] == 1) & (rank_of[:, None, None] == slot_ids[None, None, :])
    wanted = jnp.sum(jnp.where(placed, within_of[:, None, None], 0), axis=0)
    pick_index = owner_of * slot_count + rank_of
    asked_for = lax.all_to_all(wanted, "seq", split_axis=0, concat_axis=0, tiled=True)
    offered = jnp.take(stacked_blocks, asked_for.reshape(-1), axis=1)
    arrived = lax.all_to_all(offered, "seq", split_axis=1, concat_axis=1, tiled=True)
    chosen = jnp.take(arrived, pick_index, axis=1)
    repeated = jnp.repeat(query_blocks, rand_count, axis=0)
    rand_max, rand_total, rand_sum = source_part(repeated, chosen[0], chosen[1], head_count)
    block_max = jnp.concatenate(
        [near_max, rand_max.reshape(per_device, rand_count, head_count, BLK)], axis=1
    )
    block_total = jnp.concatenate(
        [near_total, rand_total.reshape(per_device, rand_count, head_count, BLK)], axis=1
    )
    block_sum = jnp.concatenate(
        [near_sum, rand_sum.reshape(per_device, rand_count, BLK, row_width)], axis=1
    )
    merger = partial(merge_sources, head_count=head_count)
    attended = jax.vmap(merger)(block_max, block_total, block_sum).reshape(-1, row_width)
    row_squares = jnp.sum(attended * attended, axis=1)
    all_squares = lax.psum(row_squares, "head")
    inverse = lax.rsqrt(all_squares / D + 1e-06)
    return (attended * inverse[:, None] * norm_gain[None, :]).astype(jnp.bfloat16)


def solution(mesh):
    placed = (
        P("seq", "head"),
        P("seq", "head"),
        P("seq", "head"),
        P("seq", None),
        P("seq", None),
        P(),
        P("head"),
    )
    return jax.shard_map(
        body, mesh=mesh, in_specs=placed, out_specs=P("seq", "head"), check_vma=False
    )
```

profile of v0, /device:TPU:0, one launch (start us, length us, event | category | flops | bytes accessed | tf_op | source)
XLA Modules:
  0.0 525.1 jit_solution(13108856843056933589)
XLA Ops:
  3.1 6.9 %collective-permute-start.2 = (bf16[2,256,2048]{2,1,0:T(8,128)(2,1)}, bf16[2,256,2048]{2,1,0:T(8,128)(2,1)}, u32[]{:S(2)}, u32[]{:S(2)}) collective-permute-start(bf16[2,256,2048]{2,1,0:T(8,128)(2,1)} %pad_maximum_fusion.1), channel_id=1, source_target_pairs={{0,30},{2,0},{4,2},{6,4},{8,6},{10,8},{12,10},{14,12},{16,14},{18,... | collective-permute-start | bytes 6291464 | tf_op jit(solution)/shard_map/ppermute | solution.py:15
  13.9 7.0 %all-to-all-start = ((s32[16,1,1]{2,1,0:T(1,128)}), s32[16,1,1]{2,1,0:T(1,128)S(1)}, u32[]{:S(2)}, u32[]{:S(2)}) async-start(s32[16,1,1]{2,1,0:T(1,128)} %copy.55), calls=%async_computation | async-start | bytes 16384 | tf_op jit(solution)/shard_map/all_to_all | solution.py:93
  27.6 119.9 %all-to-all-done = s32[16,1,1]{2,1,0:T(1,128)S(1)} async-done(((s32[16,1,1]{2,1,0:T(1,128)}), s32[16,1,1]{2,1,0:T(1,128)S(1)}, u32[]{:S(2)}, u32[]{:S(2)}) %all-to-all-start) | async-done | bytes 96 | tf_op jit(solution)/shard_map/all_to_all | solution.py:93
  152.4 99.3 %all-reduce.1 = bf16[2,2,64,2048]{3,2,0,1:T(8,128)(2,1)} all-reduce(f32[2,2,64,2048]{3,2,0,1:T(8,128)} %select_bitcast_fusion.2), channel_id=1, replica_groups=mesh['seq'=16,'head'=2] {'seq'}, use_global_device_ids=true, to_apply=%region_0.1 | all-reduce | flops 524288 | bytes 3145728 | tf_op jit(solution)/shard_map/psum | solution.py:63
  256.6 7.6 %select_bitcast_fusion = bf16[2,16,64,2048]{3,2,0,1:T(8,128)(2,1)} fusion(bf16[16,2,64,2048]{3,2,1,0:T(8,128)(2,1)} %gather_fusion.3, pred[16]{0:T(512)(128)(4,1)S(1)} %compare_and_fusion.1), kind=kLoop, calls=%fused_computation.33 | loop fusion | flops 4194304 | bytes 16777232 | tf_op jit(solution)/shard_map/jit(_take)/select_n | solution.py:94
  283.3 10.1 %copy.53 = bf16[2,5,256,2048]{3,2,1,0:T(8,128)(2,1)} copy(bf16[2,5,256,2048]{3,2,0,1:T(8,128)(2,1)} %bitcast_dynamic-update-slice_fusion.2) | data formatting | bytes 20971520 | tf_op jit(solution)/shard_map/stack | solution.py:64
  293.4 11.8 %pad_maximum_fusion = bf16[2,22,64,2048]{3,2,1,0:T(8,128)(2,1)} fusion(bf16[2,20,64,2048]{3,2,1,0:T(8,128)(2,1)} %bitcast.137, bf16[2,2,64,2048]{3,2,0,1:T(8,128)(2,1)S(1)} %copy-done.4), kind=kLoop, calls=%fused_computation.30 | loop fusion | flops 23068672 | bytes 23068672 | tf_op jit(solution)/shard_map/concatenate | solution.py:65
  305.2 180.4 %while.14 = (s32[]{:T(128)}, f32[4,1,16,64]{3,2,1,0:T(8,128)S(1)}, f32[4,1,16,64]{3,2,1,0:T(8,128)S(1)}, f32[4,1,64,2048]{3,0,2,1:T(4,128)}, bf16[4,64,2048]{2,1...) while((s32[]{:T(128)}, f32[4,1,16,64]{3,2,1,0:T(8,128)S(1)}, ...), condition=%wide.region_4.6_spmd, body=%wide.region_1.5_spmd.sunk | while | flops 480771136 | bytes 89444768 | solution.py:79
  306.3 11.0 %slice_bitcast_fusion.3 = (bf16[22,64,2048]{2,1,0:T(8,128)(2,1)}, bf16[22,64,2048]{2,1,0:T(8,128)(2,1)}) fusion(bf16[2,22,64,2048]{3,2,1,0:T(8,128)(2,1)} %get-tuple-element.175), kind=kLoop, calls=%fused_computation.5.clone.1 | loop fusion | bytes 23068672 | tf_op jit(solution)/shard_map/while/body/eval_jaxpr/squeeze | solution.py:76
  317.3 5.2 gather_fusion
  322.5 5.3 %gather_fusion.1 = bf16[14,64,2048]{2,1,0:T(8,128)(2,1)} fusion(bf16[22,64,2048]{2,1,0:T(8,128)(2,1)} %get-tuple-element.145, s32[1024]{0:T(1024)S(1)} %pad_clamp_fusion.5), kind=kCustom, calls=%fused_computation.clone.clone.1 | custom fusion | bytes 7340088 | tf_op jit(solution)/shard_map/while/body/eval_jaxpr/jit(_take)/gather | solution.py:75
  340.0 10.3 %dynamic_update_slice.16 = f32[4,1,64,2048]{3,0,2,1:T(4,128)} dynamic-update-slice(f32[4,1,64,2048]{3,0,2,1:T(4,128)} %get-tuple-element.164, f32[1,1,64,2048]{3,0,2,1:T(1,128)S(1)} %bitcast.136, s32[]{:T(128)S(6)} %copy.121, s32[]{:T(128)} %constant.153.clone.1..sunk, s32[]{:T(128)} %constant.153.clone.1..sunk, s32[]{:T(128)} %constant.153.clone.1..sunk) | dynamic-update-slice | bytes 1048580 | tf_op jit(solution)/shard_map/while/body/jit(dynamic_update_index_in_dim)/dynamic_update_slice | solution.py:79
  351.4 11.0 %slice_bitcast_fusion.3 = (bf16[22,64,2048]{2,1,0:T(8,128)(2,1)}, bf16[22,64,2048]{2,1,0:T(8,128)(2,1)}) fusion(bf16[2,22,64,2048]{3,2,1,0:T(8,128)(2,1)} %get-tuple-element.175), kind=kLoop, calls=%fused_computation.5.clone.1 | loop fusion | bytes 23068672 | tf_op jit(solution)/shard_map/while/body/eval_jaxpr/squeeze | solution.py:76
  362.4 5.2 gather_fusion
  367.6 5.3 %gather_fusion.1 = bf16[14,64,2048]{2,1,0:T(8,128)(2,1)} fusion(bf16[22,64,2048]{2,1,0:T(8,128)(2,1)} %get-tuple-element.145, s32[1024]{0:T(1024)S(1)} %pad_clamp_fusion.5), kind=kCustom, calls=%fused_computation.clone.clone.1 | custom fusion | bytes 7340088 | tf_op jit(solution)/shard_map/while/body/eval_jaxpr/jit(_take)/gather | solution.py:75
  385.1 10.3 %dynamic_update_slice.16 = f32[4,1,64,2048]{3,0,2,1:T(4,128)} dynamic-update-slice(f32[4,1,64,2048]{3,0,2,1:T(4,128)} %get-tuple-element.164, f32[1,1,64,2048]{3,0,2,1:T(1,128)S(1)} %bitcast.136, s32[]{:T(128)S(6)} %copy.121, s32[]{:T(128)} %constant.153.clone.1..sunk, s32[]{:T(128)} %constant.153.clone.1..sunk, s32[]{:T(128)} %constant.153.clone.1..sunk) | dynamic-update-slice | bytes 1048580 | tf_op jit(solution)/shard_map/while/body/jit(dynamic_update_index_in_dim)/dynamic_update_slice | solution.py:79
  396.5 11.0 %slice_bitcast_fusion.3 = (bf16[22,64,2048]{2,1,0:T(8,128)(2,1)}, bf16[22,64,2048]{2,1,0:T(8,128)(2,1)}) fusion(bf16[2,22,64,2048]{3,2,1,0:T(8,128)(2,1)} %get-tuple-element.175), kind=kLoop, calls=%fused_computation.5.clone.1 | loop fusion | bytes 23068672 | tf_op jit(solution)/shard_map/while/body/eval_jaxpr/squeeze | solution.py:76
  407.5 5.2 gather_fusion
  412.7 5.3 %gather_fusion.1 = bf16[14,64,2048]{2,1,0:T(8,128)(2,1)} fusion(bf16[22,64,2048]{2,1,0:T(8,128)(2,1)} %get-tuple-element.145, s32[1024]{0:T(1024)S(1)} %pad_clamp_fusion.5), kind=kCustom, calls=%fused_computation.clone.clone.1 | custom fusion | bytes 7340088 | tf_op jit(solution)/shard_map/while/body/eval_jaxpr/jit(_take)/gather | solution.py:75
  430.2 10.3 %dynamic_update_slice.16 = f32[4,1,64,2048]{3,0,2,1:T(4,128)} dynamic-update-slice(f32[4,1,64,2048]{3,0,2,1:T(4,128)} %get-tuple-element.164, f32[1,1,64,2048]{3,0,2,1:T(1,128)S(1)} %bitcast.136, s32[]{:T(128)S(6)} %copy.121, s32[]{:T(128)} %constant.153.clone.1..sunk, s32[]{:T(128)} %constant.153.clone.1..sunk, s32[]{:T(128)} %constant.153.clone.1..sunk) | dynamic-update-slice | bytes 1048580 | tf_op jit(solution)/shard_map/while/body/jit(dynamic_update_index_in_dim)/dynamic_update_slice | solution.py:79
  441.6 11.0 %slice_bitcast_fusion.3 = (bf16[22,64,2048]{2,1,0:T(8,128)(2,1)}, bf16[22,64,2048]{2,1,0:T(8,128)(2,1)}) fusion(bf16[2,22,64,2048]{3,2,1,0:T(8,128)(2,1)} %get-tuple-element.175), kind=kLoop, calls=%fused_computation.5.clone.1 | loop fusion | bytes 23068672 | tf_op jit(solution)/shard_map/while/body/eval_jaxpr/squeeze | solution.py:76
  457.8 5.3 %gather_fusion.1 = bf16[14,64,2048]{2,1,0:T(8,128)(2,1)} fusion(bf16[22,64,2048]{2,1,0:T(8,128)(2,1)} %get-tuple-element.145, s32[1024]{0:T(1024)S(1)} %pad_clamp_fusion.5), kind=kCustom, calls=%fused_computation.clone.clone.1 | custom fusion | bytes 7340088 | tf_op jit(solution)/shard_map/while/body/eval_jaxpr/jit(_take)/gather | solution.py:75
  475.3 10.3 %dynamic_update_slice.16 = f32[4,1,64,2048]{3,0,2,1:T(4,128)} dynamic-update-slice(f32[4,1,64,2048]{3,0,2,1:T(4,128)} %get-tuple-element.164, f32[1,1,64,2048]{3,0,2,1:T(1,128)S(1)} %bitcast.136, s32[]{:T(128)S(6)} %copy.121, s32[]{:T(128)} %constant.153.clone.1..sunk, s32[]{:T(128)} %constant.153.clone.1..sunk, s32[]{:T(128)} %constant.153.clone.1..sunk) | dynamic-update-slice | bytes 1048580 | tf_op jit(solution)/shard_map/while/body/jit(dynamic_update_index_in_dim)/dynamic_update_slice | solution.py:79
  490.5 7.9 %gather_fusion.4 = bf16[12,2,64,2048]{3,2,1,0:T(8,128)(2,1)} fusion(bf16[2,16,64,2048]{3,2,0,1:T(8,128)(2,1)} %all-to-all-done.1, s32[1024]{0:T(1024)} %pad_clamp_fusion.1), kind=kCustom, calls=%fused_computation.4 | custom fusion | bytes 12582960 | tf_op jit(solution)/shard_map/jit(_take)/gather | solution.py:96
  (132 shorter events, 131.6 us)
Async XLA Ops:
  0.0 21.7 %copy-start.1 = (bf16[256,2048]{1,0:T(8,128)(2,1)S(1)}, bf16[256,2048]{1,0:T(8,128)(2,1)}, u32[]{:S(2)}) copy-start(bf16[256,2048]{1,0:T(8,128)(2,1)} %param.13) | copy-start | bytes 3145732
  0.0 12.1 %copy-start.6 = (s32[4,3]{1,0:T(4,128)S(1)}, s32[4,3]{1,0:T(4,128)}, u32[]{:S(2)}) copy-start(s32[4,3]{1,0:T(4,128)} %param.15) | copy-start | bytes 148
  0.0 21.1 %copy-start.9 = (s32[2]{0:T(128)S(1)}, s32[2]{0:T(128)}, u32[]{:S(2)}) copy-start(s32[2]{0:T(128)} %param.16) | copy-start | bytes 28
  0.0 21.1 %copy-start.8 = (s32[4,12]{1,0:T(4,128)S(1)}, s32[4,12]{1,0:T(4,128)}, u32[]{:S(2)}) copy-start(s32[4,12]{1,0:T(4,128)} %param.14) | copy-start | bytes 580
  3.1 273.7 %collective-permute-start.2 = (bf16[2,256,2048]{2,1,0:T(8,128)(2,1)}, bf16[2,256,2048]{2,1,0:T(8,128)(2,1)}, u32[]{:S(2)}, u32[]{:S(2)}) collective-permute-start(bf16[2,256,2048]{2,1,0:T(8,128)(2,1)} %pad_maximum_fusion.1), channel_id=1, source_target_pairs={{0,30},{2,0},{4,2},{6,4},{8,6},{10,8},{12,10},{14,12},{16,14},{18,... | collective-permute-start | bytes 6291464 | tf_op jit(solution)/shard_map/ppermute | solution.py:15
  10.1 269.9 %collective-permute-start.3 = (bf16[2,256,2048]{2,1,0:T(8,128)(2,1)}, bf16[2,256,2048]{2,1,0:T(8,128)(2,1)}, u32[]{:S(2)}, u32[]{:S(2)}) collective-permute-start(bf16[2,256,2048]{2,1,0:T(8,128)(2,1)} %pad_maximum_fusion.1), channel_id=1, source_target_pairs={{0,28},{2,30},{4,0},{6,2},{8,4},{10,6},{12,8},{14,10},{16,12},{18,... | collective-permute-start | bytes 6291464 | tf_op jit(solution)/shard_map/ppermute | solution.py:15
  10.6 261.6 %collective-permute-start.1 = (bf16[2,256,2048]{2,1,0:T(8,128)(2,1)}, bf16[2,256,2048]{2,1,0:T(8,128)(2,1)}, u32[]{:S(2)}, u32[]{:S(2)}) collective-permute-start(bf16[2,256,2048]{2,1,0:T(8,128)(2,1)} %pad_maximum_fusion.1), channel_id=1, source_target_pairs={{0,2},{2,4},{4,6},{6,8},{8,10},{10,12},{12,14},{14,16},{16,18},{18... | collective-permute-start | bytes 6291464 | tf_op jit(solution)/shard_map/ppermute | solution.py:15
  11.2 257.8 %collective-permute-start = (bf16[2,256,2048]{2,1,0:T(8,128)(2,1)}, bf16[2,256,2048]{2,1,0:T(8,128)(2,1)}, u32[]{:S(2)}, u32[]{:S(2)}) collective-permute-start(bf16[2,256,2048]{2,1,0:T(8,128)(2,1)} %pad_maximum_fusion.1), channel_id=1, source_target_pairs={{0,4},{2,6},{4,8},{6,10},{8,12},{10,14},{12,16},{14,18},{16,20},{1... | collective-permute-start | bytes 6291464 | tf_op jit(solution)/shard_map/ppermute | solution.py:15
  13.9 133.6 %all-to-all-start = ((s32[16,1,1]{2,1,0:T(1,128)}), s32[16,1,1]{2,1,0:T(1,128)S(1)}, u32[]{:S(2)}, u32[]{:S(2)}) async-start(s32[16,1,1]{2,1,0:T(1,128)} %copy.55), calls=%async_computation | async-start | bytes 16384 | tf_op jit(solution)/shard_map/all_to_all | solution.py:93
  264.2 226.3 %all-to-all-start.1 = ((bf16[2,16,64,2048]{3,2,0,1:T(8,128)(2,1)}), bf16[2,16,64,2048]{3,2,0,1:T(8,128)(2,1)}, u32[]{:S(2)}, u32[]{:S(2)}) async-start(bf16[2,16,64,2048]{3,2,0,1:T(8,128)(2,1)} %select_bitcast_fusion), calls=%async_computation.1 | async-start | bytes 16777216 | tf_op jit(solution)/shard_map/all_to_all | solution.py:95
  268.9 6.4 %copy-start.2 = (bf16[256,2048]{1,0:T(8,128)(2,1)S(1)}, bf16[256,2048]{1,0:T(8,128)(2,1)}, u32[]{:S(2)}) copy-start(bf16[256,2048]{1,0:T(8,128)(2,1)} %param.12) | copy-start | bytes 3145732
  283.3 10.2 %copy-start.4 = (bf16[2,2,64,2048]{3,2,0,1:T(8,128)(2,1)S(1)}, bf16[2,2,64,2048]{3,2,0,1:T(8,128)(2,1)}, u32[]{:S(2)}) copy-start(bf16[2,2,64,2048]{3,2,0,1:T(8,128)(2,1)} %all-reduce.1) | copy-start | bytes 3145732
  490.5 7.9 %copy-start.7 = (pred[12]{0:T(512)(128)(4,1)S(1)}, pred[12]{0:T(512)(128)(4,1)}, u32[]{:S(2)}) copy-start(pred[12]{0:T(512)(128)(4,1)} %get-tuple-element.81) | copy-start | bytes 40
  503.4 1.9 copy-start
  509.1 4.5 copy-start.3
  518.5 4.7 copy-start.5
where the time goes:
time: 527 us; the launch traced here: 525 us
  local copies, waits for them, and re-layouts  195 us (37%)
  waiting for transfers between devices  120 us (23%)
  blocking collectives  102 us (19%)
  other arithmetic  62.5 us (12%)
  matrix products  24.9 us (5%)
  starting transfers between devices  20.7 us (4%)
    all_to_all x1, waiting for transfers between devices, body(): lax.all_to_all(wanted, 'seq', split_axis=0, concat_axis=0, tiled=True)  120 us
    psum x1, blocking collectives, body(): global_kv = lax.psum(masked, 'seq').astype(jnp.bfloat16)  99.3 us
    squeeze x4, local copies, waits for them, and re-layouts, near_block(): key_pool[1]  44 us
    dynamic_update_slice x8, local copies, waits for them, and re-layouts, body(): lax.map(near_block, (query_blocks, near_index))  41.4 us
    gather x4, local copies, waits for them, and re-layouts, near_block(): jnp.take(key_pool[0], one_index, axis=0).reshape(1, -1, row_width)  21.2 us
    gather x4, local copies, waits for them, and re-layouts, near_block(): jnp.take(key_pool[1], one_index, axis=0).reshape(1, -1, row_width)  20.9 us
    select_n x4, other arithmetic, near_block(): jnp.take(key_pool[1], one_index, axis=0).reshape(1, -1, row_width)  15.5 us
    unnamed x26, local copies, waits for them, and re-layouts  15.3 us
  transfers between devices with their start and end apart: 6, of which 1 were waited for; matrix products, arithmetic and copies ran while one was open for 47% of the time, Pallas kernels for 0%

commit v1 on v0

v1 whole, which is shorter than its diff:
```python
from functools import partial
import math

import jax
import jax.numpy as jnp
from jax import lax
from jax.experimental import pallas as pl
from jax.experimental.pallas import tpu as pltpu
from jax.sharding import PartitionSpec as P

HD = 128
D = 4096
BLK = 64
PLANE = 4
CHUNKS = 2
ABSENT = -1e30
VMEM = 40 * 2**20


def up_to(rows, multiple):
    return -(-rows // multiple) * multiple


def exchange(array, shards, flip):
    return lax.ppermute(array, "seq", [(i, i ^ flip) for i in range(shards)])


def along(array, shards, step, first, last):
    pairs = [(z * PLANE + c, (z + step) * PLANE + c) for z in range(first, last) for c in range(PLANE)]
    return lax.ppermute(array, "seq", pairs)


def split_lse(lse):
    high = lse.astype(jnp.bfloat16).astype(jnp.float32)
    rest = lse - high
    middle = rest.astype(jnp.bfloat16).astype(jnp.float32)
    low = rest - middle
    return jnp.concatenate([high, middle, low, jnp.zeros_like(low)], axis=0).astype(jnp.bfloat16)


def join_lse(packed):
    rows = packed.shape[0] // 4
    pieces = packed.astype(jnp.float32)
    return pieces[:rows] + pieces[rows : 2 * rows] + pieces[2 * rows : 3 * rows]


def attend(planes, heads, plane_ref, bias_ref, *refs):
    queries = refs[: 2 * planes - 1]
    pairs = refs[2 * planes - 1 : 2 * planes - 1 + PLANE]
    outs = refs[2 * planes - 1 + PLANE : -1]
    messages, own_ref, own_lse_ref = outs[: planes - 1], outs[planes - 1], outs[planes]
    lse_ref = refs[-1]
    head = pl.program_id(0)
    plane = plane_ref[0]
    scale = HD**-0.5 * math.log2(math.e)
    shard_rows = pairs[0].shape[1]
    blocks = shard_rows // BLK
    for slot in range(planes):
        if slot == 0:
            query = queries[0][...]
        else:
            query = jnp.where(plane + slot < planes, queries[planes - 1 + slot][...], queries[planes - slot][...])
        tiles = []
        for j in range(PLANE):
            scores = lax.dot_general(pairs[j][0], query, (((1,), (1,)), ((), ())), preferred_element_type=jnp.float32)
            bias = bias_ref[slot, j * blocks : (j + 1) * blocks, :]
            lifted = scores.reshape(blocks, BLK, -1) * scale + bias[:, None, :]
            tiles.append(lifted.reshape(shard_rows, -1))
        peak = jnp.max(tiles[0], axis=0, keepdims=True)
        for j in range(1, PLANE):
            peak = jnp.maximum(peak, jnp.max(tiles[j], axis=0, keepdims=True))
        total, part = 0.0, 0.0
        for j in range(PLANE):
            weight = jnp.exp2(tiles[j] - peak)
            total = total + jnp.sum(weight, axis=0, keepdims=True)
            part = part + lax.dot_general(
                pairs[j][1], weight.astype(jnp.bfloat16), (((0,), (0,)), ((), ())), preferred_element_type=jnp.float32
            )
        part = part * (1.0 / total)
        lse_ref[slot, pl.ds(head, 1), :] = peak + jnp.log2(total)
        if slot == 0:
            own_ref[...] = part
        else:
            messages[slot - 1][pl.ds(pl.multiple_of(head * HD, HD), HD), :] = part.astype(jnp.bfloat16)

    @pl.when(head == heads - 1)
    def _():
        own_lse_ref[...] = lse_ref[0]
        for slot in range(1, planes):
            messages[slot - 1][heads * HD :, :] = split_lse(lse_ref[slot])


def attention(plane, bias, own, ups, downs, pairs):
    rows, width = own.shape
    heads, planes = width // HD, len(ups) + 1
    lse_rows = up_to(heads, 8)
    query_spec = pl.BlockSpec((rows, HD), lambda h, s: (0, h))
    pair_spec = pl.BlockSpec((2, rows, HD), lambda h, s: (0, 0, h))
    message = jax.ShapeDtypeStruct((width + 4 * lse_rows, rows), jnp.bfloat16)
    message_spec = pl.BlockSpec(message.shape, lambda h, s: (0, 0))
    products = heads * planes * PLANE * rows * rows
    return pl.pallas_call(
        partial(attend, planes, heads),
        out_shape=[message] * (planes - 1)
        + [jax.ShapeDtypeStruct((width, rows), jnp.float32), jax.ShapeDtypeStruct((lse_rows, rows), jnp.float32)],
        grid_spec=pltpu.PrefetchScalarGridSpec(
            num_scalar_prefetch=1,
            grid=(heads,),
            in_specs=[pl.BlockSpec(bias.shape, lambda h, s: (0, 0, 0))]
            + [query_spec] * (2 * planes - 1)
            + [pair_spec] * PLANE,
            out_specs=[message_spec] * (planes - 1)
            + [
                pl.BlockSpec((HD, rows), lambda h, s: (h, 0)),
                pl.BlockSpec((lse_rows, rows), lambda h, s: (0, 0)),
            ],
            scratch_shapes=[pltpu.VMEM((planes, lse_rows, rows), jnp.float32)],
        ),
        cost_estimate=pl.CostEstimate(
            flops=4 * products * HD, bytes_accessed=8 * 2**20, transcendentals=products
        ),
        compiler_params=pltpu.CompilerParams(vmem_limit_bytes=VMEM),
        name="attention",
    )(plane, bias, own, *ups, *downs, *pairs)


def merge(planes, heads, plane_ref, *refs):
    plane = plane_ref[0]
    for mine, came, out, valid in (
        (refs[0], refs[1], refs[4], plane > 0),
        (refs[2], refs[3], refs[5], plane < planes - 1),
    ):
        mine_lse = join_lse(mine[heads * HD :, :])
        came_lse = jnp.where(valid, join_lse(came[heads * HD :, :]), ABSENT)
        peak = jnp.maximum(mine_lse, came_lse)
        mine_weight, came_weight = jnp.exp2(mine_lse - peak), jnp.exp2(came_lse - peak)
        total = mine_weight + came_weight
        mine_weight, came_weight = mine_weight / total, came_weight / total
        for head in range(heads):
            at = slice(head * HD, (head + 1) * HD)
            mixed = mine[at, :].astype(jnp.float32) * mine_weight[head : head + 1]
            mixed += came[at, :].astype(jnp.float32) * came_weight[head : head + 1]
            out[at, :] = mixed.astype(jnp.bfloat16)
        out[heads * HD :, :] = split_lse(peak + jnp.log2(total))


def merged(plane, planes, heads, *messages):
    spec = pl.BlockSpec(memory_space=pltpu.VMEM)
    size = math.prod(messages[0].shape)
    return pl.pallas_call(
        partial(merge, planes, heads),
        out_shape=[jax.ShapeDtypeStruct(messages[0].shape, jnp.bfloat16)] * 2,
        in_specs=[pl.BlockSpec(memory_space=pltpu.SMEM)] + [spec] * 4,
        out_specs=[spec] * 2,
        cost_estimate=pl.CostEstimate(flops=8 * size, bytes_accessed=12 * size, transcendentals=0),
        compiler_params=pltpu.CompilerParams(vmem_limit_bytes=VMEM),
        name="merge",
    )(plane, *messages)


def finish(planes, heads, plane_ref, own_ref, own_lse_ref, up_ref, down_ref, gain_ref, out_ref, squares_ref):
    plane = plane_ref[0]
    own_lse = own_lse_ref[...]
    up_lse = jnp.where(plane > 0, join_lse(up_ref[heads * HD :, :]), ABSENT)
    down_lse = jnp.where(plane < planes - 1, join_lse(down_ref[heads * HD :, :]), ABSENT)
    peak = jnp.maximum(own_lse, jnp.maximum(up_lse, down_lse))
    weights = [jnp.exp2(lse - peak) for lse in (own_lse, up_lse, down_lse)]
    total = weights[0] + weights[1] + weights[2]
    weights = [weight / total for weight in weights]
    squares = 0.0
    for head in range(heads):
        at = slice(head * HD, (head + 1) * HD)
        row = slice(head, head + 1)
        mixed = own_ref[at, :] * weights[0][row]
        mixed += up_ref[at, :].astype(jnp.float32) * weights[1][row]
        mixed += down_ref[at, :].astype(jnp.float32) * weights[2][row]
        squares += jnp.sum(mixed * mixed, axis=0, keepdims=True)
        out_ref[:, at] = mixed.T * gain_ref[:, at]
    squares_ref[...] = squares


def finished(plane, planes, heads, own, own_lse, up, down, gain):
    spec = pl.BlockSpec(memory_space=pltpu.VMEM)
    width, rows = own.shape
    return pl.pallas_call(
        partial(finish, planes, heads),
        out_shape=[
            jax.ShapeDtypeStruct((rows, width), jnp.float32),
            jax.ShapeDtypeStruct((1, rows), jnp.float32),
        ],
        in_specs=[pl.BlockSpec(memory_space=pltpu.SMEM)] + [spec] * 5,
        out_specs=[spec] * 2,
        cost_estimate=pl.CostEstimate(flops=8 * own.size, bytes_accessed=12 * own.size, transcendentals=0),
        compiler_params=pltpu.CompilerParams(vmem_limit_bytes=VMEM),
        name="finish",
    )(plane, own, own_lse, up, down, gain)


def count_bias(window, random_blocks, global_blocks, position, shards):
    per_device = window.shape[0]
    planes = shards // PLANE
    plane, corner = position // PLANE, position % PLANE
    named = lax.all_gather(jnp.concatenate([window, random_blocks], axis=1), "seq")
    slots = (plane + jnp.arange(planes, dtype=jnp.int32)) % planes
    named = jnp.take(named, slots * PLANE + corner, axis=0)
    owners = plane * PLANE + (corner ^ jnp.arange(PLANE, dtype=jnp.int32))
    blocks = (owners[:, None] * per_device + jnp.arange(per_device, dtype=jnp.int32)[None, :]).reshape(-1)
    counts = jnp.sum(named[:, None, :, :] == blocks[None, :, None, None], axis=3)
    counts = counts + jnp.sum(global_blocks[None, :] == blocks[:, None], axis=1)[None, :, None]
    bias = jnp.where(counts > 0, jnp.log2(counts.astype(jnp.float32)), ABSENT)
    return jnp.repeat(bias, BLK, axis=2)


def body(queries, key_rows, value_rows, window, random_blocks, global_blocks, norm_gain):
    rows, row_width = queries.shape
    head_count = row_width // HD
    shards = lax.axis_size("seq")
    planes = shards // PLANE
    position = lax.axis_index("seq").astype(jnp.int32)
    plane = (position // PLANE).reshape(1)
    bias = count_bias(window, random_blocks, global_blocks, position, shards)
    chunks = min(CHUNKS, head_count)
    width = head_count // chunks * HD
    spans = [slice(c * width, (c + 1) * width) for c in range(chunks)]
    own_queries = [queries[:, span] for span in spans]
    own_pairs = [jnp.stack([key_rows[:, span], value_rows[:, span]]) for span in spans]
    ups, downs = [[q] for q in own_queries], [[q] for q in own_queries]
    pairs = [None] * chunks
    for hop in range(1, planes):
        for c in range(chunks):
            up = along(ups[c][-1], shards, 1, hop - 1, planes - 1)
            down = along(downs[c][-1], shards, -1, 1, planes - hop + 1)
            if hop == 1:
                pairs[c] = [own_pairs[c], exchange(own_pairs[c], shards, 1), exchange(own_pairs[c], shards, 2)]
            up, down = lax.optimization_barrier((up, down))
            if hop == min(2, planes - 1):
                up, down, *pairs[c][1:] = lax.optimization_barrier((up, down, *pairs[c][1:]))
                relay, flip = (pairs[c][1], 2) if c % 2 == 0 else (pairs[c][2], 1)
                pairs[c].append(exchange(relay, shards, flip))
            ups[c].append(up)
            downs[c].append(down)
    heads = width // HD
    parts = [attention(plane, bias, own_queries[c], ups[c][1:], downs[c][1:], pairs[c]) for c in range(chunks)]
    up_runs, down_runs = [None] * chunks, [None] * chunks
    for step in range(1, planes):
        for c in range(chunks):
            up, down = parts[c][planes - step - 1], parts[c][step - 1]
            if step > 1:
                up, down = merged(plane, planes, heads, up, up_runs[c], down, down_runs[c])
            up = along(up, shards, 1, 0, step)
            down = along(down, shards, -1, planes - step, planes)
            up_runs[c], down_runs[c] = lax.optimization_barrier((up, down))
    gain = norm_gain.reshape(1, row_width)
    attended, squares = [], 0.0
    for c in range(chunks):
        own, own_lse = parts[c][-2:]
        rows_c, squares_c = finished(
            plane, planes, heads, own, own_lse, up_runs[c], down_runs[c], gain[:, spans[c]]
        )
        attended.append(rows_c)
        squares = squares + squares_c
    all_squares = lax.psum(squares.reshape(-1), "head")
    inverse = lax.rsqrt(all_squares / D + 1e-06)
    return (jnp.concatenate(attended, axis=1) * inverse[:, None]).astype(jnp.bfloat16)


def solution(mesh):
    placed = (
        P("seq", "head"),
        P("seq", "head"),
        P("seq", "head"),
        P("seq", None),
        P("seq", None),
        P(),
        P("head"),
    )
    return jax.shard_map(
        body, mesh=mesh, in_specs=placed, out_specs=P("seq", "head"), check_vma=False
    )
```

time: 527 us -> 222 us (0.42)
  local copies, waits for them, and re-layouts: 195 us -> 6.99 us
  other arithmetic: 62.5 us -> 1.87 us
  waiting for transfers between devices: 120 us -> 61.9 us
  blocking collectives: 102 us -> 54 us
  Pallas kernels: 0 us -> 42.4 us
  starting transfers between devices: 20.7 us -> 53.6 us
  matrix products: 24.9 us -> 0 us
    all_to_all x2 -> x0, waiting for transfers between devices: 120 us -> none  [the longest x1 120 us: body(): lax.all_to_all(wanted, 'seq', split_axis=0, concat_axis=0, tiled=True)]
    psum x2 -> x1, blocking collectives: 102 us -> 2.47 us  [body(): all_squares = lax.psum(squares.reshape(-1), 'head')]
    ppermute x4 -> x30, waiting for transfers between devices: 0.01 us -> 61.9 us  [the longest x24 61.9 us: along(): return lax.ppermute(array, 'seq', pairs)]
    gather x11 -> x1, local copies, waits for them, and re-layouts: 56.5 us -> 0.57 us  [count_bias(): named = jnp.take(named, slots * PLANE + corner, axis=0)]
    all_gather x0 -> x1, blocking collectives: none -> 51.5 us  [count_bias(): lax.all_gather(jnp.concatenate([window, random_blocks], axis=1), 'seq')]
    ppermute x4 -> x30, starting transfers between devices: 8.97 us -> 53.6 us  [the longest x24 45.9 us: along(): return lax.ppermute(array, 'seq', pairs)]
    squeeze x4 -> x0, local copies, waits for them, and re-layouts: 44 us -> none  [near_block(): key_pool[1]]
    pallas_call x0 -> x8, Pallas kernels: none -> 42.4 us  [the longest x2 39.8 us: attention(): pl.pallas_call(partial(attend, planes, heads), out_shape=[message] * (pla...]
  transfers between devices with their start and end apart: 6 -> 30, of which waited for: 1 -> 13; matrix products, arithmetic and copies ran while one was open for 47% -> 1% of each run, Pallas kernels for 0% -> 19%
where the time goes in v1:
time: 222 us; the launch traced here: 221 us
  waiting for transfers between devices  61.9 us (28%)
  blocking collectives  54 us (24%)
  starting transfers between devices  53.6 us (24%)
  Pallas kernels  42.4 us (19%)
  local copies, waits for them, and re-layouts  6.99 us (3%)
    ppermute x24, waiting for transfers between devices, along(): return lax.ppermute(array, 'seq', pairs)  61.9 us
    all_gather x1, blocking collectives, count_bias(): lax.all_gather(jnp.concatenate([window, random_blocks], axis=1), 'seq')  51.5 us
    ppermute x24, starting transfers between devices, along(): return lax.ppermute(array, 'seq', pairs)  45.9 us
    pallas_call x2, Pallas kernels, attention(): pl.pallas_call(partial(attend, planes, heads), out_shape=[message] * (pla...  39.8 us
    ppermute x6, starting transfers between devices, exchange(): return lax.ppermute(array, 'seq', [(i, i ^ flip) for i in range(shards)])  7.69 us
  transfers between devices with their start and end apart: 30, of which 13 were waited for; matrix products, arithmetic and copies ran while one was open for 1% of the time, Pallas kernels for 19%

profile of v1, /device:TPU:0, one launch (start us, length us, event | category | flops | bytes accessed | tf_op | source)
XLA Modules:
  0.0 221.3 jit_solution(9989951193011631951)
XLA Ops:
  1.4 5.0 %collective-permute-start = (bf16[256,1024]{1,0:T(8,128)(2,1)S(1)}, bf16[256,1024]{1,0:T(8,128)(2,1)S(1)}, u32[]{:S(2)}, u32[]{:S(2)}) collective-permute-start(bf16[256,1024]{1,0:T(8,128)(2,1)S(1)} %get-tuple-element.117.refs_0_), channel_id=1, source_target_pairs={{0,8},{2,10},{4,12},{6,14},{8,16},{10,18},{12,20},{14,22},{16,24},... | collective-permute-start | bytes 1572872 | tf_op jit(solution)/shard_map/ppermute | solution.py:30
  7.7 5.3 %collective-permute-start.15 = (bf16[256,1024]{1,0:T(8,128)(2,1)S(1)}, bf16[256,1024]{1,0:T(8,128)(2,1)}, u32[]{:S(2)}, u32[]{:S(2)}) collective-permute-start(bf16[256,1024]{1,0:T(8,128)(2,1)S(1)} %get-tuple-element.118.refs_0_), channel_id=1, source_target_pairs={{0,8},{2,10},{4,12},{6,14},{8,16},{10,18},{12,20},{14,22},{16,24},... | collective-permute-start | bytes 1572872 | tf_op jit(solution)/shard_map/ppermute | solution.py:30
  13.4 1.6 collective-permute-start.4
  16.5 2.2 %collective-permute-done.refs_1_ = bf16[256,1024]{1,0:T(8,128)(2,1)S(1)} collective-permute-done((bf16[256,1024]{1,0:T(8,128)(2,1)S(1)}, bf16[256,1024]{1,0:T(8,128)(2,1)S(1)}, u32[]{:S(2)}, u32[]{:S(2)}) %collective-permute-start) | collective-permute-done | bytes 524320 | tf_op jit(solution)/shard_map/ppermute | solution.py:30
  20.0 1.7 collective-permute-done.1.refs_4_
  22.4 6.4 %collective-permute-done.15.refs_1_ = bf16[256,1024]{1,0:T(8,128)(2,1)} collective-permute-done((bf16[256,1024]{1,0:T(8,128)(2,1)S(1)}, bf16[256,1024]{1,0:T(8,128)(2,1)}, u32[]{:S(2)}, u32[]{:S(2)}) %collective-permute-start.15) | collective-permute-done | bytes 524320 | tf_op jit(solution)/shard_map/ppermute | solution.py:30
  30.2 2.8 %collective-permute-done.16.refs_4_ = bf16[256,1024]{1,0:T(8,128)(2,1)S(1)} collective-permute-done((bf16[256,1024]{1,0:T(8,128)(2,1)S(1)}, bf16[256,1024]{1,0:T(8,128)(2,1)S(1)}, u32[]{:S(2)}, u32[]{:S(2)}) %collective-permute-start.16) | collective-permute-done | bytes 524320 | tf_op jit(solution)/shard_map/ppermute | solution.py:30
  34.6 1.5 collective-permute-start.20
  36.1 8.2 %collective-permute-done.3.refs_5_ = bf16[256,1024]{1,0:T(8,128)(2,1)S(1)} collective-permute-done((bf16[256,1024]{1,0:T(8,128)(2,1)S(1)}, bf16[256,1024]{1,0:T(8,128)(2,1)S(1)}, u32[]{:S(2)}, u32[]{:S(2)}) %collective-permute-start.3) | collective-permute-done | bytes 524320 | tf_op jit(solution)/shard_map/ppermute | solution.py:30
  48.7 1.5 collective-permute-start.8
  50.2 51.5 %all-gather.1 = s32[16,4,15]{2,1,0:T(4,128)S(1)} all-gather(s32[1,4,15]{2,1,0:T(4,128)S(1)} %add_bitcast_fusion), channel_id=2, replica_groups=mesh['seq'=16,'head'=2] {'seq'}, dimensions={0}, use_global_device_ids=true | all-gather | bytes 4080 | tf_op jit(solution)/shard_map/all_gather | solution.py:203
  107.5 6.3 %collective-permute-done.7.refs_6_ = bf16[256,1024]{1,0:T(8,128)(2,1)} collective-permute-done((bf16[256,1024]{1,0:T(8,128)(2,1)}, bf16[256,1024]{1,0:T(8,128)(2,1)}, u32[]{:S(2)}, u32[]{:S(2)}) %collective-permute-start.7) | collective-permute-done | bytes 524320 | tf_op jit(solution)/shard_map/ppermute | solution.py:30
  113.8 5.6 %collective-permute-done.22.refs_6_ = bf16[256,1024]{1,0:T(8,128)(2,1)} collective-permute-done((bf16[256,1024]{1,0:T(8,128)(2,1)}, bf16[256,1024]{1,0:T(8,128)(2,1)}, u32[]{:S(2)}, u32[]{:S(2)}) %collective-permute-start.22) | collective-permute-done | bytes 524320 | tf_op jit(solution)/shard_map/ppermute | solution.py:30
  123.6 20.0 %attention.2 = (bf16[1056,256]{1,0:T(8,128)(2,1)S(1)}, bf16[1056,256]{1,0:T(8,128)(2,1)S(1)}, bf16[1056,256]{1,0:T(8,128)(2,1)S(1)}, f32[1024,256]{1,0:T(8,128)S(1)}, f32[8,256]{1,0:T(8,128)S(1)}) custom-call(s32[1]{0:T(128)} %bitcast.plane_ref, f32[4,16,256]{2,1,0:T(8,128)S(1)} %reshape.113.bias_ref, bf16[256,1024]{1,0:T(8,128)(2,1)S(1)} %get-tuple-element.117.refs_0_, ...), custom_call_target="tpu_custom_call" | custom-call | flops 4294967296 | bytes 8388608 | tf_op jit(solution)/shard_map/attention/pallas_call | solution.py:102
  145.8 19.8 %attention.3 = (bf16[1056,256]{1,0:T(8,128)(2,1)S(1)}, bf16[1056,256]{1,0:T(8,128)(2,1)S(1)}, bf16[1056,256]{1,0:T(8,128)(2,1)S(1)}, f32[1024,256]{1,0:T(8,128)S(1)}, f32[8,256]{1,0:T(8,128)S(1)}) custom-call(s32[1]{0:T(128)} %bitcast.plane_ref, f32[4,16,256]{2,1,0:T(8,128)S(1)} %reshape.113.bias_ref, bf16[256,1024]{1,0:T(8,128)(2,1)S(1)} %get-tuple-element.118.refs_0_, ...), custom_call_target="tpu_custom_call" | custom-call | flops 4294967296 | bytes 8388608 | tf_op jit(solution)/shard_map/attention/pallas_call | solution.py:102
  170.1 9.5 %collective-permute-done.24.refs_1_ = bf16[1056,256]{1,0:T(8,128)(2,1)S(1)} collective-permute-done((bf16[1056,256]{1,0:T(8,128)(2,1)S(1)}, bf16[1056,256]{1,0:T(8,128)(2,1)S(1)}, u32[]{:S(2)}, u32[]{:S(2)}) %collective-permute-start.24) | collective-permute-done | bytes 540704 | tf_op jit(solution)/shard_map/ppermute | solution.py:30
  180.1 4.4 %collective-permute-start.26 = (bf16[1056,256]{1,0:T(8,128)(2,1)S(1)}, bf16[1056,256]{1,0:T(8,128)(2,1)S(1)}, u32[]{:S(2)}, u32[]{:S(2)}) collective-permute-start(bf16[1056,256]{1,0:T(8,128)(2,1)S(1)} %get-tuple-element.102), channel_id=1, source_target_pairs={{0,8},{2,10},{4,12},{6,14},{8,16},{10,18},{12,20},{14,22},{1,9},{3... | collective-permute-start | bytes 1622024 | tf_op jit(solution)/shard_map/ppermute | solution.py:30
  185.2 6.0 %collective-permute-done.11.refs_1_ = bf16[1056,256]{1,0:T(8,128)(2,1)S(1)} collective-permute-done((bf16[1056,256]{1,0:T(8,128)(2,1)S(1)}, bf16[1056,256]{1,0:T(8,128)(2,1)S(1)}, u32[]{:S(2)}, u32[]{:S(2)}) %collective-permute-start.11) | collective-permute-done | bytes 540704 | tf_op jit(solution)/shard_map/ppermute | solution.py:30
  191.7 4.4 %collective-permute-start.13 = (bf16[1056,256]{1,0:T(8,128)(2,1)S(1)}, bf16[1056,256]{1,0:T(8,128)(2,1)S(1)}, u32[]{:S(2)}, u32[]{:S(2)}) collective-permute-start(bf16[1056,256]{1,0:T(8,128)(2,1)S(1)} %get-tuple-element.80), channel_id=1, source_target_pairs={{0,8},{2,10},{4,12},{6,14},{8,16},{10,18},{12,20},{14,22},{16,24},... | collective-permute-start | bytes 1622024 | tf_op jit(solution)/shard_map/ppermute | solution.py:30
  197.4 3.2 %collective-permute-done.26.refs_1_ = bf16[1056,256]{1,0:T(8,128)(2,1)S(1)} collective-permute-done((bf16[1056,256]{1,0:T(8,128)(2,1)S(1)}, bf16[1056,256]{1,0:T(8,128)(2,1)S(1)}, u32[]{:S(2)}, u32[]{:S(2)}) %collective-permute-start.26) | collective-permute-done | bytes 540704 | tf_op jit(solution)/shard_map/ppermute | solution.py:30
  201.0 4.4 %collective-permute-start.28 = (bf16[1056,256]{1,0:T(8,128)(2,1)S(1)}, bf16[1056,256]{1,0:T(8,128)(2,1)S(1)}, u32[]{:S(2)}, u32[]{:S(2)}) collective-permute-start(bf16[1056,256]{1,0:T(8,128)(2,1)S(1)} %get-tuple-element.106), channel_id=1, source_target_pairs={{0,8},{2,10},{4,12},{6,14},{8,16},{10,18},{12,20},{14,22},{16,24},... | collective-permute-start | bytes 1622024 | tf_op jit(solution)/shard_map/ppermute | solution.py:30
  207.3 4.9 %collective-permute-done.28.up_ref = bf16[1056,256]{1,0:T(8,128)(2,1)S(1)} collective-permute-done((bf16[1056,256]{1,0:T(8,128)(2,1)S(1)}, bf16[1056,256]{1,0:T(8,128)(2,1)S(1)}, u32[]{:S(2)}, u32[]{:S(2)}) %collective-permute-start.28) | collective-permute-done | bytes 540704 | tf_op jit(solution)/shard_map/ppermute | solution.py:30
  212.3 4.4 %collective-permute-done.29.down_ref = bf16[1056,256]{1,0:T(8,128)(2,1)S(1)} collective-permute-done((bf16[1056,256]{1,0:T(8,128)(2,1)S(1)}, bf16[1056,256]{1,0:T(8,128)(2,1)S(1)}, u32[]{:S(2)}, u32[]{:S(2)}) %collective-permute-start.29) | collective-permute-done | bytes 540704 | tf_op jit(solution)/shard_map/ppermute | solution.py:30
  217.6 2.5 %psum.7 = f32[256]{0:T(256)S(1)} all-reduce(f32[256]{0:T(256)S(1)} %bitcast.16), channel_id=1, replica_groups=mesh['seq'=16,'head'=2] {'head'}, use_global_device_ids=true, to_apply=%region_2.3 | all-reduce | flops 256 | bytes 2048 | tf_op jit(solution)/shard_map/psum | solution.py:262
  (102 shorter events, 37.5 us)
Async XLA Ops:
  1.4 17.2 %collective-permute-start = (bf16[256,1024]{1,0:T(8,128)(2,1)S(1)}, bf16[256,1024]{1,0:T(8,128)(2,1)S(1)}, u32[]{:S(2)}, u32[]{:S(2)}) collective-permute-start(bf16[256,1024]{1,0:T(8,128)(2,1)S(1)} %get-tuple-element.117.refs_0_), channel_id=1, source_target_pairs={{0,8},{2,10},{4,12},{6,14},{8,16},{10,18},{12,20},{14,22},{16,24},... | collective-permute-start | bytes 1572872 | tf_op jit(solution)/shard_map/ppermute | solution.py:30
  6.4 15.3 %collective-permute-start.1 = (bf16[256,1024]{1,0:T(8,128)(2,1)S(1)}, bf16[256,1024]{1,0:T(8,128)(2,1)S(1)}, u32[]{:S(2)}, u32[]{:S(2)}) collective-permute-start(bf16[256,1024]{1,0:T(8,128)(2,1)S(1)} %get-tuple-element.117.refs_0_), channel_id=1, source_target_pairs={{8,0},{10,2},{12,4},{14,6},{16,8},{18,10},{20,12},{22,14},{24,16},... | collective-permute-start | bytes 1572872 | tf_op jit(solution)/shard_map/ppermute | solution.py:30
  7.7 21.1 %collective-permute-start.15 = (bf16[256,1024]{1,0:T(8,128)(2,1)S(1)}, bf16[256,1024]{1,0:T(8,128)(2,1)}, u32[]{:S(2)}, u32[]{:S(2)}) collective-permute-start(bf16[256,1024]{1,0:T(8,128)(2,1)S(1)} %get-tuple-element.118.refs_0_), channel_id=1, source_target_pairs={{0,8},{2,10},{4,12},{6,14},{8,16},{10,18},{12,20},{14,22},{16,24},... | collective-permute-start | bytes 1572872 | tf_op jit(solution)/shard_map/ppermute | solution.py:30
  13.4 32.4 %collective-permute-start.4 = (bf16[2,256,1024]{2,1,0:T(8,128)(2,1)S(1)}, bf16[2,256,1024]{2,1,0:T(8,128)(2,1)}, u32[]{:S(2)}, u32[]{:S(2)}) collective-permute-start(bf16[2,256,1024]{2,1,0:T(8,128)(2,1)S(1)} %pad_maximum_fusion.refs_7_), channel_id=1, source_target_pairs={{0,2},{2,0},{4,6},{6,4},{8,10},{10,8},{12,14},{14,12},{16,18},{18,... | collective-permute-start | bytes 3145736 | tf_op jit(solution)/shard_map/ppermute | solution.py:25
  14.9 32.2 %collective-permute-start.5 = (bf16[2,256,1024]{2,1,0:T(8,128)(2,1)S(1)}, bf16[2,256,1024]{2,1,0:T(8,128)(2,1)}, u32[]{:S(2)}, u32[]{:S(2)}) collective-permute-start(bf16[2,256,1024]{2,1,0:T(8,128)(2,1)S(1)} %pad_maximum_fusion.refs_7_), channel_id=1, source_target_pairs={{0,4},{2,6},{4,0},{6,2},{8,12},{10,14},{12,8},{14,10},{16,20},{18,... | collective-permute-start | bytes 3145736 | tf_op jit(solution)/shard_map/ppermute | solution.py:25
  18.7 14.4 %collective-permute-start.16 = (bf16[256,1024]{1,0:T(8,128)(2,1)S(1)}, bf16[256,1024]{1,0:T(8,128)(2,1)S(1)}, u32[]{:S(2)}, u32[]{:S(2)}) collective-permute-start(bf16[256,1024]{1,0:T(8,128)(2,1)S(1)} %get-tuple-element.118.refs_0_), channel_id=1, source_target_pairs={{8,0},{10,2},{12,4},{14,6},{16,8},{18,10},{20,12},{22,14},{24,16},... | collective-permute-start | bytes 1572872 | tf_op jit(solution)/shard_map/ppermute | solution.py:30
  21.7 12.9 %collective-permute-start.2 = (bf16[256,1024]{1,0:T(8,128)(2,1)S(1)}, bf16[256,1024]{1,0:T(8,128)(2,1)S(1)}, u32[]{:S(2)}, u32[]{:S(2)}) collective-permute-start(bf16[256,1024]{1,0:T(8,128)(2,1)S(1)} %collective-permute-done.refs_1_), channel_id=1, source_target_pairs={{8,16},{10,18},{12,20},{14,22},{16,24},{18,26},{20,28},{22,30},{9,... | collective-permute-start | bytes 1572872 | tf_op jit(solution)/shard_map/ppermute | solution.py:30
  28.8 15.5 %collective-permute-start.3 = (bf16[256,1024]{1,0:T(8,128)(2,1)S(1)}, bf16[256,1024]{1,0:T(8,128)(2,1)S(1)}, u32[]{:S(2)}, u32[]{:S(2)}) collective-permute-start(bf16[256,1024]{1,0:T(8,128)(2,1)S(1)} %collective-permute-done.1.refs_4_), channel_id=1, source_target_pairs={{8,0},{10,2},{12,4},{14,6},{16,8},{18,10},{20,12},{22,14},{9,1},{1... | collective-permute-start | bytes 1572872 | tf_op jit(solution)/shard_map/ppermute | solution.py:30
  33.1 70.7 %collective-permute-start.19 = (bf16[2,256,1024]{2,1,0:T(8,128)(2,1)S(1)}, bf16[2,256,1024]{2,1,0:T(8,128)(2,1)}, u32[]{:S(2)}, u32[]{:S(2)}) collective-permute-start(bf16[2,256,1024]{2,1,0:T(8,128)(2,1)S(1)} %pad_maximum_fusion.1.refs_7_), channel_id=1, source_target_pairs={{0,2},{2,0},{4,6},{6,4},{8,10},{10,8},{12,14},{14,12},{16,18},{18,... | collective-permute-start | bytes 3145736 | tf_op jit(solution)/shard_map/ppermute | solution.py:25
  34.6 69.2 %collective-permute-start.20 = (bf16[2,256,1024]{2,1,0:T(8,128)(2,1)S(1)}, bf16[2,256,1024]{2,1,0:T(8,128)(2,1)}, u32[]{:S(2)}, u32[]{:S(2)}) collective-permute-start(bf16[2,256,1024]{2,1,0:T(8,128)(2,1)S(1)} %pad_maximum_fusion.1.refs_7_), channel_id=1, source_target_pairs={{0,4},{2,6},{4,0},{6,2},{8,12},{10,14},{12,8},{14,10},{16,20},{18,... | collective-permute-start | bytes 3145736 | tf_op jit(solution)/shard_map/ppermute | solution.py:25
  45.8 56.6 %collective-permute-start.18 = (bf16[256,1024]{1,0:T(8,128)(2,1)}, bf16[256,1024]{1,0:T(8,128)(2,1)}, u32[]{:S(2)}, u32[]{:S(2)}) collective-permute-start(bf16[256,1024]{1,0:T(8,128)(2,1)} %copy-done.4), channel_id=1, source_target_pairs={{8,0},{10,2},{12,4},{14,6},{16,8},{18,10},{20,12},{22,14},{9,1},{1... | collective-permute-start | bytes 1572872 | tf_op jit(solution)/shard_map/ppermute | solution.py:30
  47.1 59.4 %collective-permute-start.6 = (bf16[256,1024]{1,0:T(8,128)(2,1)}, bf16[256,1024]{1,0:T(8,128)(2,1)}, u32[]{:S(2)}, u32[]{:S(2)}) collective-permute-start(bf16[256,1024]{1,0:T(8,128)(2,1)} %copy-done.6), channel_id=1, source_target_pairs={{16,24},{18,26},{20,28},{22,30},{17,25},{19,27},{21,29},{23,31}} | collective-permute-start | bytes 1572872 | tf_op jit(solution)/shard_map/ppermute | solution.py:30
  48.7 70.8 %collective-permute-start.8 = (bf16[2,256,1024]{2,1,0:T(8,128)(2,1)}, bf16[2,256,1024]{2,1,0:T(8,128)(2,1)}, u32[]{:S(2)}, u32[]{:S(2)}) collective-permute-start(bf16[2,256,1024]{2,1,0:T(8,128)(2,1)} %collective-permute-done.4.refs_8_), channel_id=1, source_target_pairs={{0,4},{2,6},{4,0},{6,2},{8,12},{10,14},{12,8},{14,10},{16,20},{18,... | collective-permute-start | bytes 3145736 | tf_op jit(solution)/shard_map/ppermute | solution.py:25
  105.2 14.2 %collective-permute-start.22 = (bf16[256,1024]{1,0:T(8,128)(2,1)}, bf16[256,1024]{1,0:T(8,128)(2,1)}, u32[]{:S(2)}, u32[]{:S(2)}) collective-permute-start(bf16[256,1024]{1,0:T(8,128)(2,1)} %collective-permute-done.18.refs_5_), channel_id=1, source_target_pairs={{8,0},{10,2},{12,4},{14,6},{9,1},{11,3},{13,5},{15,7}} | collective-permute-start | bytes 1572872 | tf_op jit(solution)/shard_map/ppermute | solution.py:30
  106.5 39.3 %collective-permute-start.23 = (bf16[2,256,1024]{2,1,0:T(8,128)(2,1)}, bf16[2,256,1024]{2,1,0:T(8,128)(2,1)}, u32[]{:S(2)}, u32[]{:S(2)}) collective-permute-start(bf16[2,256,1024]{2,1,0:T(8,128)(2,1)} %collective-permute-done.20.refs_9_), channel_id=1, source_target_pairs={{0,2},{2,0},{4,6},{6,4},{8,10},{10,8},{12,14},{14,12},{16,18},{18,... | collective-permute-start | bytes 3145736 | tf_op jit(solution)/shard_map/ppermute | solution.py:25
  143.6 24.0 %collective-permute-start.10 = (bf16[1056,256]{1,0:T(8,128)(2,1)S(1)}, bf16[1056,256]{1,0:T(8,128)(2,1)S(1)}, u32[]{:S(2)}, u32[]{:S(2)}) collective-permute-start(bf16[1056,256]{1,0:T(8,128)(2,1)S(1)} %get-tuple-element.71.refs_0_), channel_id=1, source_target_pairs={{24,16},{26,18},{28,20},{30,22},{25,17},{27,19},{29,21},{31,23}} | collective-permute-start | bytes 1622024 | tf_op jit(solution)/shard_map/ppermute | solution.py:30
  144.3 23.3 %collective-permute-start.9 = (bf16[1056,256]{1,0:T(8,128)(2,1)S(1)}, bf16[1056,256]{1,0:T(8,128)(2,1)S(1)}, u32[]{:S(2)}, u32[]{:S(2)}) collective-permute-start(bf16[1056,256]{1,0:T(8,128)(2,1)S(1)} %get-tuple-element.73.refs_2_), channel_id=1, source_target_pairs={{0,8},{2,10},{4,12},{6,14},{1,9},{3,11},{5,13},{7,15}} | collective-permute-start | bytes 1622024 | tf_op jit(solution)/shard_map/ppermute | solution.py:30
  165.6 14.0 %collective-permute-start.24 = (bf16[1056,256]{1,0:T(8,128)(2,1)S(1)}, bf16[1056,256]{1,0:T(8,128)(2,1)S(1)}, u32[]{:S(2)}, u32[]{:S(2)}) collective-permute-start(bf16[1056,256]{1,0:T(8,128)(2,1)S(1)} %get-tuple-element.99.refs_2_), channel_id=1, source_target_pairs={{0,8},{2,10},{4,12},{6,14},{1,9},{3,11},{5,13},{7,15}} | collective-permute-start | bytes 1622024 | tf_op jit(solution)/shard_map/ppermute | solution.py:30
  166.9 12.7 %collective-permute-start.25 = (bf16[1056,256]{1,0:T(8,128)(2,1)S(1)}, bf16[1056,256]{1,0:T(8,128)(2,1)S(1)}, u32[]{:S(2)}, u32[]{:S(2)}) collective-permute-start(bf16[1056,256]{1,0:T(8,128)(2,1)S(1)} %get-tuple-element.97.refs_0_), channel_id=1, source_target_pairs={{24,16},{26,18},{28,20},{30,22},{25,17},{27,19},{29,21},{31,23}} | collective-permute-start | bytes 1622024 | tf_op jit(solution)/shard_map/ppermute | solution.py:30
  168.1 23.1 %collective-permute-start.11 = (bf16[1056,256]{1,0:T(8,128)(2,1)S(1)}, bf16[1056,256]{1,0:T(8,128)(2,1)S(1)}, u32[]{:S(2)}, u32[]{:S(2)}) collective-permute-start(bf16[1056,256]{1,0:T(8,128)(2,1)S(1)} %get-tuple-element.76), channel_id=1, source_target_pairs={{0,8},{2,10},{4,12},{6,14},{8,16},{10,18},{12,20},{14,22},{1,9},{3... | collective-permute-start | bytes 1622024 | tf_op jit(solution)/shard_map/ppermute | solution.py:30
  169.4 21.8 %collective-permute-start.12 = (bf16[1056,256]{1,0:T(8,128)(2,1)S(1)}, bf16[1056,256]{1,0:T(8,128)(2,1)S(1)}, u32[]{:S(2)}, u32[]{:S(2)}) collective-permute-start(bf16[1056,256]{1,0:T(8,128)(2,1)S(1)} %get-tuple-element.77), channel_id=1, source_target_pairs={{16,8},{18,10},{20,12},{22,14},{24,16},{26,18},{28,20},{30,22},{17... | collective-permute-start | bytes 1622024 | tf_op jit(solution)/shard_map/ppermute | solution.py:30
  180.1 20.5 %collective-permute-start.26 = (bf16[1056,256]{1,0:T(8,128)(2,1)S(1)}, bf16[1056,256]{1,0:T(8,128)(2,1)S(1)}, u32[]{:S(2)}, u32[]{:S(2)}) collective-permute-start(bf16[1056,256]{1,0:T(8,128)(2,1)S(1)} %get-tuple-element.102), channel_id=1, source_target_pairs={{0,8},{2,10},{4,12},{6,14},{8,16},{10,18},{12,20},{14,22},{1,9},{3... | collective-permute-start | bytes 1622024 | tf_op jit(solution)/shard_map/ppermute | solution.py:30
  184.5 16.1 %collective-permute-start.27 = (bf16[1056,256]{1,0:T(8,128)(2,1)S(1)}, bf16[1056,256]{1,0:T(8,128)(2,1)S(1)}, u32[]{:S(2)}, u32[]{:S(2)}) collective-permute-start(bf16[1056,256]{1,0:T(8,128)(2,1)S(1)} %get-tuple-element.103), channel_id=1, source_target_pairs={{16,8},{18,10},{20,12},{22,14},{24,16},{26,18},{28,20},{30,22},{17... | collective-permute-start | bytes 1622024 | tf_op jit(solution)/shard_map/ppermute | solution.py:30
  191.7 15.1 %collective-permute-start.13 = (bf16[1056,256]{1,0:T(8,128)(2,1)S(1)}, bf16[1056,256]{1,0:T(8,128)(2,1)S(1)}, u32[]{:S(2)}, u32[]{:S(2)}) collective-permute-start(bf16[1056,256]{1,0:T(8,128)(2,1)S(1)} %get-tuple-element.80), channel_id=1, source_target_pairs={{0,8},{2,10},{4,12},{6,14},{8,16},{10,18},{12,20},{14,22},{16,24},... | collective-permute-start | bytes 1622024 | tf_op jit(solution)/shard_map/ppermute | solution.py:30
  (22 other events, 280.6 us)

commit v2 on v1

v2 whole, which is shorter than its diff:
```python
from functools import partial
import math

import jax
import jax.numpy as jnp
from jax import lax
from jax.experimental import pallas as pl
from jax.experimental.pallas import tpu as pltpu
from jax.sharding import PartitionSpec as P

HD = 128
D = 4096
BLK = 64
PLANE = 4
GROUP = 8
SHARES = (1, 2)
TIES = ((1, 1), (1, 1), 0, 1)
SPLIT = True
COST = 8
TIEOWN = (3, 0)
TIES0 = 0
ABSENT = -1e30
NOTHING = 1e-30
VMEM = 40 * 2**20
BIG = 40 * 2**20
SPACE = pltpu.HBM


def up_to(rows, multiple):
    return -(-rows // multiple) * multiple


def exchange(array, shards, flip):
    return lax.ppermute(array, "seq", [(i, i ^ flip) for i in range(shards)])


def along(array, shards, step, first, last):
    pairs = [(z * PLANE + c, (z + step) * PLANE + c) for z in range(first, last) for c in range(PLANE)]
    return lax.ppermute(array, "seq", pairs)


def split_lse(lse):
    high = lse.astype(jnp.bfloat16).astype(jnp.float32)
    rest = lse - high
    middle = rest.astype(jnp.bfloat16).astype(jnp.float32)
    low = rest - middle
    return jnp.concatenate([high, middle, low, jnp.zeros_like(low)], axis=0).astype(jnp.bfloat16)


def join_lse(packed):
    rows = packed.shape[0] // 4
    pieces = packed.astype(jnp.float32)
    return pieces[:rows] + pieces[rows : 2 * rows] + pieces[2 * rows : 3 * rows]


def chain_sources(order, plane, ups, downs):
    low, even = plane < 2, plane % 2 == 0
    if order == 1:
        return ((plane == 0, downs[3]), (plane == 1, downs[1]), (plane == 2, ups[1]), (plane == 3, ups[3]))
    if order == 2:
        return ((low, downs[2]), (jnp.logical_not(low), ups[2]))
    return ((even, downs[1]), (jnp.logical_not(even), ups[1]))


def attend(planes, orders, heads, group, chained, stacked, table_ref, bias_ref, *refs):
    names = iter(refs)
    own = next(names)
    sources = [own] + [next(names) for _ in range(2 * (planes - 1) if chained else planes - 1)]
    ups, downs = sources[:planes], [own] + sources[planes:]
    if stacked:
        pairs = [(ref.at[0], ref.at[1]) for ref in (next(names) for _ in range(PLANE))]
    else:
        pairs = [(next(names), next(names)) for _ in range(PLANE)]
    sent = [order for order in orders if order]
    outs = {order: next(names) for order in sent}
    if 0 in orders:
        own_ref, own_lse_ref = next(names), next(names)
    query_ref, pair_ref, lse_ref, query_sem, pair_sem = names
    plane = table_ref[0]
    rows = own.shape[0]
    blocks = PLANE * rows // BLK
    batch = blocks // PLANE
    lanes = group * HD
    steps = heads // group
    scale = HD**-0.5 * math.log2(math.e)

    def pair_copy(step, j, half):
        at = pl.ds(pl.multiple_of(step * lanes, lanes), lanes)
        return pltpu.make_async_copy(
            pairs[j][half].at[:, at], pair_ref.at[half, pl.ds(j * rows, rows), at], pair_sem.at[step, j, half]
        )

    def query_copy(step, n, source):
        at = pl.ds(pl.multiple_of(step * lanes, lanes), lanes)
        return pltpu.make_async_copy(source.at[pl.ds(0, rows), at], query_ref.at[n, :, at], query_sem.at[step, n])

    for step in range(steps):
        for n, order in enumerate(orders):
            if order == 0 or not chained:
                query_copy(step, n, sources[order]).start()
            else:
                for holds, source in chain_sources(order, plane, ups, downs):
                    pl.when(holds)(query_copy(step, n, source).start)
        for j in range(PLANE):
            for half in range(2):
                pair_copy(step, j, half).start()

    def one_step(step, carry):
        for n in range(len(orders)):
            query_copy(step, n, own).wait()
        for j in range(PLANE):
            for half in range(2):
                pair_copy(step, j, half).wait()
        at = pl.ds(pl.multiple_of(step * lanes, lanes), lanes)
        for n, order in enumerate(orders):
            query = query_ref[n, :, at]
            count = table_ref[1 + order]

            def batch_scores(i):
                start = 1 + planes + order * blocks + i * batch
                spots = [pl.ds(pl.multiple_of(table_ref[start + b] * BLK, BLK), BLK) for b in range(batch)]
                keys = jnp.concatenate([pair_ref[0, spot, at] for spot in spots], axis=0)
                values = jnp.concatenate([pair_ref[1, spot, at] for spot in spots], axis=0)
                bias = bias_ref[order * PLANE + i][:batch]
                scores = []
                for h in range(group):
                    of = slice(h * HD, (h + 1) * HD)
                    product = lax.dot_general(
                        keys[:, of], query[:, of], (((1,), (1,)), ((), ())), preferred_element_type=jnp.float32
                    )
                    scores.append(product.reshape(batch, BLK, rows))
                return scores, bias, values

            def highest(scores, bias):
                top = jnp.max(scores.reshape(batch, BLK // 8, 8, rows), axis=1) * scale + bias[:, None, :]
                return jnp.max(jnp.max(top, axis=0), axis=0, keepdims=True)

            def weigh(scores, bias, peak, values, h):
                weight = jnp.exp2(scores * scale - (peak - bias)[:, None, :])
                total = jnp.sum(weight.reshape(batch * BLK, rows), axis=0, keepdims=True)
                part = lax.dot_general(
                    values[:, h * HD : (h + 1) * HD],
                    weight.astype(jnp.bfloat16).reshape(batch * BLK, rows),
                    (((0,), (0,)), ((), ())),
                    preferred_element_type=jnp.float32,
                )
                return total, part

            def first():
                scores, bias, values = batch_scores(0)
                state = []
                for h in range(group):
                    peak = jnp.maximum(highest(scores[h], bias), ABSENT / 2)
                    state.append((peak, *weigh(scores[h], bias, peak, values, h)))
                return tuple(state)

            def more(i, state):
                scores, bias, values = batch_scores(i)
                after = []
                for h in range(group):
                    peak, total, part = state[h]
                    higher = jnp.maximum(peak, highest(scores[h], bias))
                    shrink = jnp.exp2(peak - higher)
                    added, extra = weigh(scores[h], bias, higher, values, h)
                    after.append((higher, total * shrink + added, part * shrink + extra))
                return tuple(after)

            state = lax.fori_loop(1, count, more, first())
            for h in range(group):
                peak, total, part = state[h]
                total = jnp.maximum(total, NOTHING)
                head = step * group + h
                part = part * (1.0 / total)
                lse_ref[n, pl.ds(head, 1), :] = peak + jnp.log2(total)
                to = pl.ds(pl.multiple_of(head * HD, HD), HD)
                if order == 0:
                    own_ref[to, :] = part
                else:
                    outs[order][to, :] = part.astype(jnp.bfloat16)
        return carry

    lax.fori_loop(0, steps, one_step, 0)
    for n, order in enumerate(orders):
        if order == 0:
            own_lse_ref[...] = lse_ref[n]
        else:
            outs[order][heads * HD :, :] = split_lse(lse_ref[n])


def attention(name, orders, table, bias, own, arrived, pairs):
    rows, width = own.shape
    heads, planes = width // HD, bias.shape[0] // PLANE
    chained, stacked = len(arrived) > planes - 1, len(pairs) == PLANE
    group = math.gcd(heads, GROUP)
    lse_rows = up_to(heads, 8)
    anywhere, whole = pl.BlockSpec(memory_space=SPACE), pl.BlockSpec(memory_space=pltpu.VMEM)
    message = jax.ShapeDtypeStruct((width + 4 * lse_rows, rows), jnp.bfloat16)
    outs = [message for order in orders if order]
    if 0 in orders:
        outs += [jax.ShapeDtypeStruct((width, rows), jnp.float32), jax.ShapeDtypeStruct((lse_rows, rows), jnp.float32)]
    products = heads * len(orders) * PLANE * rows * rows // 2
    return pl.pallas_call(
        partial(attend, planes, orders, heads, group, chained, stacked),
        out_shape=outs,
        in_specs=[pl.BlockSpec(memory_space=pltpu.SMEM), whole] + [anywhere] * (1 + len(arrived) + len(pairs)),
        out_specs=[whole] * len(outs),
        scratch_shapes=[
            pltpu.VMEM((len(orders), rows, width), jnp.bfloat16),
            pltpu.VMEM((2, PLANE * rows, width), jnp.bfloat16),
            pltpu.VMEM((len(orders), lse_rows, rows), jnp.float32),
            pltpu.SemaphoreType.DMA((heads // group, len(orders))),
            pltpu.SemaphoreType.DMA((heads // group, PLANE, 2)),
        ],
        cost_estimate=pl.CostEstimate(
            flops=4 * products * HD, bytes_accessed=COST * 2**20, transcendentals=products
        ),
        compiler_params=pltpu.CompilerParams(vmem_limit_bytes=BIG),
        name=name,
    )(table, bias, own, *arrived, *pairs)


def merge(planes, heads, plane_ref, one_ref, other_ref, up_ref, down_ref, up_out, down_out):
    plane = plane_ref[0]

    def merge_into(mine, came, out, valid):
        mine_lse = join_lse(mine[heads * HD :, :])
        came_lse = jnp.where(valid, join_lse(came[heads * HD :, :]), ABSENT)
        peak = jnp.maximum(mine_lse, came_lse)
        mine_weight, came_weight = jnp.exp2(mine_lse - peak), jnp.exp2(came_lse - peak)
        total = mine_weight + came_weight
        mine_weight, came_weight = mine_weight / total, came_weight / total
        for head in range(heads):
            at = slice(head * HD, (head + 1) * HD)
            mixed = mine[at, :].astype(jnp.float32) * mine_weight[head : head + 1]
            mixed += came[at, :].astype(jnp.float32) * came_weight[head : head + 1]
            out[at, :] = mixed.astype(jnp.bfloat16)
        out[heads * HD :, :] = split_lse(peak + jnp.log2(total))

    @pl.when(plane % 2 == 0)
    def _():
        merge_into(one_ref, up_ref, up_out, plane > 0)
        merge_into(other_ref, down_ref, down_out, plane < planes - 1)

    @pl.when(plane % 2 == 1)
    def _():
        merge_into(other_ref, up_ref, up_out, plane > 0)
        merge_into(one_ref, down_ref, down_out, plane < planes - 1)


def merged(plane, planes, heads, *messages):
    spec = pl.BlockSpec(memory_space=pltpu.VMEM)
    size = math.prod(messages[0].shape)
    return pl.pallas_call(
        partial(merge, planes, heads),
        out_shape=[jax.ShapeDtypeStruct(messages[0].shape, jnp.bfloat16)] * 2,
        in_specs=[pl.BlockSpec(memory_space=pltpu.SMEM)] + [spec] * 4,
        out_specs=[spec] * 2,
        cost_estimate=pl.CostEstimate(flops=8 * size, bytes_accessed=12 * size, transcendentals=0),
        compiler_params=pltpu.CompilerParams(vmem_limit_bytes=VMEM),
        name="merge",
    )(plane, *messages)


def finish(planes, heads, chained, plane_ref, own_ref, own_lse_ref, gain_ref, *refs):
    messages, (out_ref, squares_ref) = refs[:-2], refs[-2:]
    plane = plane_ref[0]
    lses = [own_lse_ref[...]] + [join_lse(message[heads * HD :, :]) for message in messages]
    if chained:
        lses[1] = jnp.where(plane > 0, lses[1], ABSENT)
        lses[2] = jnp.where(plane < planes - 1, lses[2], ABSENT)
    peak = lses[0]
    for lse in lses[1:]:
        peak = jnp.maximum(peak, lse)
    weights = [jnp.exp2(lse - peak) for lse in lses]
    total = sum(weights[1:], weights[0])
    weights = [weight / total for weight in weights]
    squares = 0.0
    for head in range(heads):
        at = slice(head * HD, (head + 1) * HD)
        row = slice(head, head + 1)
        mixed = own_ref[at, :] * weights[0][row]
        for message, weight in zip(messages, weights[1:]):
            mixed += message[at, :].astype(jnp.float32) * weight[row]
        squares += jnp.sum(mixed * mixed, axis=0, keepdims=True)
        out_ref[:, at] = mixed.T * gain_ref[:, at]
    squares_ref[...] = squares


def finished(plane, planes, heads, chained, own, own_lse, gain, messages):
    spec = pl.BlockSpec(memory_space=pltpu.VMEM)
    width, rows = own.shape
    return pl.pallas_call(
        partial(finish, planes, heads, chained),
        out_shape=[
            jax.ShapeDtypeStruct((rows, width), jnp.float32),
            jax.ShapeDtypeStruct((1, rows), jnp.float32),
        ],
        in_specs=[pl.BlockSpec(memory_space=pltpu.SMEM)] + [spec] * (3 + len(messages)),
        out_specs=[spec] * 2,
        cost_estimate=pl.CostEstimate(flops=8 * own.size, bytes_accessed=12 * own.size, transcendentals=0),
        compiler_params=pltpu.CompilerParams(vmem_limit_bytes=VMEM),
        name="finish",
    )(plane, own, own_lse, gain, *messages)


def tables(named, global_blocks, plane, corner, planes):
    per_device = named.shape[1]
    count = PLANE * per_device
    owners = plane * PLANE + (corner ^ jnp.arange(PLANE, dtype=jnp.int32))
    blocks = (owners[:, None] * per_device + jnp.arange(per_device, dtype=jnp.int32)[None, :]).reshape(-1)
    times = jnp.sum(named[:, None, :, :] == blocks[None, :, None, None], axis=3)
    times = times + jnp.sum(global_blocks[None, :] == blocks[:, None], axis=1)[None, :, None]
    needed = jnp.max(times, axis=2) > 0
    earlier = jnp.arange(count)[:, None] < jnp.arange(count)[None, :]
    place = jnp.sum(needed[:, :, None] & earlier[None], axis=1)
    chosen = needed[:, None, :] & (place[:, None, :] == jnp.arange(count)[None, :, None])
    spots = jnp.sum(jnp.where(chosen, jnp.arange(count)[None, None, :], 0), axis=2)
    times = jnp.sum(jnp.where(chosen[:, :, :, None], times[:, None, :, :], 0), axis=2)
    bias = jnp.where(times > 0, jnp.log2(times.astype(jnp.float32)), ABSENT)
    bias = jnp.repeat(bias, BLK, axis=2).reshape(planes * PLANE, per_device, per_device * BLK)
    bias = jnp.pad(bias, ((0, 0), (0, up_to(per_device, 8) - per_device), (0, 0)))
    batches = jnp.maximum(-(-jnp.sum(needed, axis=1) // per_device), 1)
    table = jnp.concatenate([plane.reshape(1), batches, spots.reshape(-1)]).astype(jnp.int32)
    return table, bias


def flipped(array, shards, flip):
    return exchange(array, shards, flip * PLANE)


tie = lax.optimization_barrier


def travel(owns, keys, values, own_named, shards, plane):
    planes = shards // PLANE
    arrived, pairs = [], []
    for own, key, value in zip(owns, keys, values):
        arrived.append([flipped(own, shards, planes - order) for order in range(1, planes)])
        pairs.append([exchange(half, shards, flip) if flip else half for flip in range(PLANE) for half in (key, value)])
    return arrived, pairs, [flipped(own_named, shards, planes - order) for order in range(1, planes)]


def travel_on_line(owns, keys, values, own_named, shards, plane):
    groups = range(len(owns))
    ups, downs, near, far, diagonal = ([[] for _ in groups] for _ in range(5))
    rows, width = owns[0].shape
    blocks, names = own_named.shape
    note = jnp.pad(own_named.astype(owns[0].dtype), ((0, up_to(blocks, 16) - blocks), (0, width - names)))
    owns = [jnp.concatenate([owns[0], note], axis=0), *owns[1:]]
    for hop in range(1, 4):
        for c in groups:
            up, down = (ups[c][-1], downs[c][-1]) if hop > 1 else (owns[c], owns[c])
            key, value = keys[c], values[c]
            if hop == 2:
                up, down, *first = tie((up, down, near[c][0], far[c][1]) if TIES[0][c] else (up, down))
                near[c][0], far[c][1] = first or (near[c][0], far[c][1])
            if hop == 3:
                up, down, *second = tie((up, down, near[c][1], far[c][0]) if TIES[1][c] else (up, down))
                near[c][1], far[c][0] = second or (near[c][1], far[c][0])
            up, down = along(up, shards, 1, hop - 1, 3), along(down, shards, -1, 1, 5 - hop)
            if hop == 1:
                if c and TIES[2]:
                    key, value, *_ = tie((key, value, near[c - 1][1], far[c - 1][0]))
                elif c and TIES[3]:
                    key, value, *_ = tie((key, value, near[c - 1][0], far[c - 1][1]))
                near[c] = [exchange(key, shards, 1), exchange(value, shards, 1)]
                far[c] = [exchange(key, shards, 2), exchange(value, shards, 2)]
            up, down = tie((up, down))
            if hop == 2:
                diagonal[c] = [exchange(near[c][0], shards, 2), exchange(far[c][1], shards, 1)]
            ups[c].append(up)
            downs[c].append(down)
    arrived = [[*ups[c], *downs[c]] for c in groups]
    ups, downs = ([array[rows : rows + blocks, :names] for array in arrays] for arrays in (ups[0], downs[0]))
    named = [jnp.zeros_like(ups[0])] * 3
    for order in range(1, 4):
        for holds, array in chain_sources(order, plane, [None, *ups], [None, *downs]):
            named[order - 1] = jnp.where(holds, array, named[order - 1])
    named = [name.astype(own_named.dtype) for name in named]
    pairs = [[keys[c], values[c], *near[c], *far[c], *diagonal[c]] for c in groups]
    return arrived, pairs, named


def body(queries, key_rows, value_rows, window, random_blocks, global_blocks, norm_gain):
    rows, row_width = queries.shape
    head_count = row_width // HD
    shards = lax.axis_size("seq")
    planes = shards // PLANE
    line = planes == 4
    position = lax.axis_index("seq").astype(jnp.int32)
    plane, corner = position // PLANE, position % PLANE
    own_named = jnp.concatenate([window, random_blocks], axis=1)
    bounds = [0] + [head_count * share // SHARES[-1] * HD for share in SHARES]
    spans = [slice(low, high) for low, high in zip(bounds[:-1], bounds[1:])]
    owns, keys, values = ([array[:, span] for span in spans] for array in (queries, key_rows, value_rows))
    arrived, pairs, named = (travel_on_line if line else travel)(owns, keys, values, own_named, shards, plane)
    table, bias = tables(jnp.stack([own_named, *named]), global_blocks, plane, corner, planes)
    plane = plane.reshape(1)
    gain = norm_gain.reshape(1, row_width)
    parts, own_parts = [], []
    for own, came, pair in zip(owns, arrived, pairs):
        given = table, bias, own, came, pair
        if SPLIT:
            if TIES0:
                own_part, own_lse = attention("own_part", (0,), *given)
                given = (*given[:2], *tie((given[2], own_lse))[:1], *given[3:])
            sent = attention("sent_parts", tuple(range(1, planes)), *given)
            if not TIES0:
                own_part, own_lse = attention("own_part", (0,), *given)
        else:
            sent = attention("far_part", (1,), *given)
            *rest, own_part, own_lse = attention("near_parts", (*range(2, planes), 0), *given)
            sent = [*sent, *rest]
        parts.append([None, *sent])
        own_parts.append((own_part, own_lse))
    heads = [(span.stop - span.start) // HD for span in spans]
    runs = [None] * len(spans)
    for step in range(1, planes):
        for c in range(len(spans)):
            if line:
                up = down = parts[c][step]
                if step > 1:
                    up, down = merged(plane, planes, heads[c], up, parts[c][planes - step], *runs[c])
                if step == TIEOWN[c]:
                    up, down, *own_parts[c] = tie((up, down, *own_parts[c]))
                runs[c] = tie((along(up, shards, 1, 0, step), along(down, shards, -1, planes - step, planes)))
            elif step == 1:
                runs[c] = [flipped(parts[c][order], shards, planes - order) for order in range(1, planes)]
    attended, squares = [], 0.0
    for c, span in enumerate(spans):
        rows_c, squares_c = finished(plane, planes, heads[c], line, *own_parts[c], gain[:, span], runs[c])
        attended.append(rows_c)
        squares = squares + squares_c
    all_squares = lax.psum(squares.reshape(-1), "head")
    inverse = lax.rsqrt(all_squares / D + 1e-06)
    return (jnp.concatenate(attended, axis=1) * inverse[:, None]).astype(jnp.bfloat16)


def solution(mesh):
    placed = (
        P("seq", "head"),
        P("seq", "head"),
        P("seq", "head"),
        P("seq", None),
        P("seq", None),
        P(),
        P("head"),
    )
    return jax.shard_map(
        body, mesh=mesh, in_specs=placed, out_specs=P("seq", "head"), check_vma=False
    )
```

time: 222 us -> 168 us (0.76)
  blocking collectives: 54 us -> 2.47 us
  starting transfers between devices: 53.6 us -> 64.7 us
  Pallas kernels: 42.4 us -> 33.7 us
  waiting for transfers between devices: 61.9 us -> 56.6 us
    all_gather x1 -> x0, blocking collectives: 51.5 us -> none  [count_bias(): lax.all_gather(jnp.concatenate([window, random_blocks], axis=1), 'seq')]
    ppermute x24, waiting for transfers between devices: 61.9 us -> 48.2 us  [along(): return lax.ppermute(array, 'seq', pairs)]
    pallas_call x4 -> x6, Pallas kernels: 40.7 us -> 31.7 us  [the longest x4 30.8 us: attention(): pl.pallas_call(partial(attend, planes, orders, heads, group, chained, sta...]
    ppermute x6 -> x12, waiting for transfers between devices: 0.02 us -> 8.45 us  [exchange(): return lax.ppermute(array, 'seq', [(i, i ^ flip) for i in range(shards)])]
    ppermute x24, starting transfers between devices: 45.9 us -> 52.4 us  [along(): return lax.ppermute(array, 'seq', pairs)]
    ppermute x6 -> x12, starting transfers between devices: 7.69 us -> 12.3 us  [exchange(): return lax.ppermute(array, 'seq', [(i, i ^ flip) for i in range(shards)])]
  transfers between devices with their start and end apart: 30 -> 36, of which waited for: 13 -> 13; matrix products, arithmetic and copies ran while one was open for 1% -> 2% of each run, Pallas kernels for 19% -> 20%
where the time goes in v2:
time: 168 us; the launch traced here: 167 us
  starting transfers between devices  64.7 us (39%)
  waiting for transfers between devices  56.6 us (34%)
  Pallas kernels  33.7 us (20%)
  local copies, waits for them, and re-layouts  5.6 us (3%)
  other arithmetic  3.15 us (2%)
  blocking collectives  2.47 us (1%)
    ppermute x24, starting transfers between devices, along(): return lax.ppermute(array, 'seq', pairs)  52.4 us
    ppermute x24, waiting for transfers between devices, along(): return lax.ppermute(array, 'seq', pairs)  48.2 us
    pallas_call x4, Pallas kernels, attention(): pl.pallas_call(partial(attend, planes, orders, heads, group, chained, sta...  30.8 us
    ppermute x12, starting transfers between devices, exchange(): return lax.ppermute(array, 'seq', [(i, i ^ flip) for i in range(shards)])  12.3 us
    ppermute x12, waiting for transfers between devices, exchange(): return lax.ppermute(array, 'seq', [(i, i ^ flip) for i in range(shards)])  8.45 us
    unnamed x34, local copies, waits for them, and re-layouts  3.5 us
  transfers between devices with their start and end apart: 36, of which 13 were waited for; matrix products, arithmetic and copies ran while one was open for 2% of the time, Pallas kernels for 20%

profile of v2, /device:TPU:0, one launch (start us, length us, event | category | flops | bytes accessed | tf_op | source)
XLA Modules:
  0.0 166.8 jit_solution(15469899048139247476)
XLA Ops:
  1.5 5.9 %collective-permute-start = (bf16[272,1024]{1,0:T(8,128)(2,1)S(1)}, bf16[272,1024]{1,0:T(8,128)(2,1)}, u32[]{:S(2)}, u32[]{:S(2)}) collective-permute-start(bf16[272,1024]{1,0:T(8,128)(2,1)S(1)} %fusion.2), channel_id=1, source_target_pairs={{0,8},{2,10},{4,12},{6,14},{8,16},{10,18},{12,20},{14,22},{16,24},... | collective-permute-start | bytes 1671176 | tf_op jit(solution)/shard_map/ppermute | solution.py:39
  7.5 1.6 collective-permute-start.2
  9.1 1.6 collective-permute-start.3
  12.0 5.3 %collective-permute-start.18 = (bf16[256,1024]{1,0:T(8,128)(2,1)S(1)}, bf16[256,1024]{1,0:T(8,128)(2,1)}, u32[]{:S(2)}, u32[]{:S(2)}) collective-permute-start(bf16[256,1024]{1,0:T(8,128)(2,1)S(1)} %get-tuple-element.151.refs_0_), channel_id=1, source_target_pairs={{0,8},{2,10},{4,12},{6,14},{8,16},{10,18},{12,20},{14,22},{16,24},... | collective-permute-start | bytes 1572872 | tf_op jit(solution)/shard_map/ppermute | solution.py:39
  17.3 3.6 %collective-permute-done.2.refs_9_ = bf16[256,1024]{1,0:T(8,128)(2,1)S(1)} collective-permute-done((bf16[256,1024]{1,0:T(8,128)(2,1)S(1)}, bf16[256,1024]{1,0:T(8,128)(2,1)S(1)}, u32[]{:S(2)}, u32[]{:S(2)}) %collective-permute-start.2) | collective-permute-done | bytes 524320 | tf_op jit(solution)/shard_map/ppermute | solution.py:34
  26.0 2.1 %collective-permute-done.1.refs_4_ = bf16[272,1024]{1,0:T(8,128)(2,1)} collective-permute-done((bf16[272,1024]{1,0:T(8,128)(2,1)S(1)}, bf16[272,1024]{1,0:T(8,128)(2,1)}, u32[]{:S(2)}, u32[]{:S(2)}) %collective-permute-start.1) | collective-permute-done | bytes 557088 | tf_op jit(solution)/shard_map/ppermute | solution.py:39
  30.9 8.3 %collective-permute-done.19.refs_4_ = bf16[256,1024]{1,0:T(8,128)(2,1)S(1)} collective-permute-done((bf16[256,1024]{1,0:T(8,128)(2,1)S(1)}, bf16[256,1024]{1,0:T(8,128)(2,1)S(1)}, u32[]{:S(2)}, u32[]{:S(2)}) %collective-permute-start.19) | collective-permute-done | bytes 524320 | tf_op jit(solution)/shard_map/ppermute | solution.py:39
  42.9 6.5 %collective-permute-done.5.refs_5_ = bf16[272,1024]{1,0:T(8,128)(2,1)} collective-permute-done((bf16[272,1024]{1,0:T(8,128)(2,1)}, bf16[272,1024]{1,0:T(8,128)(2,1)}, u32[]{:S(2)}, u32[]{:S(2)}) %collective-permute-start.5) | collective-permute-done | bytes 557088 | tf_op jit(solution)/shard_map/ppermute | solution.py:39
  49.9 4.3 %collective-permute-done.6.refs_10_ = bf16[256,1024]{1,0:T(8,128)(2,1)} collective-permute-done((bf16[256,1024]{1,0:T(8,128)(2,1)S(1)}, bf16[256,1024]{1,0:T(8,128)(2,1)}, u32[]{:S(2)}, u32[]{:S(2)}) %collective-permute-start.6) | collective-permute-done | bytes 524320 | tf_op jit(solution)/shard_map/ppermute | solution.py:34
  58.5 11.8 %collective-permute-done.23.refs_5_ = bf16[256,1024]{1,0:T(8,128)(2,1)} collective-permute-done((bf16[256,1024]{1,0:T(8,128)(2,1)}, bf16[256,1024]{1,0:T(8,128)(2,1)}, u32[]{:S(2)}, u32[]{:S(2)}) %collective-permute-start.23) | collective-permute-done | bytes 524320 | tf_op jit(solution)/shard_map/ppermute | solution.py:39
  74.4 1.9 %collective-permute-done.9.refs_6_ = bf16[272,1024]{1,0:T(8,128)(2,1)} collective-permute-done((bf16[272,1024]{1,0:T(8,128)(2,1)}, bf16[272,1024]{1,0:T(8,128)(2,1)}, u32[]{:S(2)}, u32[]{:S(2)}) %collective-permute-start.9) | collective-permute-done | bytes 557088 | tf_op jit(solution)/shard_map/ppermute | solution.py:39
  84.1 8.5 %sent_parts.2 = (bf16[1056,256]{1,0:T(8,128)(2,1)S(1)}, bf16[1056,256]{1,0:T(8,128)(2,1)S(1)}, bf16[1056,256]{1,0:T(8,128)(2,1)S(1)}) custom-call(s32[69]{0:T(128)S(1)} %pad_add_fusion.2.table_ref, f32[16,8,256]{2,1,0:T(8,128)S(1)} %pad.9.bias_ref, bf16[256,1024]{1,0:T(8,128)(2,1)S(1)} %get-tuple-element.152.refs_0_, ...), custom_call_target="tpu_custom_call" | custom-call | flops 1610612736 | bytes 8388608 | tf_op jit(solution)/shard_map/sent_parts/pallas_call | solution.py:202
  92.6 5.4 %collective-permute-start.12 = (bf16[1056,256]{1,0:T(8,128)(2,1)S(1)}, bf16[1056,256]{1,0:T(8,128)(2,1)S(1)}, u32[]{:S(2)}, u32[]{:S(2)}) collective-permute-start(bf16[1056,256]{1,0:T(8,128)(2,1)S(1)} %get-tuple-element.88.other_ref), channel_id=1, source_target_pairs={{0,8},{2,10},{4,12},{6,14},{1,9},{3,11},{5,13},{7,15}} | collective-permute-start | bytes 1622024 | tf_op jit(solution)/shard_map/ppermute | solution.py:39
  98.8 8.5 %sent_parts.3 = (bf16[1056,256]{1,0:T(8,128)(2,1)S(1)}, bf16[1056,256]{1,0:T(8,128)(2,1)S(1)}, bf16[1056,256]{1,0:T(8,128)(2,1)S(1)}) custom-call(s32[69]{0:T(128)S(1)} %pad_add_fusion.2.table_ref, f32[16,8,256]{2,1,0:T(8,128)S(1)} %pad.9.bias_ref, bf16[256,1024]{1,0:T(8,128)(2,1)S(1)} %get-tuple-element.151.refs_0_, ...), custom_call_target="tpu_custom_call" | custom-call | flops 1610612736 | bytes 8388608 | tf_op jit(solution)/shard_map/sent_parts/pallas_call | solution.py:202
  109.8 3.5 %collective-permute-start.14 = (bf16[1056,256]{1,0:T(8,128)(2,1)S(1)}, bf16[1056,256]{1,0:T(8,128)(2,1)S(1)}, u32[]{:S(2)}, u32[]{:S(2)}) collective-permute-start(bf16[1056,256]{1,0:T(8,128)(2,1)S(1)} %get-tuple-element.92), channel_id=1, source_target_pairs={{0,8},{2,10},{4,12},{6,14},{8,16},{10,18},{12,20},{14,22},{1,9},{3... | collective-permute-start | bytes 1622024 | tf_op jit(solution)/shard_map/ppermute | solution.py:39
  113.9 7.3 %collective-permute-done.30.up_ref = bf16[1056,256]{1,0:T(8,128)(2,1)S(1)} collective-permute-done((bf16[1056,256]{1,0:T(8,128)(2,1)S(1)}, bf16[1056,256]{1,0:T(8,128)(2,1)S(1)}, u32[]{:S(2)}, u32[]{:S(2)}) %collective-permute-start.30) | collective-permute-done | bytes 540704 | tf_op jit(solution)/shard_map/ppermute | solution.py:39
  121.7 4.4 %collective-permute-start.32 = (bf16[1056,256]{1,0:T(8,128)(2,1)S(1)}, bf16[1056,256]{1,0:T(8,128)(2,1)S(1)}, u32[]{:S(2)}, u32[]{:S(2)}) collective-permute-start(bf16[1056,256]{1,0:T(8,128)(2,1)S(1)} %get-tuple-element.130), channel_id=1, source_target_pairs={{0,8},{2,10},{4,12},{6,14},{8,16},{10,18},{12,20},{14,22},{1,9},{3... | collective-permute-start | bytes 1622024 | tf_op jit(solution)/shard_map/ppermute | solution.py:39
  126.8 6.9 %own_part.2 = (f32[1024,256]{1,0:T(8,128)S(1)}, f32[8,256]{1,0:T(8,128)S(1)}) custom-call(s32[69]{0:T(128)S(1)} %pad_add_fusion.2.table_ref, f32[16,8,256]{2,1,0:T(8,128)S(1)} %pad.9.bias_ref, bf16[256,1024]{1,0:T(8,128)(2,1)S(1)} %get-tuple-element.152.refs_0_, bf16[272,1024]{1,0:T(8,128)(2,1)} %collective-permute-done.refs_1_, ...), custom_call_target="tpu_custom_call" | custom-call | flops 536870912 | bytes 8388608 | tf_op jit(solution)/shard_map/own_part/pallas_call | solution.py:202
  134.3 3.4 %collective-permute-start.16 = (bf16[1056,256]{1,0:T(8,128)(2,1)S(1)}, bf16[1056,256]{1,0:T(8,128)(2,1)S(1)}, u32[]{:S(2)}, u32[]{:S(2)}) collective-permute-start(bf16[1056,256]{1,0:T(8,128)(2,1)S(1)} %get-tuple-element.102), channel_id=1, source_target_pairs={{0,8},{2,10},{4,12},{6,14},{8,16},{10,18},{12,20},{14,22},{16,24},... | collective-permute-start | bytes 1622024 | tf_op jit(solution)/shard_map/ppermute | solution.py:39
  139.0 5.4 %collective-permute-done.32.up_ref = bf16[1056,256]{1,0:T(8,128)(2,1)S(1)} collective-permute-done((bf16[1056,256]{1,0:T(8,128)(2,1)S(1)}, bf16[1056,256]{1,0:T(8,128)(2,1)S(1)}, u32[]{:S(2)}, u32[]{:S(2)}) %collective-permute-start.32) | collective-permute-done | bytes 540704 | tf_op jit(solution)/shard_map/ppermute | solution.py:39
  145.1 4.2 %collective-permute-start.34 = (bf16[1056,256]{1,0:T(8,128)(2,1)S(1)}, bf16[1056,256]{1,0:T(8,128)(2,1)S(1)}, u32[]{:S(2)}, u32[]{:S(2)}) collective-permute-start(bf16[1056,256]{1,0:T(8,128)(2,1)S(1)} %get-tuple-element.134), channel_id=1, source_target_pairs={{0,8},{2,10},{4,12},{6,14},{8,16},{10,18},{12,20},{14,22},{16,24},... | collective-permute-start | bytes 1622024 | tf_op jit(solution)/shard_map/ppermute | solution.py:39
  150.6 6.9 %own_part.3 = (f32[1024,256]{1,0:T(8,128)S(1)}, f32[8,256]{1,0:T(8,128)S(1)}) custom-call(s32[69]{0:T(128)S(1)} %pad_add_fusion.2.table_ref, f32[16,8,256]{2,1,0:T(8,128)S(1)} %pad.9.bias_ref, bf16[256,1024]{1,0:T(8,128)(2,1)S(1)} %get-tuple-element.151.refs_0_, bf16[256,1024]{1,0:T(8,128)(2,1)} %collective-permute-done.18.refs_1_, ...), custom_call_target="tpu_custom_call" | custom-call | flops 536870912 | bytes 8388608 | tf_op jit(solution)/shard_map/own_part/pallas_call | solution.py:202
  158.1 4.7 %collective-permute-done.34.refs_0_ = bf16[1056,256]{1,0:T(8,128)(2,1)S(1)} collective-permute-done((bf16[1056,256]{1,0:T(8,128)(2,1)S(1)}, bf16[1056,256]{1,0:T(8,128)(2,1)S(1)}, u32[]{:S(2)}, u32[]{:S(2)}) %collective-permute-start.34) | collective-permute-done | bytes 540704 | tf_op jit(solution)/shard_map/ppermute | solution.py:39
  163.2 2.5 %psum.7 = f32[256]{0:T(256)S(1)} all-reduce(f32[256]{0:T(256)S(1)} %bitcast.15), channel_id=1, replica_groups=mesh['seq'=16,'head'=2] {'head'}, use_global_device_ids=true, to_apply=%region_7.8 | all-reduce | flops 256 | bytes 2048 | tf_op jit(solution)/shard_map/psum | solution.py:434
  (125 shorter events, 41.7 us)
Async XLA Ops:
  1.5 23.0 %collective-permute-start = (bf16[272,1024]{1,0:T(8,128)(2,1)S(1)}, bf16[272,1024]{1,0:T(8,128)(2,1)}, u32[]{:S(2)}, u32[]{:S(2)}) collective-permute-start(bf16[272,1024]{1,0:T(8,128)(2,1)S(1)} %fusion.2), channel_id=1, source_target_pairs={{0,8},{2,10},{4,12},{6,14},{8,16},{10,18},{12,20},{14,22},{16,24},... | collective-permute-start | bytes 1671176 | tf_op jit(solution)/shard_map/ppermute | solution.py:39
  10.7 17.4 %collective-permute-start.1 = (bf16[272,1024]{1,0:T(8,128)(2,1)S(1)}, bf16[272,1024]{1,0:T(8,128)(2,1)}, u32[]{:S(2)}, u32[]{:S(2)}) collective-permute-start(bf16[272,1024]{1,0:T(8,128)(2,1)S(1)} %fusion.2), channel_id=1, source_target_pairs={{8,0},{10,2},{12,4},{14,6},{16,8},{18,10},{20,12},{22,14},{24,16},... | collective-permute-start | bytes 1671176 | tf_op jit(solution)/shard_map/ppermute | solution.py:39
  12.0 17.7 %collective-permute-start.18 = (bf16[256,1024]{1,0:T(8,128)(2,1)S(1)}, bf16[256,1024]{1,0:T(8,128)(2,1)}, u32[]{:S(2)}, u32[]{:S(2)}) collective-permute-start(bf16[256,1024]{1,0:T(8,128)(2,1)S(1)} %get-tuple-element.151.refs_0_), channel_id=1, source_target_pairs={{0,8},{2,10},{4,12},{6,14},{8,16},{10,18},{12,20},{14,22},{16,24},... | collective-permute-start | bytes 1572872 | tf_op jit(solution)/shard_map/ppermute | solution.py:39
  20.9 18.3 %collective-permute-start.19 = (bf16[256,1024]{1,0:T(8,128)(2,1)S(1)}, bf16[256,1024]{1,0:T(8,128)(2,1)S(1)}, u32[]{:S(2)}, u32[]{:S(2)}) collective-permute-start(bf16[256,1024]{1,0:T(8,128)(2,1)S(1)} %get-tuple-element.151.refs_0_), channel_id=1, source_target_pairs={{8,0},{10,2},{12,4},{14,6},{16,8},{18,10},{20,12},{22,14},{24,16},... | collective-permute-start | bytes 1572872 | tf_op jit(solution)/shard_map/ppermute | solution.py:39
  29.6 19.7 %collective-permute-start.5 = (bf16[272,1024]{1,0:T(8,128)(2,1)}, bf16[272,1024]{1,0:T(8,128)(2,1)}, u32[]{:S(2)}, u32[]{:S(2)}) collective-permute-start(bf16[272,1024]{1,0:T(8,128)(2,1)} %collective-permute-done.1.refs_4_), channel_id=1, source_target_pairs={{8,0},{10,2},{12,4},{14,6},{16,8},{18,10},{20,12},{22,14},{9,1},{1... | collective-permute-start | bytes 1671176 | tf_op jit(solution)/shard_map/ppermute | solution.py:39
  39.3 16.2 %collective-permute-start.7 = (bf16[256,1024]{1,0:T(8,128)(2,1)S(1)}, bf16[256,1024]{1,0:T(8,128)(2,1)}, u32[]{:S(2)}, u32[]{:S(2)}) collective-permute-start(bf16[256,1024]{1,0:T(8,128)(2,1)S(1)} %get-tuple-element.150.refs_7_), channel_id=1, source_target_pairs={{0,4},{2,6},{4,0},{6,2},{8,12},{10,14},{12,8},{14,10},{16,20},{18,... | collective-permute-start | bytes 1572872 | tf_op jit(solution)/shard_map/ppermute | solution.py:34
  40.0 16.9 %collective-permute-start.22 = (bf16[256,1024]{1,0:T(8,128)(2,1)}, bf16[256,1024]{1,0:T(8,128)(2,1)}, u32[]{:S(2)}, u32[]{:S(2)}) collective-permute-start(bf16[256,1024]{1,0:T(8,128)(2,1)} %collective-permute-done.18.refs_1_), channel_id=1, source_target_pairs={{8,16},{10,18},{12,20},{14,22},{16,24},{18,26},{20,28},{22,30},{9,... | collective-permute-start | bytes 1572872 | tf_op jit(solution)/shard_map/ppermute | solution.py:39
  41.5 29.7 %collective-permute-start.24 = (bf16[256,1024]{1,0:T(8,128)(2,1)S(1)}, bf16[256,1024]{1,0:T(8,128)(2,1)}, u32[]{:S(2)}, u32[]{:S(2)}) collective-permute-start(bf16[256,1024]{1,0:T(8,128)(2,1)S(1)} %get-tuple-element.110.refs_8_), channel_id=1, source_target_pairs={{0,2},{2,0},{4,6},{6,4},{8,10},{10,8},{12,14},{14,12},{16,18},{18,... | collective-permute-start | bytes 1572872 | tf_op jit(solution)/shard_map/ppermute | solution.py:34
  49.4 22.2 %collective-permute-start.25 = (bf16[256,1024]{1,0:T(8,128)(2,1)S(1)}, bf16[256,1024]{1,0:T(8,128)(2,1)}, u32[]{:S(2)}, u32[]{:S(2)}) collective-permute-start(bf16[256,1024]{1,0:T(8,128)(2,1)S(1)} %get-tuple-element.109.refs_7_), channel_id=1, source_target_pairs={{0,4},{2,6},{4,0},{6,2},{8,12},{10,14},{12,8},{14,10},{16,20},{18,... | collective-permute-start | bytes 1572872 | tf_op jit(solution)/shard_map/ppermute | solution.py:34
  54.2 16.2 %collective-permute-start.23 = (bf16[256,1024]{1,0:T(8,128)(2,1)}, bf16[256,1024]{1,0:T(8,128)(2,1)}, u32[]{:S(2)}, u32[]{:S(2)}) collective-permute-start(bf16[256,1024]{1,0:T(8,128)(2,1)} %copy-done), channel_id=1, source_target_pairs={{8,0},{10,2},{12,4},{14,6},{16,8},{18,10},{20,12},{22,14},{9,1},{1... | collective-permute-start | bytes 1572872 | tf_op jit(solution)/shard_map/ppermute | solution.py:39
  55.5 17.6 %collective-permute-start.8 = (bf16[272,1024]{1,0:T(8,128)(2,1)}, bf16[272,1024]{1,0:T(8,128)(2,1)}, u32[]{:S(2)}, u32[]{:S(2)}) collective-permute-start(bf16[272,1024]{1,0:T(8,128)(2,1)} %collective-permute-done.4.refs_2_), channel_id=1, source_target_pairs={{16,24},{18,26},{20,28},{22,30},{17,25},{19,27},{21,29},{23,31}} | collective-permute-start | bytes 1671176 | tf_op jit(solution)/shard_map/ppermute | solution.py:39
  57.0 19.4 %collective-permute-start.9 = (bf16[272,1024]{1,0:T(8,128)(2,1)}, bf16[272,1024]{1,0:T(8,128)(2,1)}, u32[]{:S(2)}, u32[]{:S(2)}) collective-permute-start(bf16[272,1024]{1,0:T(8,128)(2,1)} %collective-permute-done.5.refs_5_), channel_id=1, source_target_pairs={{8,0},{10,2},{12,4},{14,6},{9,1},{11,3},{13,5},{15,7}} | collective-permute-start | bytes 1671176 | tf_op jit(solution)/shard_map/ppermute | solution.py:39
  71.6 27.1 %collective-permute-start.28 = (bf16[256,1024]{1,0:T(8,128)(2,1)}, bf16[256,1024]{1,0:T(8,128)(2,1)}, u32[]{:S(2)}, u32[]{:S(2)}) collective-permute-start(bf16[256,1024]{1,0:T(8,128)(2,1)} %copy-done.2), channel_id=1, source_target_pairs={{0,4},{2,6},{4,0},{6,2},{8,12},{10,14},{12,8},{14,10},{16,20},{18,... | collective-permute-start | bytes 1572872 | tf_op jit(solution)/shard_map/ppermute | solution.py:34
  73.1 25.6 %collective-permute-start.29 = (bf16[256,1024]{1,0:T(8,128)(2,1)}, bf16[256,1024]{1,0:T(8,128)(2,1)}, u32[]{:S(2)}, u32[]{:S(2)}) collective-permute-start(bf16[256,1024]{1,0:T(8,128)(2,1)} %copy-done.4), channel_id=1, source_target_pairs={{0,2},{2,0},{4,6},{6,4},{8,10},{10,8},{12,14},{14,12},{16,18},{18,... | collective-permute-start | bytes 1572872 | tf_op jit(solution)/shard_map/ppermute | solution.py:34
  76.4 21.6 %collective-permute-start.26 = (bf16[256,1024]{1,0:T(8,128)(2,1)}, bf16[256,1024]{1,0:T(8,128)(2,1)}, u32[]{:S(2)}, u32[]{:S(2)}) collective-permute-start(bf16[256,1024]{1,0:T(8,128)(2,1)} %collective-permute-done.22.refs_2_), channel_id=1, source_target_pairs={{16,24},{18,26},{20,28},{22,30},{17,25},{19,27},{21,29},{23,31}} | collective-permute-start | bytes 1572872 | tf_op jit(solution)/shard_map/ppermute | solution.py:39
  79.9 18.8 %collective-permute-start.27 = (bf16[256,1024]{1,0:T(8,128)(2,1)}, bf16[256,1024]{1,0:T(8,128)(2,1)}, u32[]{:S(2)}, u32[]{:S(2)}) collective-permute-start(bf16[256,1024]{1,0:T(8,128)(2,1)} %collective-permute-done.23.refs_5_), channel_id=1, source_target_pairs={{8,0},{10,2},{12,4},{14,6},{9,1},{11,3},{13,5},{15,7}} | collective-permute-start | bytes 1572872 | tf_op jit(solution)/shard_map/ppermute | solution.py:39
  92.6 16.7 %collective-permute-start.12 = (bf16[1056,256]{1,0:T(8,128)(2,1)S(1)}, bf16[1056,256]{1,0:T(8,128)(2,1)S(1)}, u32[]{:S(2)}, u32[]{:S(2)}) collective-permute-start(bf16[1056,256]{1,0:T(8,128)(2,1)S(1)} %get-tuple-element.88.other_ref), channel_id=1, source_target_pairs={{0,8},{2,10},{4,12},{6,14},{1,9},{3,11},{5,13},{7,15}} | collective-permute-start | bytes 1622024 | tf_op jit(solution)/shard_map/ppermute | solution.py:39
  109.8 24.0 %collective-permute-start.14 = (bf16[1056,256]{1,0:T(8,128)(2,1)S(1)}, bf16[1056,256]{1,0:T(8,128)(2,1)S(1)}, u32[]{:S(2)}, u32[]{:S(2)}) collective-permute-start(bf16[1056,256]{1,0:T(8,128)(2,1)S(1)} %get-tuple-element.92), channel_id=1, source_target_pairs={{0,8},{2,10},{4,12},{6,14},{8,16},{10,18},{12,20},{14,22},{1,9},{3... | collective-permute-start | bytes 1622024 | tf_op jit(solution)/shard_map/ppermute | solution.py:39
  113.2 20.6 %collective-permute-start.15 = (bf16[1056,256]{1,0:T(8,128)(2,1)S(1)}, bf16[1056,256]{1,0:T(8,128)(2,1)S(1)}, u32[]{:S(2)}, u32[]{:S(2)}) collective-permute-start(bf16[1056,256]{1,0:T(8,128)(2,1)S(1)} %get-tuple-element.93), channel_id=1, source_target_pairs={{16,8},{18,10},{20,12},{22,14},{24,16},{26,18},{28,20},{30,22},{17... | collective-permute-start | bytes 1622024 | tf_op jit(solution)/shard_map/ppermute | solution.py:39
  121.7 22.7 %collective-permute-start.32 = (bf16[1056,256]{1,0:T(8,128)(2,1)S(1)}, bf16[1056,256]{1,0:T(8,128)(2,1)S(1)}, u32[]{:S(2)}, u32[]{:S(2)}) collective-permute-start(bf16[1056,256]{1,0:T(8,128)(2,1)S(1)} %get-tuple-element.130), channel_id=1, source_target_pairs={{0,8},{2,10},{4,12},{6,14},{8,16},{10,18},{12,20},{14,22},{1,9},{3... | collective-permute-start | bytes 1622024 | tf_op jit(solution)/shard_map/ppermute | solution.py:39
  126.1 18.3 %collective-permute-start.33 = (bf16[1056,256]{1,0:T(8,128)(2,1)S(1)}, bf16[1056,256]{1,0:T(8,128)(2,1)S(1)}, u32[]{:S(2)}, u32[]{:S(2)}) collective-permute-start(bf16[1056,256]{1,0:T(8,128)(2,1)S(1)} %get-tuple-element.131), channel_id=1, source_target_pairs={{16,8},{18,10},{20,12},{22,14},{24,16},{26,18},{28,20},{30,22},{17... | collective-permute-start | bytes 1622024 | tf_op jit(solution)/shard_map/ppermute | solution.py:39
  134.3 23.3 %collective-permute-start.16 = (bf16[1056,256]{1,0:T(8,128)(2,1)S(1)}, bf16[1056,256]{1,0:T(8,128)(2,1)S(1)}, u32[]{:S(2)}, u32[]{:S(2)}) collective-permute-start(bf16[1056,256]{1,0:T(8,128)(2,1)S(1)} %get-tuple-element.102), channel_id=1, source_target_pairs={{0,8},{2,10},{4,12},{6,14},{8,16},{10,18},{12,20},{14,22},{16,24},... | collective-permute-start | bytes 1622024 | tf_op jit(solution)/shard_map/ppermute | solution.py:39
  137.7 19.9 %collective-permute-start.17 = (bf16[1056,256]{1,0:T(8,128)(2,1)S(1)}, bf16[1056,256]{1,0:T(8,128)(2,1)S(1)}, u32[]{:S(2)}, u32[]{:S(2)}) collective-permute-start(bf16[1056,256]{1,0:T(8,128)(2,1)S(1)} %get-tuple-element.103), channel_id=1, source_target_pairs={{8,0},{10,2},{12,4},{14,6},{16,8},{18,10},{20,12},{22,14},{24,16},... | collective-permute-start | bytes 1622024 | tf_op jit(solution)/shard_map/ppermute | solution.py:39
  145.1 17.6 %collective-permute-start.34 = (bf16[1056,256]{1,0:T(8,128)(2,1)S(1)}, bf16[1056,256]{1,0:T(8,128)(2,1)S(1)}, u32[]{:S(2)}, u32[]{:S(2)}) collective-permute-start(bf16[1056,256]{1,0:T(8,128)(2,1)S(1)} %get-tuple-element.134), channel_id=1, source_target_pairs={{0,8},{2,10},{4,12},{6,14},{8,16},{10,18},{12,20},{14,22},{16,24},... | collective-permute-start | bytes 1622024 | tf_op jit(solution)/shard_map/ppermute | solution.py:39
  (29 other events, 315.4 us)

commit v3 on v2

--- a/solution.py
+++ b/solution.py
@@ -15,10 +15,8 @@
 GROUP = 8
 SHARES = (1, 2)
 TIES = ((1, 1), (1, 1), 0, 1)
-SPLIT = True
-COST = 8
+SPLIT = ((1,), (2, 3), (0,))
 TIEOWN = (3, 0)
-TIES0 = 0
 ABSENT = -1e30
 NOTHING = 1e-30
 VMEM = 40 * 2**20
@@ -212,7 +210,7 @@
             pltpu.SemaphoreType.DMA((heads // group, PLANE, 2)),
         ],
         cost_estimate=pl.CostEstimate(
-            flops=4 * products * HD, bytes_accessed=COST * 2**20, transcendentals=products
+            flops=4 * products * HD, bytes_accessed=8 * 2**20, transcendentals=products
         ),
         compiler_params=pltpu.CompilerParams(vmem_limit_bytes=BIG),
         name=name,
@@ -400,17 +398,12 @@
     parts, own_parts = [], []
     for own, came, pair in zip(owns, arrived, pairs):
         given = table, bias, own, came, pair
-        if SPLIT:
-            if TIES0:
-                own_part, own_lse = attention("own_part", (0,), *given)
-                given = (*given[:2], *tie((given[2], own_lse))[:1], *given[3:])
-            sent = attention("sent_parts", tuple(range(1, planes)), *given)
-            if not TIES0:
-                own_part, own_lse = attention("own_part", (0,), *given)
-        else:
-            sent = attention("far_part", (1,), *given)
-            *rest, own_part, own_lse = attention("near_parts", (*range(2, planes), 0), *given)
-            sent = [*sent, *rest]
+        sent = []
+        for orders in SPLIT if line else ((*range(1, planes),), (0,)):
+            outs = attention("part", orders, *given)
+            if 0 in orders:
+                *outs, own_part, own_lse = outs
+            sent += outs
         parts.append([None, *sent])
         own_parts.append((own_part, own_lse))
     heads = [(span.stop - span.start) // HD for span in spans]

time: 168 us -> 165 us (0.982)
  waiting for transfers between devices: 56.6 us -> 47 us
  starting transfers between devices: 64.7 us -> 69.1 us
  Pallas kernels: 33.7 us -> 35.9 us
    ppermute x24, waiting for transfers between devices: 48.2 us -> 39 us  [along(): return lax.ppermute(array, 'seq', pairs)]
    ppermute x24, starting transfers between devices: 52.4 us -> 56.8 us  [along(): return lax.ppermute(array, 'seq', pairs)]
    pallas_call x4 -> x6, Pallas kernels: 30.8 us -> 33 us  [attention(): pl.pallas_call(partial(attend, planes, orders, heads, group, chained, sta...]
    unnamed x34 -> x36, local copies, waits for them, and re-layouts: 3.5 us -> 3.52 us
  transfers between devices with their start and end apart: 36 -> 36, of which waited for: 13 -> 12; matrix products, arithmetic and copies ran while one was open for 2% -> 2% of each run, Pallas kernels for 20% -> 22%
where the time goes in v3:
time: 165 us; the launch traced here: 164 us
  starting transfers between devices  69.1 us (42%)
  waiting for transfers between devices  47 us (28%)
  Pallas kernels  35.9 us (22%)
  local copies, waits for them, and re-layouts  5.63 us (3%)
  other arithmetic  3.17 us (2%)
  blocking collectives  2.47 us (1%)
    ppermute x24, starting transfers between devices, along(): return lax.ppermute(array, 'seq', pairs)  56.8 us
    ppermute x24, waiting for transfers between devices, along(): return lax.ppermute(array, 'seq', pairs)  39 us
    pallas_call x6, Pallas kernels, attention(): pl.pallas_call(partial(attend, planes, orders, heads, group, chained, sta...  33 us
    ppermute x12, starting transfers between devices, exchange(): return lax.ppermute(array, 'seq', [(i, i ^ flip) for i in range(shards)])  12.3 us
    ppermute x12, waiting for transfers between devices, exchange(): return lax.ppermute(array, 'seq', [(i, i ^ flip) for i in range(shards)])  8.04 us
    unnamed x36, local copies, waits for them, and re-layouts  3.52 us
  transfers between devices with their start and end apart: 36, of which 12 were waited for; matrix products, arithmetic and copies ran while one was open for 2% of the time, Pallas kernels for 22%

profile of v3, /device:TPU:0, one launch (start us, length us, event | category | flops | bytes accessed | tf_op | source)
XLA Modules:
  0.0 164.0 jit_solution(6728990265197920551)
XLA Ops:
  1.5 5.9 %collective-permute-start = (bf16[272,1024]{1,0:T(8,128)(2,1)S(1)}, bf16[272,1024]{1,0:T(8,128)(2,1)}, u32[]{:S(2)}, u32[]{:S(2)}) collective-permute-start(bf16[272,1024]{1,0:T(8,128)(2,1)S(1)} %fusion.2), channel_id=1, source_target_pairs={{0,8},{2,10},{4,12},{6,14},{8,16},{10,18},{12,20},{14,22},{16,24},... | collective-permute-start | bytes 1671176 | tf_op jit(solution)/shard_map/ppermute | solution.py:37
  12.0 5.3 %collective-permute-start.18 = (bf16[256,1024]{1,0:T(8,128)(2,1)S(1)}, bf16[256,1024]{1,0:T(8,128)(2,1)}, u32[]{:S(2)}, u32[]{:S(2)}) collective-permute-start(bf16[256,1024]{1,0:T(8,128)(2,1)S(1)} %get-tuple-element.147.refs_0_), channel_id=1, source_target_pairs={{0,8},{2,10},{4,12},{6,14},{8,16},{10,18},{12,20},{14,22},{16,24},... | collective-permute-start | bytes 1572872 | tf_op jit(solution)/shard_map/ppermute | solution.py:37
  17.3 3.6 %collective-permute-done.2.refs_9_ = bf16[256,1024]{1,0:T(8,128)(2,1)S(1)} collective-permute-done((bf16[256,1024]{1,0:T(8,128)(2,1)S(1)}, bf16[256,1024]{1,0:T(8,128)(2,1)S(1)}, u32[]{:S(2)}, u32[]{:S(2)}) %collective-permute-start.2) | collective-permute-done | bytes 524320 | tf_op jit(solution)/shard_map/ppermute | solution.py:32
  26.1 2.1 %collective-permute-done.1.refs_4_ = bf16[272,1024]{1,0:T(8,128)(2,1)} collective-permute-done((bf16[272,1024]{1,0:T(8,128)(2,1)S(1)}, bf16[272,1024]{1,0:T(8,128)(2,1)}, u32[]{:S(2)}, u32[]{:S(2)}) %collective-permute-start.1) | collective-permute-done | bytes 557088 | tf_op jit(solution)/shard_map/ppermute | solution.py:37
  30.9 8.3 %collective-permute-done.19.refs_4_ = bf16[256,1024]{1,0:T(8,128)(2,1)S(1)} collective-permute-done((bf16[256,1024]{1,0:T(8,128)(2,1)S(1)}, bf16[256,1024]{1,0:T(8,128)(2,1)S(1)}, u32[]{:S(2)}, u32[]{:S(2)}) %collective-permute-start.19) | collective-permute-done | bytes 524320 | tf_op jit(solution)/shard_map/ppermute | solution.py:37
  42.9 6.5 %collective-permute-done.5.refs_5_ = bf16[272,1024]{1,0:T(8,128)(2,1)} collective-permute-done((bf16[272,1024]{1,0:T(8,128)(2,1)}, bf16[272,1024]{1,0:T(8,128)(2,1)}, u32[]{:S(2)}, u32[]{:S(2)}) %collective-permute-start.5) | collective-permute-done | bytes 557088 | tf_op jit(solution)/shard_map/ppermute | solution.py:37
  49.9 4.3 %collective-permute-done.6.refs_10_ = bf16[256,1024]{1,0:T(8,128)(2,1)} collective-permute-done((bf16[256,1024]{1,0:T(8,128)(2,1)S(1)}, bf16[256,1024]{1,0:T(8,128)(2,1)}, u32[]{:S(2)}, u32[]{:S(2)}) %collective-permute-start.6) | collective-permute-done | bytes 524320 | tf_op jit(solution)/shard_map/ppermute | solution.py:32
  58.5 11.8 %collective-permute-done.23.refs_5_ = bf16[256,1024]{1,0:T(8,128)(2,1)} collective-permute-done((bf16[256,1024]{1,0:T(8,128)(2,1)}, bf16[256,1024]{1,0:T(8,128)(2,1)}, u32[]{:S(2)}, u32[]{:S(2)}) %collective-permute-start.23) | collective-permute-done | bytes 524320 | tf_op jit(solution)/shard_map/ppermute | solution.py:37
  74.5 1.9 %collective-permute-done.9.refs_6_ = bf16[272,1024]{1,0:T(8,128)(2,1)} collective-permute-done((bf16[272,1024]{1,0:T(8,128)(2,1)}, bf16[272,1024]{1,0:T(8,128)(2,1)}, u32[]{:S(2)}, u32[]{:S(2)}) %collective-permute-start.9) | collective-permute-done | bytes 557088 | tf_op jit(solution)/shard_map/ppermute | solution.py:37
  83.7 3.5 %part.7.other_ref = bf16[1056,256]{1,0:T(8,128)(2,1)S(1)} custom-call(s32[69]{0:T(128)S(1)} %pad_add_fusion.2.table_ref, f32[16,8,256]{2,1,0:T(8,128)S(1)} %pad.9.bias_ref, bf16[256,1024]{1,0:T(8,128)(2,1)S(1)} %get-tuple-element.148.refs_0_, bf16[272,1024]{1,0:T(8,128)(2,1)} %collective-permute-done.refs_1_, ...), custom_call_target="tpu_custom_call" | custom-call | flops 536870912 | bytes 8388608 | tf_op jit(solution)/shard_map/part/pallas_call | solution.py:200
  87.2 8.0 %collective-permute-start.12 = (bf16[1056,256]{1,0:T(8,128)(2,1)S(1)}, bf16[1056,256]{1,0:T(8,128)(2,1)S(1)}, u32[]{:S(2)}, u32[]{:S(2)}) collective-permute-start(bf16[1056,256]{1,0:T(8,128)(2,1)S(1)} %part.7.other_ref), channel_id=1, source_target_pairs={{0,8},{2,10},{4,12},{6,14},{1,9},{3,11},{5,13},{7,15}} | collective-permute-start | bytes 1622024 | tf_op jit(solution)/shard_map/ppermute | solution.py:37
  96.0 3.5 %part.11.other_ref = bf16[1056,256]{1,0:T(8,128)(2,1)S(1)} custom-call(s32[69]{0:T(128)S(1)} %pad_add_fusion.2.table_ref, f32[16,8,256]{2,1,0:T(8,128)S(1)} %pad.9.bias_ref, bf16[256,1024]{1,0:T(8,128)(2,1)S(1)} %get-tuple-element.147.refs_0_, bf16[256,1024]{1,0:T(8,128)(2,1)} %collective-permute-done.18.refs_1_, ...), custom_call_target="tpu_custom_call" | custom-call | flops 536870912 | bytes 8388608 | tf_op jit(solution)/shard_map/part/pallas_call | solution.py:200
  99.5 3.6 %collective-permute-start.30 = (bf16[1056,256]{1,0:T(8,128)(2,1)S(1)}, bf16[1056,256]{1,0:T(8,128)(2,1)S(1)}, u32[]{:S(2)}, u32[]{:S(2)}) collective-permute-start(bf16[1056,256]{1,0:T(8,128)(2,1)S(1)} %part.11.other_ref), channel_id=1, source_target_pairs={{0,8},{2,10},{4,12},{6,14},{1,9},{3,11},{5,13},{7,15}} | collective-permute-start | bytes 1622024 | tf_op jit(solution)/shard_map/ppermute | solution.py:37
  103.9 6.2 %part.6 = (bf16[1056,256]{1,0:T(8,128)(2,1)S(1)}, bf16[1056,256]{1,0:T(8,128)(2,1)S(1)}) custom-call(s32[69]{0:T(128)S(1)} %pad_add_fusion.2.table_ref, f32[16,8,256]{2,1,0:T(8,128)S(1)} %pad.9.bias_ref, bf16[256,1024]{1,0:T(8,128)(2,1)S(1)} %get-tuple-element.148.refs_0_, bf16[272,1024]{1,0:T(8,128)(2,1)} %collective-permute-done.refs_1_, ...), custom_call_target="tpu_custom_call" | custom-call | flops 1073741824 | bytes 8388608 | tf_op jit(solution)/shard_map/part/pallas_call | solution.py:200
  110.6 2.1 %collective-permute-start.14 = (bf16[1056,256]{1,0:T(8,128)(2,1)S(1)}, bf16[1056,256]{1,0:T(8,128)(2,1)S(1)}, u32[]{:S(2)}, u32[]{:S(2)}) collective-permute-start(bf16[1056,256]{1,0:T(8,128)(2,1)S(1)} %get-tuple-element.89), channel_id=1, source_target_pairs={{0,8},{2,10},{4,12},{6,14},{8,16},{10,18},{12,20},{14,22},{1,9},{3... | collective-permute-start | bytes 1622024 | tf_op jit(solution)/shard_map/ppermute | solution.py:37
  113.4 5.9 %part.10 = (bf16[1056,256]{1,0:T(8,128)(2,1)S(1)}, bf16[1056,256]{1,0:T(8,128)(2,1)S(1)}) custom-call(s32[69]{0:T(128)S(1)} %pad_add_fusion.2.table_ref, f32[16,8,256]{2,1,0:T(8,128)S(1)} %pad.9.bias_ref, bf16[256,1024]{1,0:T(8,128)(2,1)S(1)} %get-tuple-element.147.refs_0_, bf16[256,1024]{1,0:T(8,128)(2,1)} %collective-permute-done.18.refs_1_, ...), custom_call_target="tpu_custom_call" | custom-call | flops 1073741824 | bytes 8388608 | tf_op jit(solution)/shard_map/part/pallas_call | solution.py:200
  119.9 4.4 %collective-permute-start.32 = (bf16[1056,256]{1,0:T(8,128)(2,1)S(1)}, bf16[1056,256]{1,0:T(8,128)(2,1)S(1)}, u32[]{:S(2)}, u32[]{:S(2)}) collective-permute-start(bf16[1056,256]{1,0:T(8,128)(2,1)S(1)} %get-tuple-element.126), channel_id=1, source_target_pairs={{0,8},{2,10},{4,12},{6,14},{8,16},{10,18},{12,20},{14,22},{1,9},{3... | collective-permute-start | bytes 1622024 | tf_op jit(solution)/shard_map/ppermute | solution.py:37
  125.0 6.9 %part.8 = (f32[1024,256]{1,0:T(8,128)S(1)}, f32[8,256]{1,0:T(8,128)S(1)}) custom-call(s32[69]{0:T(128)S(1)} %pad_add_fusion.2.table_ref, f32[16,8,256]{2,1,0:T(8,128)S(1)} %pad.9.bias_ref, bf16[256,1024]{1,0:T(8,128)(2,1)S(1)} %get-tuple-element.148.refs_0_, bf16[272,1024]{1,0:T(8,128)(2,1)} %collective-permute-done.refs_1_, ...), custom_call_target="tpu_custom_call" | custom-call | flops 536870912 | bytes 8388608 | tf_op jit(solution)/shard_map/part/pallas_call | solution.py:200
  132.4 4.3 %collective-permute-start.16 = (bf16[1056,256]{1,0:T(8,128)(2,1)S(1)}, bf16[1056,256]{1,0:T(8,128)(2,1)S(1)}, u32[]{:S(2)}, u32[]{:S(2)}) collective-permute-start(bf16[1056,256]{1,0:T(8,128)(2,1)S(1)} %get-tuple-element.99), channel_id=1, source_target_pairs={{0,8},{2,10},{4,12},{6,14},{8,16},{10,18},{12,20},{14,22},{16,24},... | collective-permute-start | bytes 1622024 | tf_op jit(solution)/shard_map/ppermute | solution.py:37
  138.1 4.5 %collective-permute-done.32.up_ref = bf16[1056,256]{1,0:T(8,128)(2,1)S(1)} collective-permute-done((bf16[1056,256]{1,0:T(8,128)(2,1)S(1)}, bf16[1056,256]{1,0:T(8,128)(2,1)S(1)}, u32[]{:S(2)}, u32[]{:S(2)}) %collective-permute-start.32) | collective-permute-done | bytes 540704 | tf_op jit(solution)/shard_map/ppermute | solution.py:37
  143.3 4.2 %collective-permute-start.34 = (bf16[1056,256]{1,0:T(8,128)(2,1)S(1)}, bf16[1056,256]{1,0:T(8,128)(2,1)S(1)}, u32[]{:S(2)}, u32[]{:S(2)}) collective-permute-start(bf16[1056,256]{1,0:T(8,128)(2,1)S(1)} %get-tuple-element.130), channel_id=1, source_target_pairs={{0,8},{2,10},{4,12},{6,14},{8,16},{10,18},{12,20},{14,22},{16,24},... | collective-permute-start | bytes 1622024 | tf_op jit(solution)/shard_map/ppermute | solution.py:37
  148.8 6.9 %part.9 = (f32[1024,256]{1,0:T(8,128)S(1)}, f32[8,256]{1,0:T(8,128)S(1)}) custom-call(s32[69]{0:T(128)S(1)} %pad_add_fusion.2.table_ref, f32[16,8,256]{2,1,0:T(8,128)S(1)} %pad.9.bias_ref, bf16[256,1024]{1,0:T(8,128)(2,1)S(1)} %get-tuple-element.147.refs_0_, bf16[256,1024]{1,0:T(8,128)(2,1)} %collective-permute-done.18.refs_1_, ...), custom_call_target="tpu_custom_call" | custom-call | flops 536870912 | bytes 8388608 | tf_op jit(solution)/shard_map/part/pallas_call | solution.py:200
  156.2 3.7 %collective-permute-done.34.refs_0_ = bf16[1056,256]{1,0:T(8,128)(2,1)S(1)} collective-permute-done((bf16[1056,256]{1,0:T(8,128)(2,1)S(1)}, bf16[1056,256]{1,0:T(8,128)(2,1)S(1)}, u32[]{:S(2)}, u32[]{:S(2)}) %collective-permute-start.34) | collective-permute-done | bytes 540704 | tf_op jit(solution)/shard_map/ppermute | solution.py:37
  160.3 2.5 %psum.7 = f32[256]{0:T(256)S(1)} all-reduce(f32[256]{0:T(256)S(1)} %bitcast.15), channel_id=1, replica_groups=mesh['seq'=16,'head'=2] {'head'}, use_global_device_ids=true, to_apply=%region_7.8 | all-reduce | flops 256 | bytes 2048 | tf_op jit(solution)/shard_map/psum | solution.py:427
  (129 shorter events, 43.3 us)
Async XLA Ops:
  1.5 23.1 %collective-permute-start = (bf16[272,1024]{1,0:T(8,128)(2,1)S(1)}, bf16[272,1024]{1,0:T(8,128)(2,1)}, u32[]{:S(2)}, u32[]{:S(2)}) collective-permute-start(bf16[272,1024]{1,0:T(8,128)(2,1)S(1)} %fusion.2), channel_id=1, source_target_pairs={{0,8},{2,10},{4,12},{6,14},{8,16},{10,18},{12,20},{14,22},{16,24},... | collective-permute-start | bytes 1671176 | tf_op jit(solution)/shard_map/ppermute | solution.py:37
  10.7 17.4 %collective-permute-start.1 = (bf16[272,1024]{1,0:T(8,128)(2,1)S(1)}, bf16[272,1024]{1,0:T(8,128)(2,1)}, u32[]{:S(2)}, u32[]{:S(2)}) collective-permute-start(bf16[272,1024]{1,0:T(8,128)(2,1)S(1)} %fusion.2), channel_id=1, source_target_pairs={{8,0},{10,2},{12,4},{14,6},{16,8},{18,10},{20,12},{22,14},{24,16},... | collective-permute-start | bytes 1671176 | tf_op jit(solution)/shard_map/ppermute | solution.py:37
  12.0 17.7 %collective-permute-start.18 = (bf16[256,1024]{1,0:T(8,128)(2,1)S(1)}, bf16[256,1024]{1,0:T(8,128)(2,1)}, u32[]{:S(2)}, u32[]{:S(2)}) collective-permute-start(bf16[256,1024]{1,0:T(8,128)(2,1)S(1)} %get-tuple-element.147.refs_0_), channel_id=1, source_target_pairs={{0,8},{2,10},{4,12},{6,14},{8,16},{10,18},{12,20},{14,22},{16,24},... | collective-permute-start | bytes 1572872 | tf_op jit(solution)/shard_map/ppermute | solution.py:37
  20.9 18.3 %collective-permute-start.19 = (bf16[256,1024]{1,0:T(8,128)(2,1)S(1)}, bf16[256,1024]{1,0:T(8,128)(2,1)S(1)}, u32[]{:S(2)}, u32[]{:S(2)}) collective-permute-start(bf16[256,1024]{1,0:T(8,128)(2,1)S(1)} %get-tuple-element.147.refs_0_), channel_id=1, source_target_pairs={{8,0},{10,2},{12,4},{14,6},{16,8},{18,10},{20,12},{22,14},{24,16},... | collective-permute-start | bytes 1572872 | tf_op jit(solution)/shard_map/ppermute | solution.py:37
  29.6 19.7 %collective-permute-start.5 = (bf16[272,1024]{1,0:T(8,128)(2,1)}, bf16[272,1024]{1,0:T(8,128)(2,1)}, u32[]{:S(2)}, u32[]{:S(2)}) collective-permute-start(bf16[272,1024]{1,0:T(8,128)(2,1)} %collective-permute-done.1.refs_4_), channel_id=1, source_target_pairs={{8,0},{10,2},{12,4},{14,6},{16,8},{18,10},{20,12},{22,14},{9,1},{1... | collective-permute-start | bytes 1671176 | tf_op jit(solution)/shard_map/ppermute | solution.py:37
  39.3 16.2 %collective-permute-start.7 = (bf16[256,1024]{1,0:T(8,128)(2,1)S(1)}, bf16[256,1024]{1,0:T(8,128)(2,1)}, u32[]{:S(2)}, u32[]{:S(2)}) collective-permute-start(bf16[256,1024]{1,0:T(8,128)(2,1)S(1)} %get-tuple-element.146.refs_7_), channel_id=1, source_target_pairs={{0,4},{2,6},{4,0},{6,2},{8,12},{10,14},{12,8},{14,10},{16,20},{18,... | collective-permute-start | bytes 1572872 | tf_op jit(solution)/shard_map/ppermute | solution.py:32
  40.0 17.0 %collective-permute-start.22 = (bf16[256,1024]{1,0:T(8,128)(2,1)}, bf16[256,1024]{1,0:T(8,128)(2,1)}, u32[]{:S(2)}, u32[]{:S(2)}) collective-permute-start(bf16[256,1024]{1,0:T(8,128)(2,1)} %collective-permute-done.18.refs_1_), channel_id=1, source_target_pairs={{8,16},{10,18},{12,20},{14,22},{16,24},{18,26},{20,28},{22,30},{9,... | collective-permute-start | bytes 1572872 | tf_op jit(solution)/shard_map/ppermute | solution.py:37
  41.5 29.7 %collective-permute-start.24 = (bf16[256,1024]{1,0:T(8,128)(2,1)S(1)}, bf16[256,1024]{1,0:T(8,128)(2,1)}, u32[]{:S(2)}, u32[]{:S(2)}) collective-permute-start(bf16[256,1024]{1,0:T(8,128)(2,1)S(1)} %get-tuple-element.107.refs_8_), channel_id=1, source_target_pairs={{0,2},{2,0},{4,6},{6,4},{8,10},{10,8},{12,14},{14,12},{16,18},{18,... | collective-permute-start | bytes 1572872 | tf_op jit(solution)/shard_map/ppermute | solution.py:32
  49.4 22.2 %collective-permute-start.25 = (bf16[256,1024]{1,0:T(8,128)(2,1)S(1)}, bf16[256,1024]{1,0:T(8,128)(2,1)}, u32[]{:S(2)}, u32[]{:S(2)}) collective-permute-start(bf16[256,1024]{1,0:T(8,128)(2,1)S(1)} %get-tuple-element.106.refs_7_), channel_id=1, source_target_pairs={{0,4},{2,6},{4,0},{6,2},{8,12},{10,14},{12,8},{14,10},{16,20},{18,... | collective-permute-start | bytes 1572872 | tf_op jit(solution)/shard_map/ppermute | solution.py:32
  55.5 17.6 %collective-permute-start.8 = (bf16[272,1024]{1,0:T(8,128)(2,1)}, bf16[272,1024]{1,0:T(8,128)(2,1)}, u32[]{:S(2)}, u32[]{:S(2)}) collective-permute-start(bf16[272,1024]{1,0:T(8,128)(2,1)} %collective-permute-done.4.refs_2_), channel_id=1, source_target_pairs={{16,24},{18,26},{20,28},{22,30},{17,25},{19,27},{21,29},{23,31}} | collective-permute-start | bytes 1671176 | tf_op jit(solution)/shard_map/ppermute | solution.py:37
  57.0 19.4 %collective-permute-start.9 = (bf16[272,1024]{1,0:T(8,128)(2,1)}, bf16[272,1024]{1,0:T(8,128)(2,1)}, u32[]{:S(2)}, u32[]{:S(2)}) collective-permute-start(bf16[272,1024]{1,0:T(8,128)(2,1)} %collective-permute-done.5.refs_5_), channel_id=1, source_target_pairs={{8,0},{10,2},{12,4},{14,6},{9,1},{11,3},{13,5},{15,7}} | collective-permute-start | bytes 1671176 | tf_op jit(solution)/shard_map/ppermute | solution.py:37
  71.6 24.3 %collective-permute-start.28 = (bf16[256,1024]{1,0:T(8,128)(2,1)}, bf16[256,1024]{1,0:T(8,128)(2,1)}, u32[]{:S(2)}, u32[]{:S(2)}) collective-permute-start(bf16[256,1024]{1,0:T(8,128)(2,1)} %copy-done.2), channel_id=1, source_target_pairs={{0,4},{2,6},{4,0},{6,2},{8,12},{10,14},{12,8},{14,10},{16,20},{18,... | collective-permute-start | bytes 1572872 | tf_op jit(solution)/shard_map/ppermute | solution.py:32
  73.1 22.8 %collective-permute-start.29 = (bf16[256,1024]{1,0:T(8,128)(2,1)}, bf16[256,1024]{1,0:T(8,128)(2,1)}, u32[]{:S(2)}, u32[]{:S(2)}) collective-permute-start(bf16[256,1024]{1,0:T(8,128)(2,1)} %copy-done.4), channel_id=1, source_target_pairs={{0,2},{2,0},{4,6},{6,4},{8,10},{10,8},{12,14},{14,12},{16,18},{18,... | collective-permute-start | bytes 1572872 | tf_op jit(solution)/shard_map/ppermute | solution.py:32
  76.4 18.9 %collective-permute-start.26 = (bf16[256,1024]{1,0:T(8,128)(2,1)}, bf16[256,1024]{1,0:T(8,128)(2,1)}, u32[]{:S(2)}, u32[]{:S(2)}) collective-permute-start(bf16[256,1024]{1,0:T(8,128)(2,1)} %collective-permute-done.22.refs_2_), channel_id=1, source_target_pairs={{16,24},{18,26},{20,28},{22,30},{17,25},{19,27},{21,29},{23,31}} | collective-permute-start | bytes 1572872 | tf_op jit(solution)/shard_map/ppermute | solution.py:37
  87.2 22.9 %collective-permute-start.12 = (bf16[1056,256]{1,0:T(8,128)(2,1)S(1)}, bf16[1056,256]{1,0:T(8,128)(2,1)S(1)}, u32[]{:S(2)}, u32[]{:S(2)}) collective-permute-start(bf16[1056,256]{1,0:T(8,128)(2,1)S(1)} %part.7.other_ref), channel_id=1, source_target_pairs={{0,8},{2,10},{4,12},{6,14},{1,9},{3,11},{5,13},{7,15}} | collective-permute-start | bytes 1622024 | tf_op jit(solution)/shard_map/ppermute | solution.py:37
  99.5 19.9 %collective-permute-start.30 = (bf16[1056,256]{1,0:T(8,128)(2,1)S(1)}, bf16[1056,256]{1,0:T(8,128)(2,1)S(1)}, u32[]{:S(2)}, u32[]{:S(2)}) collective-permute-start(bf16[1056,256]{1,0:T(8,128)(2,1)S(1)} %part.11.other_ref), channel_id=1, source_target_pairs={{0,8},{2,10},{4,12},{6,14},{1,9},{3,11},{5,13},{7,15}} | collective-permute-start | bytes 1622024 | tf_op jit(solution)/shard_map/ppermute | solution.py:37
  103.1 16.3 %collective-permute-start.31 = (bf16[1056,256]{1,0:T(8,128)(2,1)S(1)}, bf16[1056,256]{1,0:T(8,128)(2,1)S(1)}, u32[]{:S(2)}, u32[]{:S(2)}) collective-permute-start(bf16[1056,256]{1,0:T(8,128)(2,1)S(1)} %part.11.other_ref), channel_id=1, source_target_pairs={{24,16},{26,18},{28,20},{30,22},{25,17},{27,19},{29,21},{31,23}} | collective-permute-start | bytes 1622024 | tf_op jit(solution)/shard_map/ppermute | solution.py:37
  110.6 21.4 %collective-permute-start.14 = (bf16[1056,256]{1,0:T(8,128)(2,1)S(1)}, bf16[1056,256]{1,0:T(8,128)(2,1)S(1)}, u32[]{:S(2)}, u32[]{:S(2)}) collective-permute-start(bf16[1056,256]{1,0:T(8,128)(2,1)S(1)} %get-tuple-element.89), channel_id=1, source_target_pairs={{0,8},{2,10},{4,12},{6,14},{8,16},{10,18},{12,20},{14,22},{1,9},{3... | collective-permute-start | bytes 1622024 | tf_op jit(solution)/shard_map/ppermute | solution.py:37
  112.7 19.3 %collective-permute-start.15 = (bf16[1056,256]{1,0:T(8,128)(2,1)S(1)}, bf16[1056,256]{1,0:T(8,128)(2,1)S(1)}, u32[]{:S(2)}, u32[]{:S(2)}) collective-permute-start(bf16[1056,256]{1,0:T(8,128)(2,1)S(1)} %get-tuple-element.90), channel_id=1, source_target_pairs={{16,8},{18,10},{20,12},{22,14},{24,16},{26,18},{28,20},{30,22},{17... | collective-permute-start | bytes 1622024 | tf_op jit(solution)/shard_map/ppermute | solution.py:37
  119.9 22.7 %collective-permute-start.32 = (bf16[1056,256]{1,0:T(8,128)(2,1)S(1)}, bf16[1056,256]{1,0:T(8,128)(2,1)S(1)}, u32[]{:S(2)}, u32[]{:S(2)}) collective-permute-start(bf16[1056,256]{1,0:T(8,128)(2,1)S(1)} %get-tuple-element.126), channel_id=1, source_target_pairs={{0,8},{2,10},{4,12},{6,14},{8,16},{10,18},{12,20},{14,22},{1,9},{3... | collective-permute-start | bytes 1622024 | tf_op jit(solution)/shard_map/ppermute | solution.py:37
  124.3 18.3 %collective-permute-start.33 = (bf16[1056,256]{1,0:T(8,128)(2,1)S(1)}, bf16[1056,256]{1,0:T(8,128)(2,1)S(1)}, u32[]{:S(2)}, u32[]{:S(2)}) collective-permute-start(bf16[1056,256]{1,0:T(8,128)(2,1)S(1)} %get-tuple-element.127), channel_id=1, source_target_pairs={{16,8},{18,10},{20,12},{22,14},{24,16},{26,18},{28,20},{30,22},{17... | collective-permute-start | bytes 1622024 | tf_op jit(solution)/shard_map/ppermute | solution.py:37
  132.4 23.3 %collective-permute-start.16 = (bf16[1056,256]{1,0:T(8,128)(2,1)S(1)}, bf16[1056,256]{1,0:T(8,128)(2,1)S(1)}, u32[]{:S(2)}, u32[]{:S(2)}) collective-permute-start(bf16[1056,256]{1,0:T(8,128)(2,1)S(1)} %get-tuple-element.99), channel_id=1, source_target_pairs={{0,8},{2,10},{4,12},{6,14},{8,16},{10,18},{12,20},{14,22},{16,24},... | collective-permute-start | bytes 1622024 | tf_op jit(solution)/shard_map/ppermute | solution.py:37
  136.8 19.0 %collective-permute-start.17 = (bf16[1056,256]{1,0:T(8,128)(2,1)S(1)}, bf16[1056,256]{1,0:T(8,128)(2,1)S(1)}, u32[]{:S(2)}, u32[]{:S(2)}) collective-permute-start(bf16[1056,256]{1,0:T(8,128)(2,1)S(1)} %get-tuple-element.100), channel_id=1, source_target_pairs={{8,0},{10,2},{12,4},{14,6},{16,8},{18,10},{20,12},{22,14},{24,16},... | collective-permute-start | bytes 1622024 | tf_op jit(solution)/shard_map/ppermute | solution.py:37
  143.3 16.6 %collective-permute-start.34 = (bf16[1056,256]{1,0:T(8,128)(2,1)S(1)}, bf16[1056,256]{1,0:T(8,128)(2,1)S(1)}, u32[]{:S(2)}, u32[]{:S(2)}) collective-permute-start(bf16[1056,256]{1,0:T(8,128)(2,1)S(1)} %get-tuple-element.130), channel_id=1, source_target_pairs={{0,8},{2,10},{4,12},{6,14},{8,16},{10,18},{12,20},{14,22},{16,24},... | collective-permute-start | bytes 1622024 | tf_op jit(solution)/shard_map/ppermute | solution.py:37
  (30 other events, 343.7 us)

commit v4 on v3

--- a/solution.py
+++ b/solution.py
@@ -14,7 +14,7 @@
 PLANE = 4
 GROUP = 8
 SHARES = (1, 2)
-TIES = ((1, 1), (1, 1), 0, 1)
+TIES = ((1, 1), (0, 1), 0, 0)
 SPLIT = ((1,), (2, 3), (0,))
 TIEOWN = (3, 0)
 ABSENT = -1e30
@@ -352,6 +352,8 @@
             if hop == 2:
                 up, down, *first = tie((up, down, near[c][0], far[c][1]) if TIES[0][c] else (up, down))
                 near[c][0], far[c][1] = first or (near[c][0], far[c][1])
+            if hop == 3 and c == 0:
+                up, down, *diagonal[0] = tie((up, down, *diagonal[0]))
             if hop == 3:
                 up, down, *second = tie((up, down, near[c][1], far[c][0]) if TIES[1][c] else (up, down))
                 near[c][1], far[c][0] = second or (near[c][1], far[c][0])

time: 165 us -> 164 us (level)
  local copies, waits for them, and re-layouts: 5.63 us -> 2.16 us
  Pallas kernels: 35.9 us -> 39.1 us
    ppermute x24, starting transfers between devices: 56.8 us -> 52.5 us  [along(): return lax.ppermute(array, 'seq', pairs)]
    unnamed x36 -> x24, local copies, waits for them, and re-layouts: 3.52 us -> 0.05 us
    ppermute x12, starting transfers between devices: 12.3 us -> 15.5 us  [exchange(): return lax.ppermute(array, 'seq', [(i, i ^ flip) for i in range(shards)])]
    pallas_call x6, Pallas kernels: 33 us -> 36.1 us  [attention(): pl.pallas_call(partial(attend, planes, orders, heads, group, chained, sta...]
  transfers between devices with their start and end apart: 36 -> 36, of which waited for: 12 -> 10; matrix products, arithmetic and copies ran while one was open for 2% -> 2% of each run, Pallas kernels for 22% -> 23%
where the time goes in v4:
time: 164 us; the launch traced here: 163 us
  starting transfers between devices  68 us (41%)
  waiting for transfers between devices  47.7 us (29%)
  Pallas kernels  39.1 us (24%)
  other arithmetic  3.17 us (2%)
  blocking collectives  2.47 us (2%)
  local copies, waits for them, and re-layouts  2.16 us (1%)
    ppermute x24, starting transfers between devices, along(): return lax.ppermute(array, 'seq', pairs)  52.5 us
    ppermute x24, waiting for transfers between devices, along(): return lax.ppermute(array, 'seq', pairs)  38.3 us
    pallas_call x6, Pallas kernels, attention(): pl.pallas_call(partial(attend, planes, orders, heads, group, chained, sta...  36.1 us
    ppermute x12, starting transfers between devices, exchange(): return lax.ppermute(array, 'seq', [(i, i ^ flip) for i in range(shards)])  15.5 us
    ppermute x12, waiting for transfers between devices, exchange(): return lax.ppermute(array, 'seq', [(i, i ^ flip) for i in range(shards)])  9.47 us
  transfers between devices with their start and end apart: 36, of which 10 were waited for; matrix products, arithmetic and copies ran while one was open for 2% of the time, Pallas kernels for 23%

profile of v4, /device:TPU:0, one launch (start us, length us, event | category | flops | bytes accessed | tf_op | source)
XLA Modules:
  0.0 163.1 jit_solution(12310511750171509838)
XLA Ops:
  1.5 5.9 %collective-permute-start = (bf16[272,1024]{1,0:T(8,128)(2,1)S(1)}, bf16[272,1024]{1,0:T(8,128)(2,1)}, u32[]{:S(2)}, u32[]{:S(2)}) collective-permute-start(bf16[272,1024]{1,0:T(8,128)(2,1)S(1)} %fusion.2), channel_id=1, source_target_pairs={{0,8},{2,10},{4,12},{6,14},{8,16},{10,18},{12,20},{14,22},{16,24},... | collective-permute-start | bytes 1671176 | tf_op jit(solution)/shard_map/ppermute | solution.py:37
  8.8 1.6 collective-permute-start.2
  10.4 1.6 collective-permute-start.3
  12.0 5.3 %collective-permute-start.18 = (bf16[256,1024]{1,0:T(8,128)(2,1)S(1)}, bf16[256,1024]{1,0:T(8,128)(2,1)}, u32[]{:S(2)}, u32[]{:S(2)}) collective-permute-start(bf16[256,1024]{1,0:T(8,128)(2,1)S(1)} %get-tuple-element.147.refs_0_), channel_id=1, source_target_pairs={{0,8},{2,10},{4,12},{6,14},{8,16},{10,18},{12,20},{14,22},{16,24},... | collective-permute-start | bytes 1572872 | tf_op jit(solution)/shard_map/ppermute | solution.py:37
  17.4 5.0 %collective-permute-done.2.refs_9_ = bf16[256,1024]{1,0:T(8,128)(2,1)} collective-permute-done((bf16[256,1024]{1,0:T(8,128)(2,1)S(1)}, bf16[256,1024]{1,0:T(8,128)(2,1)}, u32[]{:S(2)}, u32[]{:S(2)}) %collective-permute-start.2) | collective-permute-done | bytes 524320 | tf_op jit(solution)/shard_map/ppermute | solution.py:32
  30.9 8.4 %collective-permute-done.19.refs_4_ = bf16[256,1024]{1,0:T(8,128)(2,1)S(1)} collective-permute-done((bf16[256,1024]{1,0:T(8,128)(2,1)S(1)}, bf16[256,1024]{1,0:T(8,128)(2,1)S(1)}, u32[]{:S(2)}, u32[]{:S(2)}) %collective-permute-start.19) | collective-permute-done | bytes 524320 | tf_op jit(solution)/shard_map/ppermute | solution.py:37
  39.4 1.6 collective-permute-start.6
  44.5 4.5 %collective-permute-done.5.refs_5_ = bf16[272,1024]{1,0:T(8,128)(2,1)} collective-permute-done((bf16[272,1024]{1,0:T(8,128)(2,1)}, bf16[272,1024]{1,0:T(8,128)(2,1)}, u32[]{:S(2)}, u32[]{:S(2)}) %collective-permute-start.5) | collective-permute-done | bytes 557088 | tf_op jit(solution)/shard_map/ppermute | solution.py:37
  51.9 3.9 %collective-permute-done.7.refs_14_ = bf16[256,1024]{1,0:T(8,128)(2,1)} collective-permute-done((bf16[256,1024]{1,0:T(8,128)(2,1)}, bf16[256,1024]{1,0:T(8,128)(2,1)}, u32[]{:S(2)}, u32[]{:S(2)}) %collective-permute-start.7) | collective-permute-done | bytes 524320 | tf_op jit(solution)/shard_map/ppermute | solution.py:32
  58.8 8.9 %collective-permute-done.23.refs_5_ = bf16[256,1024]{1,0:T(8,128)(2,1)} collective-permute-done((bf16[256,1024]{1,0:T(8,128)(2,1)}, bf16[256,1024]{1,0:T(8,128)(2,1)}, u32[]{:S(2)}, u32[]{:S(2)}) %collective-permute-start.23) | collective-permute-done | bytes 524320 | tf_op jit(solution)/shard_map/ppermute | solution.py:37
  71.7 4.3 %collective-permute-done.9.refs_6_ = bf16[272,1024]{1,0:T(8,128)(2,1)} collective-permute-done((bf16[272,1024]{1,0:T(8,128)(2,1)}, bf16[272,1024]{1,0:T(8,128)(2,1)}, u32[]{:S(2)}, u32[]{:S(2)}) %collective-permute-start.9) | collective-permute-done | bytes 557088 | tf_op jit(solution)/shard_map/ppermute | solution.py:37
  81.8 3.8 %part.7.other_ref = bf16[1056,256]{1,0:T(8,128)(2,1)S(1)} custom-call(s32[69]{0:T(128)S(1)} %pad_add_fusion.2.table_ref, f32[16,8,256]{2,1,0:T(8,128)S(1)} %pad.9.bias_ref, bf16[256,1024]{1,0:T(8,128)(2,1)S(1)} %get-tuple-element.148.refs_0_, bf16[272,1024]{1,0:T(8,128)(2,1)} %collective-permute-done.refs_1_, ...), custom_call_target="tpu_custom_call" | custom-call | flops 536870912 | bytes 8388608 | tf_op jit(solution)/shard_map/part/pallas_call | solution.py:200
  85.6 7.8 %collective-permute-start.12 = (bf16[1056,256]{1,0:T(8,128)(2,1)S(1)}, bf16[1056,256]{1,0:T(8,128)(2,1)S(1)}, u32[]{:S(2)}, u32[]{:S(2)}) collective-permute-start(bf16[1056,256]{1,0:T(8,128)(2,1)S(1)} %part.7.other_ref), channel_id=1, source_target_pairs={{0,8},{2,10},{4,12},{6,14},{1,9},{3,11},{5,13},{7,15}} | collective-permute-start | bytes 1622024 | tf_op jit(solution)/shard_map/ppermute | solution.py:37
  94.1 3.5 %part.11.other_ref = bf16[1056,256]{1,0:T(8,128)(2,1)S(1)} custom-call(s32[69]{0:T(128)S(1)} %pad_add_fusion.2.table_ref, f32[16,8,256]{2,1,0:T(8,128)S(1)} %pad.9.bias_ref, bf16[256,1024]{1,0:T(8,128)(2,1)S(1)} %get-tuple-element.147.refs_0_, bf16[256,1024]{1,0:T(8,128)(2,1)} %collective-permute-done.18.refs_1_, ...), custom_call_target="tpu_custom_call" | custom-call | flops 536870912 | bytes 8388608 | tf_op jit(solution)/shard_map/part/pallas_call | solution.py:200
  97.6 3.6 %collective-permute-start.30 = (bf16[1056,256]{1,0:T(8,128)(2,1)S(1)}, bf16[1056,256]{1,0:T(8,128)(2,1)S(1)}, u32[]{:S(2)}, u32[]{:S(2)}) collective-permute-start(bf16[1056,256]{1,0:T(8,128)(2,1)S(1)} %part.11.other_ref), channel_id=1, source_target_pairs={{0,8},{2,10},{4,12},{6,14},{1,9},{3,11},{5,13},{7,15}} | collective-permute-start | bytes 1622024 | tf_op jit(solution)/shard_map/ppermute | solution.py:37
  102.0 7.6 %part.6 = (bf16[1056,256]{1,0:T(8,128)(2,1)S(1)}, bf16[1056,256]{1,0:T(8,128)(2,1)S(1)}) custom-call(s32[69]{0:T(128)S(1)} %pad_add_fusion.2.table_ref, f32[16,8,256]{2,1,0:T(8,128)S(1)} %pad.9.bias_ref, bf16[256,1024]{1,0:T(8,128)(2,1)S(1)} %get-tuple-element.148.refs_0_, bf16[272,1024]{1,0:T(8,128)(2,1)} %collective-permute-done.refs_1_, ...), custom_call_target="tpu_custom_call" | custom-call | flops 1073741824 | bytes 8388608 | tf_op jit(solution)/shard_map/part/pallas_call | solution.py:200
  112.1 7.0 %part.10 = (bf16[1056,256]{1,0:T(8,128)(2,1)S(1)}, bf16[1056,256]{1,0:T(8,128)(2,1)S(1)}) custom-call(s32[69]{0:T(128)S(1)} %pad_add_fusion.2.table_ref, f32[16,8,256]{2,1,0:T(8,128)S(1)} %pad.9.bias_ref, bf16[256,1024]{1,0:T(8,128)(2,1)S(1)} %get-tuple-element.147.refs_0_, bf16[256,1024]{1,0:T(8,128)(2,1)} %collective-permute-done.18.refs_1_, ...), custom_call_target="tpu_custom_call" | custom-call | flops 1073741824 | bytes 8388608 | tf_op jit(solution)/shard_map/part/pallas_call | solution.py:200
  121.7 7.2 %part.8 = (f32[1024,256]{1,0:T(8,128)S(1)}, f32[8,256]{1,0:T(8,128)S(1)}) custom-call(s32[69]{0:T(128)S(1)} %pad_add_fusion.2.table_ref, f32[16,8,256]{2,1,0:T(8,128)S(1)} %pad.9.bias_ref, bf16[256,1024]{1,0:T(8,128)(2,1)S(1)} %get-tuple-element.148.refs_0_, bf16[272,1024]{1,0:T(8,128)(2,1)} %collective-permute-done.refs_1_, ...), custom_call_target="tpu_custom_call" | custom-call | flops 536870912 | bytes 8388608 | tf_op jit(solution)/shard_map/part/pallas_call | solution.py:200
  129.4 4.0 %collective-permute-start.16 = (bf16[1056,256]{1,0:T(8,128)(2,1)S(1)}, bf16[1056,256]{1,0:T(8,128)(2,1)S(1)}, u32[]{:S(2)}, u32[]{:S(2)}) collective-permute-start(bf16[1056,256]{1,0:T(8,128)(2,1)S(1)} %get-tuple-element.101), channel_id=1, source_target_pairs={{0,8},{2,10},{4,12},{6,14},{8,16},{10,18},{12,20},{14,22},{16,24},... | collective-permute-start | bytes 1622024 | tf_op jit(solution)/shard_map/ppermute | solution.py:37
  134.7 4.3 %collective-permute-done.32.up_ref = bf16[1056,256]{1,0:T(8,128)(2,1)S(1)} collective-permute-done((bf16[1056,256]{1,0:T(8,128)(2,1)S(1)}, bf16[1056,256]{1,0:T(8,128)(2,1)S(1)}, u32[]{:S(2)}, u32[]{:S(2)}) %collective-permute-start.32) | collective-permute-done | bytes 540704 | tf_op jit(solution)/shard_map/ppermute | solution.py:37
  139.6 4.2 %collective-permute-start.34 = (bf16[1056,256]{1,0:T(8,128)(2,1)S(1)}, bf16[1056,256]{1,0:T(8,128)(2,1)S(1)}, u32[]{:S(2)}, u32[]{:S(2)}) collective-permute-start(bf16[1056,256]{1,0:T(8,128)(2,1)S(1)} %get-tuple-element.130), channel_id=1, source_target_pairs={{0,8},{2,10},{4,12},{6,14},{8,16},{10,18},{12,20},{14,22},{16,24},... | collective-permute-start | bytes 1622024 | tf_op jit(solution)/shard_map/ppermute | solution.py:37
  145.2 6.9 %part.9 = (f32[1024,256]{1,0:T(8,128)S(1)}, f32[8,256]{1,0:T(8,128)S(1)}) custom-call(s32[69]{0:T(128)S(1)} %pad_add_fusion.2.table_ref, f32[16,8,256]{2,1,0:T(8,128)S(1)} %pad.9.bias_ref, bf16[256,1024]{1,0:T(8,128)(2,1)S(1)} %get-tuple-element.147.refs_0_, bf16[256,1024]{1,0:T(8,128)(2,1)} %collective-permute-done.18.refs_1_, ...), custom_call_target="tpu_custom_call" | custom-call | flops 536870912 | bytes 8388608 | tf_op jit(solution)/shard_map/part/pallas_call | solution.py:200
  152.1 6.4 %collective-permute-done.34.refs_0_ = bf16[1056,256]{1,0:T(8,128)(2,1)S(1)} collective-permute-done((bf16[1056,256]{1,0:T(8,128)(2,1)S(1)}, bf16[1056,256]{1,0:T(8,128)(2,1)S(1)}, u32[]{:S(2)}, u32[]{:S(2)}) %collective-permute-start.34) | collective-permute-done | bytes 540704 | tf_op jit(solution)/shard_map/ppermute | solution.py:37
  159.5 2.5 %psum.7 = f32[256]{0:T(256)S(1)} all-reduce(f32[256]{0:T(256)S(1)} %bitcast.15), channel_id=1, replica_groups=mesh['seq'=16,'head'=2] {'head'}, use_global_device_ids=true, to_apply=%region_7.8 | all-reduce | flops 256 | bytes 2048 | tf_op jit(solution)/shard_map/psum | solution.py:429
  (117 shorter events, 42.7 us)
Async XLA Ops:
  1.5 22.2 %collective-permute-start = (bf16[272,1024]{1,0:T(8,128)(2,1)S(1)}, bf16[272,1024]{1,0:T(8,128)(2,1)}, u32[]{:S(2)}, u32[]{:S(2)}) collective-permute-start(bf16[272,1024]{1,0:T(8,128)(2,1)S(1)} %fusion.2), channel_id=1, source_target_pairs={{0,8},{2,10},{4,12},{6,14},{8,16},{10,18},{12,20},{14,22},{16,24},... | collective-permute-start | bytes 1671176 | tf_op jit(solution)/shard_map/ppermute | solution.py:37
  7.4 17.8 %collective-permute-start.1 = (bf16[272,1024]{1,0:T(8,128)(2,1)S(1)}, bf16[272,1024]{1,0:T(8,128)(2,1)}, u32[]{:S(2)}, u32[]{:S(2)}) collective-permute-start(bf16[272,1024]{1,0:T(8,128)(2,1)S(1)} %fusion.2), channel_id=1, source_target_pairs={{8,0},{10,2},{12,4},{14,6},{16,8},{18,10},{20,12},{22,14},{24,16},... | collective-permute-start | bytes 1671176 | tf_op jit(solution)/shard_map/ppermute | solution.py:37
  12.0 17.6 %collective-permute-start.18 = (bf16[256,1024]{1,0:T(8,128)(2,1)S(1)}, bf16[256,1024]{1,0:T(8,128)(2,1)}, u32[]{:S(2)}, u32[]{:S(2)}) collective-permute-start(bf16[256,1024]{1,0:T(8,128)(2,1)S(1)} %get-tuple-element.147.refs_0_), channel_id=1, source_target_pairs={{0,8},{2,10},{4,12},{6,14},{8,16},{10,18},{12,20},{14,22},{16,24},... | collective-permute-start | bytes 1572872 | tf_op jit(solution)/shard_map/ppermute | solution.py:37
  23.6 17.3 %collective-permute-start.20 = (bf16[256,1024]{1,0:T(8,128)(2,1)S(1)}, bf16[256,1024]{1,0:T(8,128)(2,1)S(1)}, u32[]{:S(2)}, u32[]{:S(2)}) collective-permute-start(bf16[256,1024]{1,0:T(8,128)(2,1)S(1)} %get-tuple-element.145.refs_7_), channel_id=1, source_target_pairs={{0,2},{2,0},{4,6},{6,4},{8,10},{10,8},{12,14},{14,12},{16,18},{18,... | collective-permute-start | bytes 1572872 | tf_op jit(solution)/shard_map/ppermute | solution.py:32
  25.2 17.3 %collective-permute-start.21 = (bf16[256,1024]{1,0:T(8,128)(2,1)S(1)}, bf16[256,1024]{1,0:T(8,128)(2,1)S(1)}, u32[]{:S(2)}, u32[]{:S(2)}) collective-permute-start(bf16[256,1024]{1,0:T(8,128)(2,1)S(1)} %get-tuple-element.143.refs_8_), channel_id=1, source_target_pairs={{0,4},{2,6},{4,0},{6,2},{8,12},{10,14},{12,8},{14,10},{16,20},{18,... | collective-permute-start | bytes 1572872 | tf_op jit(solution)/shard_map/ppermute | solution.py:32
  26.7 17.2 %collective-permute-start.4 = (bf16[272,1024]{1,0:T(8,128)(2,1)}, bf16[272,1024]{1,0:T(8,128)(2,1)}, u32[]{:S(2)}, u32[]{:S(2)}) collective-permute-start(bf16[272,1024]{1,0:T(8,128)(2,1)} %collective-permute-done.refs_1_), channel_id=1, source_target_pairs={{8,16},{10,18},{12,20},{14,22},{16,24},{18,26},{20,28},{22,30},{9,... | collective-permute-start | bytes 1671176 | tf_op jit(solution)/shard_map/ppermute | solution.py:37
  29.6 19.4 %collective-permute-start.5 = (bf16[272,1024]{1,0:T(8,128)(2,1)}, bf16[272,1024]{1,0:T(8,128)(2,1)}, u32[]{:S(2)}, u32[]{:S(2)}) collective-permute-start(bf16[272,1024]{1,0:T(8,128)(2,1)} %collective-permute-done.1.refs_4_), channel_id=1, source_target_pairs={{8,0},{10,2},{12,4},{14,6},{16,8},{18,10},{20,12},{22,14},{9,1},{1... | collective-permute-start | bytes 1671176 | tf_op jit(solution)/shard_map/ppermute | solution.py:37
  43.9 25.2 %collective-permute-start.24 = (bf16[256,1024]{1,0:T(8,128)(2,1)S(1)}, bf16[256,1024]{1,0:T(8,128)(2,1)}, u32[]{:S(2)}, u32[]{:S(2)}) collective-permute-start(bf16[256,1024]{1,0:T(8,128)(2,1)S(1)} %get-tuple-element.143.refs_8_), channel_id=1, source_target_pairs={{0,2},{2,0},{4,6},{6,4},{8,10},{10,8},{12,14},{14,12},{16,18},{18,... | collective-permute-start | bytes 1572872 | tf_op jit(solution)/shard_map/ppermute | solution.py:32
  49.1 20.6 %collective-permute-start.25 = (bf16[256,1024]{1,0:T(8,128)(2,1)S(1)}, bf16[256,1024]{1,0:T(8,128)(2,1)}, u32[]{:S(2)}, u32[]{:S(2)}) collective-permute-start(bf16[256,1024]{1,0:T(8,128)(2,1)S(1)} %get-tuple-element.145.refs_7_), channel_id=1, source_target_pairs={{0,4},{2,6},{4,0},{6,2},{8,12},{10,14},{12,8},{14,10},{16,20},{18,... | collective-permute-start | bytes 1572872 | tf_op jit(solution)/shard_map/ppermute | solution.py:32
  50.6 17.1 %collective-permute-start.23 = (bf16[256,1024]{1,0:T(8,128)(2,1)}, bf16[256,1024]{1,0:T(8,128)(2,1)}, u32[]{:S(2)}, u32[]{:S(2)}) collective-permute-start(bf16[256,1024]{1,0:T(8,128)(2,1)} %copy-done), channel_id=1, source_target_pairs={{8,0},{10,2},{12,4},{14,6},{16,8},{18,10},{20,12},{22,14},{9,1},{1... | collective-permute-start | bytes 1572872 | tf_op jit(solution)/shard_map/ppermute | solution.py:37
  57.2 18.8 %collective-permute-start.9 = (bf16[272,1024]{1,0:T(8,128)(2,1)}, bf16[272,1024]{1,0:T(8,128)(2,1)}, u32[]{:S(2)}, u32[]{:S(2)}) collective-permute-start(bf16[272,1024]{1,0:T(8,128)(2,1)} %collective-permute-done.5.refs_5_), channel_id=1, source_target_pairs={{8,0},{10,2},{12,4},{14,6},{9,1},{11,3},{13,5},{15,7}} | collective-permute-start | bytes 1671176 | tf_op jit(solution)/shard_map/ppermute | solution.py:37
  69.7 24.4 %collective-permute-start.28 = (bf16[256,1024]{1,0:T(8,128)(2,1)}, bf16[256,1024]{1,0:T(8,128)(2,1)}, u32[]{:S(2)}, u32[]{:S(2)}) collective-permute-start(bf16[256,1024]{1,0:T(8,128)(2,1)} %copy-done.2), channel_id=1, source_target_pairs={{0,4},{2,6},{4,0},{6,2},{8,12},{10,14},{12,8},{14,10},{16,20},{18,... | collective-permute-start | bytes 1572872 | tf_op jit(solution)/shard_map/ppermute | solution.py:32
  71.2 22.9 %collective-permute-start.29 = (bf16[256,1024]{1,0:T(8,128)(2,1)}, bf16[256,1024]{1,0:T(8,128)(2,1)}, u32[]{:S(2)}, u32[]{:S(2)}) collective-permute-start(bf16[256,1024]{1,0:T(8,128)(2,1)} %copy-done.4), channel_id=1, source_target_pairs={{0,2},{2,0},{4,6},{6,4},{8,10},{10,8},{12,14},{14,12},{16,18},{18,... | collective-permute-start | bytes 1572872 | tf_op jit(solution)/shard_map/ppermute | solution.py:32
  76.0 17.3 %collective-permute-start.26 = (bf16[256,1024]{1,0:T(8,128)(2,1)}, bf16[256,1024]{1,0:T(8,128)(2,1)}, u32[]{:S(2)}, u32[]{:S(2)}) collective-permute-start(bf16[256,1024]{1,0:T(8,128)(2,1)} %collective-permute-done.22.refs_2_), channel_id=1, source_target_pairs={{16,24},{18,26},{20,28},{22,30},{17,25},{19,27},{21,29},{23,31}} | collective-permute-start | bytes 1572872 | tf_op jit(solution)/shard_map/ppermute | solution.py:37
  85.6 24.1 %collective-permute-start.12 = (bf16[1056,256]{1,0:T(8,128)(2,1)S(1)}, bf16[1056,256]{1,0:T(8,128)(2,1)S(1)}, u32[]{:S(2)}, u32[]{:S(2)}) collective-permute-start(bf16[1056,256]{1,0:T(8,128)(2,1)S(1)} %part.7.other_ref), channel_id=1, source_target_pairs={{0,8},{2,10},{4,12},{6,14},{1,9},{3,11},{5,13},{7,15}} | collective-permute-start | bytes 1622024 | tf_op jit(solution)/shard_map/ppermute | solution.py:37
  97.6 21.6 %collective-permute-start.30 = (bf16[1056,256]{1,0:T(8,128)(2,1)S(1)}, bf16[1056,256]{1,0:T(8,128)(2,1)S(1)}, u32[]{:S(2)}, u32[]{:S(2)}) collective-permute-start(bf16[1056,256]{1,0:T(8,128)(2,1)S(1)} %part.11.other_ref), channel_id=1, source_target_pairs={{0,8},{2,10},{4,12},{6,14},{1,9},{3,11},{5,13},{7,15}} | collective-permute-start | bytes 1622024 | tf_op jit(solution)/shard_map/ppermute | solution.py:37
  101.3 17.9 %collective-permute-start.31 = (bf16[1056,256]{1,0:T(8,128)(2,1)S(1)}, bf16[1056,256]{1,0:T(8,128)(2,1)S(1)}, u32[]{:S(2)}, u32[]{:S(2)}) collective-permute-start(bf16[1056,256]{1,0:T(8,128)(2,1)S(1)} %part.11.other_ref), channel_id=1, source_target_pairs={{24,16},{26,18},{28,20},{30,22},{25,17},{27,19},{29,21},{31,23}} | collective-permute-start | bytes 1622024 | tf_op jit(solution)/shard_map/ppermute | solution.py:37
  110.1 18.8 %collective-permute-start.14 = (bf16[1056,256]{1,0:T(8,128)(2,1)S(1)}, bf16[1056,256]{1,0:T(8,128)(2,1)S(1)}, u32[]{:S(2)}, u32[]{:S(2)}) collective-permute-start(bf16[1056,256]{1,0:T(8,128)(2,1)S(1)} %get-tuple-element.91), channel_id=1, source_target_pairs={{0,8},{2,10},{4,12},{6,14},{8,16},{10,18},{12,20},{14,22},{1,9},{3... | collective-permute-start | bytes 1622024 | tf_op jit(solution)/shard_map/ppermute | solution.py:37
  111.4 17.5 %collective-permute-start.15 = (bf16[1056,256]{1,0:T(8,128)(2,1)S(1)}, bf16[1056,256]{1,0:T(8,128)(2,1)S(1)}, u32[]{:S(2)}, u32[]{:S(2)}) collective-permute-start(bf16[1056,256]{1,0:T(8,128)(2,1)S(1)} %get-tuple-element.92), channel_id=1, source_target_pairs={{16,8},{18,10},{20,12},{22,14},{24,16},{26,18},{28,20},{30,22},{17... | collective-permute-start | bytes 1622024 | tf_op jit(solution)/shard_map/ppermute | solution.py:37
  119.7 19.3 %collective-permute-start.32 = (bf16[1056,256]{1,0:T(8,128)(2,1)S(1)}, bf16[1056,256]{1,0:T(8,128)(2,1)S(1)}, u32[]{:S(2)}, u32[]{:S(2)}) collective-permute-start(bf16[1056,256]{1,0:T(8,128)(2,1)S(1)} %get-tuple-element.126), channel_id=1, source_target_pairs={{0,8},{2,10},{4,12},{6,14},{8,16},{10,18},{12,20},{14,22},{1,9},{3... | collective-permute-start | bytes 1622024 | tf_op jit(solution)/shard_map/ppermute | solution.py:37
  121.0 18.0 %collective-permute-start.33 = (bf16[1056,256]{1,0:T(8,128)(2,1)S(1)}, bf16[1056,256]{1,0:T(8,128)(2,1)S(1)}, u32[]{:S(2)}, u32[]{:S(2)}) collective-permute-start(bf16[1056,256]{1,0:T(8,128)(2,1)S(1)} %get-tuple-element.127), channel_id=1, source_target_pairs={{16,8},{18,10},{20,12},{22,14},{24,16},{26,18},{28,20},{30,22},{17... | collective-permute-start | bytes 1622024 | tf_op jit(solution)/shard_map/ppermute | solution.py:37
  129.4 22.7 %collective-permute-start.16 = (bf16[1056,256]{1,0:T(8,128)(2,1)S(1)}, bf16[1056,256]{1,0:T(8,128)(2,1)S(1)}, u32[]{:S(2)}, u32[]{:S(2)}) collective-permute-start(bf16[1056,256]{1,0:T(8,128)(2,1)S(1)} %get-tuple-element.101), channel_id=1, source_target_pairs={{0,8},{2,10},{4,12},{6,14},{8,16},{10,18},{12,20},{14,22},{16,24},... | collective-permute-start | bytes 1622024 | tf_op jit(solution)/shard_map/ppermute | solution.py:37
  133.4 18.7 %collective-permute-start.17 = (bf16[1056,256]{1,0:T(8,128)(2,1)S(1)}, bf16[1056,256]{1,0:T(8,128)(2,1)S(1)}, u32[]{:S(2)}, u32[]{:S(2)}) collective-permute-start(bf16[1056,256]{1,0:T(8,128)(2,1)S(1)} %get-tuple-element.102), channel_id=1, source_target_pairs={{8,0},{10,2},{12,4},{14,6},{16,8},{18,10},{20,12},{22,14},{24,16},... | collective-permute-start | bytes 1622024 | tf_op jit(solution)/shard_map/ppermute | solution.py:37
  139.6 18.9 %collective-permute-start.34 = (bf16[1056,256]{1,0:T(8,128)(2,1)S(1)}, bf16[1056,256]{1,0:T(8,128)(2,1)S(1)}, u32[]{:S(2)}, u32[]{:S(2)}) collective-permute-start(bf16[1056,256]{1,0:T(8,128)(2,1)S(1)} %get-tuple-element.130), channel_id=1, source_target_pairs={{0,8},{2,10},{4,12},{6,14},{8,16},{10,18},{12,20},{14,22},{16,24},... | collective-permute-start | bytes 1622024 | tf_op jit(solution)/shard_map/ppermute | solution.py:37
  (24 other events, 292.6 us)

commit v5 on v4

--- a/solution.py
+++ b/solution.py
@@ -363,8 +363,9 @@
                     key, value, *_ = tie((key, value, near[c - 1][1], far[c - 1][0]))
                 elif c and TIES[3]:
                     key, value, *_ = tie((key, value, near[c - 1][0], far[c - 1][1]))
-                near[c] = [exchange(key, shards, 1), exchange(value, shards, 1)]
-                far[c] = [exchange(key, shards, 2), exchange(value, shards, 2)]
+                near_key, far_value = exchange(key, shards, 1), exchange(value, shards, 2)
+                far_key, near_value = exchange(key, shards, 2), exchange(value, shards, 1)
+                near[c], far[c] = [near_key, near_value], [far_key, far_value]
             up, down = tie((up, down))
             if hop == 2:
                 diagonal[c] = [exchange(near[c][0], shards, 2), exchange(far[c][1], shards, 1)]

time: 164 us -> 164 us (level)
  no operation moved by 1% of the time
where the time goes in v5:
time: 164 us; the launch traced here: 163 us
  starting transfers between devices  68 us (41%)
  waiting for transfers between devices  47.7 us (29%)
  Pallas kernels  39.1 us (24%)
  other arithmetic  3.17 us (2%)
  blocking collectives  2.47 us (2%)
  local copies, waits for them, and re-layouts  2.16 us (1%)
    ppermute x24, starting transfers between devices, along(): return lax.ppermute(array, 'seq', pairs)  52.5 us
    ppermute x24, waiting for transfers between devices, along(): return lax.ppermute(array, 'seq', pairs)  38.3 us
    pallas_call x6, Pallas kernels, attention(): pl.pallas_call(partial(attend, planes, orders, heads, group, chained, sta...  36.1 us
    ppermute x12, starting transfers between devices, exchange(): return lax.ppermute(array, 'seq', [(i, i ^ flip) for i in range(shards)])  15.5 us
    ppermute x12, waiting for transfers between devices, exchange(): return lax.ppermute(array, 'seq', [(i, i ^ flip) for i in range(shards)])  9.47 us
  transfers between devices with their start and end apart: 36, of which 10 were waited for; matrix products, arithmetic and copies ran while one was open for 2% of the time, Pallas kernels for 23%

profile of v5, /device:TPU:0, one launch (start us, length us, event | category | flops | bytes accessed | tf_op | source)
XLA Modules:
  0.0 163.1 jit_solution(12310511750171509838)
XLA Ops:
  1.5 5.9 %collective-permute-start = (bf16[272,1024]{1,0:T(8,128)(2,1)S(1)}, bf16[272,1024]{1,0:T(8,128)(2,1)}, u32[]{:S(2)}, u32[]{:S(2)}) collective-permute-start(bf16[272,1024]{1,0:T(8,128)(2,1)S(1)} %fusion.2), channel_id=1, source_target_pairs={{0,8},{2,10},{4,12},{6,14},{8,16},{10,18},{12,20},{14,22},{16,24},... | collective-permute-start | bytes 1671176 | tf_op jit(solution)/shard_map/ppermute | solution.py:37
  8.8 1.6 collective-permute-start.2
  10.4 1.6 collective-permute-start.3
  12.0 5.3 %collective-permute-start.18 = (bf16[256,1024]{1,0:T(8,128)(2,1)S(1)}, bf16[256,1024]{1,0:T(8,128)(2,1)}, u32[]{:S(2)}, u32[]{:S(2)}) collective-permute-start(bf16[256,1024]{1,0:T(8,128)(2,1)S(1)} %get-tuple-element.147.refs_0_), channel_id=1, source_target_pairs={{0,8},{2,10},{4,12},{6,14},{8,16},{10,18},{12,20},{14,22},{16,24},... | collective-permute-start | bytes 1572872 | tf_op jit(solution)/shard_map/ppermute | solution.py:37
  17.4 5.0 %collective-permute-done.2.refs_9_ = bf16[256,1024]{1,0:T(8,128)(2,1)} collective-permute-done((bf16[256,1024]{1,0:T(8,128)(2,1)S(1)}, bf16[256,1024]{1,0:T(8,128)(2,1)}, u32[]{:S(2)}, u32[]{:S(2)}) %collective-permute-start.2) | collective-permute-done | bytes 524320 | tf_op jit(solution)/shard_map/ppermute | solution.py:32
  30.9 8.4 %collective-permute-done.19.refs_4_ = bf16[256,1024]{1,0:T(8,128)(2,1)S(1)} collective-permute-done((bf16[256,1024]{1,0:T(8,128)(2,1)S(1)}, bf16[256,1024]{1,0:T(8,128)(2,1)S(1)}, u32[]{:S(2)}, u32[]{:S(2)}) %collective-permute-start.19) | collective-permute-done | bytes 524320 | tf_op jit(solution)/shard_map/ppermute | solution.py:37
  39.4 1.6 collective-permute-start.6
  44.5 4.5 %collective-permute-done.5.refs_5_ = bf16[272,1024]{1,0:T(8,128)(2,1)} collective-permute-done((bf16[272,1024]{1,0:T(8,128)(2,1)}, bf16[272,1024]{1,0:T(8,128)(2,1)}, u32[]{:S(2)}, u32[]{:S(2)}) %collective-permute-start.5) | collective-permute-done | bytes 557088 | tf_op jit(solution)/shard_map/ppermute | solution.py:37
  51.9 3.9 %collective-permute-done.7.refs_14_ = bf16[256,1024]{1,0:T(8,128)(2,1)} collective-permute-done((bf16[256,1024]{1,0:T(8,128)(2,1)}, bf16[256,1024]{1,0:T(8,128)(2,1)}, u32[]{:S(2)}, u32[]{:S(2)}) %collective-permute-start.7) | collective-permute-done | bytes 524320 | tf_op jit(solution)/shard_map/ppermute | solution.py:32
  58.8 8.9 %collective-permute-done.23.refs_5_ = bf16[256,1024]{1,0:T(8,128)(2,1)} collective-permute-done((bf16[256,1024]{1,0:T(8,128)(2,1)}, bf16[256,1024]{1,0:T(8,128)(2,1)}, u32[]{:S(2)}, u32[]{:S(2)}) %collective-permute-start.23) | collective-permute-done | bytes 524320 | tf_op jit(solution)/shard_map/ppermute | solution.py:37
  71.7 4.3 %collective-permute-done.9.refs_6_ = bf16[272,1024]{1,0:T(8,128)(2,1)} collective-permute-done((bf16[272,1024]{1,0:T(8,128)(2,1)}, bf16[272,1024]{1,0:T(8,128)(2,1)}, u32[]{:S(2)}, u32[]{:S(2)}) %collective-permute-start.9) | collective-permute-done | bytes 557088 | tf_op jit(solution)/shard_map/ppermute | solution.py:37
  81.8 3.8 %part.7.other_ref = bf16[1056,256]{1,0:T(8,128)(2,1)S(1)} custom-call(s32[69]{0:T(128)S(1)} %pad_add_fusion.2.table_ref, f32[16,8,256]{2,1,0:T(8,128)S(1)} %pad.9.bias_ref, bf16[256,1024]{1,0:T(8,128)(2,1)S(1)} %get-tuple-element.148.refs_0_, bf16[272,1024]{1,0:T(8,128)(2,1)} %collective-permute-done.refs_1_, ...), custom_call_target="tpu_custom_call" | custom-call | flops 536870912 | bytes 8388608 | tf_op jit(solution)/shard_map/part/pallas_call | solution.py:200
  85.6 7.8 %collective-permute-start.12 = (bf16[1056,256]{1,0:T(8,128)(2,1)S(1)}, bf16[1056,256]{1,0:T(8,128)(2,1)S(1)}, u32[]{:S(2)}, u32[]{:S(2)}) collective-permute-start(bf16[1056,256]{1,0:T(8,128)(2,1)S(1)} %part.7.other_ref), channel_id=1, source_target_pairs={{0,8},{2,10},{4,12},{6,14},{1,9},{3,11},{5,13},{7,15}} | collective-permute-start | bytes 1622024 | tf_op jit(solution)/shard_map/ppermute | solution.py:37
  94.1 3.5 %part.11.other_ref = bf16[1056,256]{1,0:T(8,128)(2,1)S(1)} custom-call(s32[69]{0:T(128)S(1)} %pad_add_fusion.2.table_ref, f32[16,8,256]{2,1,0:T(8,128)S(1)} %pad.9.bias_ref, bf16[256,1024]{1,0:T(8,128)(2,1)S(1)} %get-tuple-element.147.refs_0_, bf16[256,1024]{1,0:T(8,128)(2,1)} %collective-permute-done.18.refs_1_, ...), custom_call_target="tpu_custom_call" | custom-call | flops 536870912 | bytes 8388608 | tf_op jit(solution)/shard_map/part/pallas_call | solution.py:200
  97.6 3.6 %collective-permute-start.30 = (bf16[1056,256]{1,0:T(8,128)(2,1)S(1)}, bf16[1056,256]{1,0:T(8,128)(2,1)S(1)}, u32[]{:S(2)}, u32[]{:S(2)}) collective-permute-start(bf16[1056,256]{1,0:T(8,128)(2,1)S(1)} %part.11.other_ref), channel_id=1, source_target_pairs={{0,8},{2,10},{4,12},{6,14},{1,9},{3,11},{5,13},{7,15}} | collective-permute-start | bytes 1622024 | tf_op jit(solution)/shard_map/ppermute | solution.py:37
  102.0 7.6 %part.6 = (bf16[1056,256]{1,0:T(8,128)(2,1)S(1)}, bf16[1056,256]{1,0:T(8,128)(2,1)S(1)}) custom-call(s32[69]{0:T(128)S(1)} %pad_add_fusion.2.table_ref, f32[16,8,256]{2,1,0:T(8,128)S(1)} %pad.9.bias_ref, bf16[256,1024]{1,0:T(8,128)(2,1)S(1)} %get-tuple-element.148.refs_0_, bf16[272,1024]{1,0:T(8,128)(2,1)} %collective-permute-done.refs_1_, ...), custom_call_target="tpu_custom_call" | custom-call | flops 1073741824 | bytes 8388608 | tf_op jit(solution)/shard_map/part/pallas_call | solution.py:200
  112.1 7.0 %part.10 = (bf16[1056,256]{1,0:T(8,128)(2,1)S(1)}, bf16[1056,256]{1,0:T(8,128)(2,1)S(1)}) custom-call(s32[69]{0:T(128)S(1)} %pad_add_fusion.2.table_ref, f32[16,8,256]{2,1,0:T(8,128)S(1)} %pad.9.bias_ref, bf16[256,1024]{1,0:T(8,128)(2,1)S(1)} %get-tuple-element.147.refs_0_, bf16[256,1024]{1,0:T(8,128)(2,1)} %collective-permute-done.18.refs_1_, ...), custom_call_target="tpu_custom_call" | custom-call | flops 1073741824 | bytes 8388608 | tf_op jit(solution)/shard_map/part/pallas_call | solution.py:200
  121.7 7.2 %part.8 = (f32[1024,256]{1,0:T(8,128)S(1)}, f32[8,256]{1,0:T(8,128)S(1)}) custom-call(s32[69]{0:T(128)S(1)} %pad_add_fusion.2.table_ref, f32[16,8,256]{2,1,0:T(8,128)S(1)} %pad.9.bias_ref, bf16[256,1024]{1,0:T(8,128)(2,1)S(1)} %get-tuple-element.148.refs_0_, bf16[272,1024]{1,0:T(8,128)(2,1)} %collective-permute-done.refs_1_, ...), custom_call_target="tpu_custom_call" | custom-call | flops 536870912 | bytes 8388608 | tf_op jit(solution)/shard_map/part/pallas_call | solution.py:200
  129.4 4.0 %collective-permute-start.16 = (bf16[1056,256]{1,0:T(8,128)(2,1)S(1)}, bf16[1056,256]{1,0:T(8,128)(2,1)S(1)}, u32[]{:S(2)}, u32[]{:S(2)}) collective-permute-start(bf16[1056,256]{1,0:T(8,128)(2,1)S(1)} %get-tuple-element.101), channel_id=1, source_target_pairs={{0,8},{2,10},{4,12},{6,14},{8,16},{10,18},{12,20},{14,22},{16,24},... | collective-permute-start | bytes 1622024 | tf_op jit(solution)/shard_map/ppermute | solution.py:37
  134.7 4.3 %collective-permute-done.32.up_ref = bf16[1056,256]{1,0:T(8,128)(2,1)S(1)} collective-permute-done((bf16[1056,256]{1,0:T(8,128)(2,1)S(1)}, bf16[1056,256]{1,0:T(8,128)(2,1)S(1)}, u32[]{:S(2)}, u32[]{:S(2)}) %collective-permute-start.32) | collective-permute-done | bytes 540704 | tf_op jit(solution)/shard_map/ppermute | solution.py:37
  139.6 4.2 %collective-permute-start.34 = (bf16[1056,256]{1,0:T(8,128)(2,1)S(1)}, bf16[1056,256]{1,0:T(8,128)(2,1)S(1)}, u32[]{:S(2)}, u32[]{:S(2)}) collective-permute-start(bf16[1056,256]{1,0:T(8,128)(2,1)S(1)} %get-tuple-element.130), channel_id=1, source_target_pairs={{0,8},{2,10},{4,12},{6,14},{8,16},{10,18},{12,20},{14,22},{16,24},... | collective-permute-start | bytes 1622024 | tf_op jit(solution)/shard_map/ppermute | solution.py:37
  145.2 6.9 %part.9 = (f32[1024,256]{1,0:T(8,128)S(1)}, f32[8,256]{1,0:T(8,128)S(1)}) custom-call(s32[69]{0:T(128)S(1)} %pad_add_fusion.2.table_ref, f32[16,8,256]{2,1,0:T(8,128)S(1)} %pad.9.bias_ref, bf16[256,1024]{1,0:T(8,128)(2,1)S(1)} %get-tuple-element.147.refs_0_, bf16[256,1024]{1,0:T(8,128)(2,1)} %collective-permute-done.18.refs_1_, ...), custom_call_target="tpu_custom_call" | custom-call | flops 536870912 | bytes 8388608 | tf_op jit(solution)/shard_map/part/pallas_call | solution.py:200
  152.1 6.4 %collective-permute-done.34.refs_0_ = bf16[1056,256]{1,0:T(8,128)(2,1)S(1)} collective-permute-done((bf16[1056,256]{1,0:T(8,128)(2,1)S(1)}, bf16[1056,256]{1,0:T(8,128)(2,1)S(1)}, u32[]{:S(2)}, u32[]{:S(2)}) %collective-permute-start.34) | collective-permute-done | bytes 540704 | tf_op jit(solution)/shard_map/ppermute | solution.py:37
  159.5 2.5 %psum.7 = f32[256]{0:T(256)S(1)} all-reduce(f32[256]{0:T(256)S(1)} %bitcast.15), channel_id=1, replica_groups=mesh['seq'=16,'head'=2] {'head'}, use_global_device_ids=true, to_apply=%region_7.8 | all-reduce | flops 256 | bytes 2048 | tf_op jit(solution)/shard_map/psum | solution.py:430
  (117 shorter events, 42.7 us)
Async XLA Ops:
  1.5 22.2 %collective-permute-start = (bf16[272,1024]{1,0:T(8,128)(2,1)S(1)}, bf16[272,1024]{1,0:T(8,128)(2,1)}, u32[]{:S(2)}, u32[]{:S(2)}) collective-permute-start(bf16[272,1024]{1,0:T(8,128)(2,1)S(1)} %fusion.2), channel_id=1, source_target_pairs={{0,8},{2,10},{4,12},{6,14},{8,16},{10,18},{12,20},{14,22},{16,24},... | collective-permute-start | bytes 1671176 | tf_op jit(solution)/shard_map/ppermute | solution.py:37
  7.4 17.8 %collective-permute-start.1 = (bf16[272,1024]{1,0:T(8,128)(2,1)S(1)}, bf16[272,1024]{1,0:T(8,128)(2,1)}, u32[]{:S(2)}, u32[]{:S(2)}) collective-permute-start(bf16[272,1024]{1,0:T(8,128)(2,1)S(1)} %fusion.2), channel_id=1, source_target_pairs={{8,0},{10,2},{12,4},{14,6},{16,8},{18,10},{20,12},{22,14},{24,16},... | collective-permute-start | bytes 1671176 | tf_op jit(solution)/shard_map/ppermute | solution.py:37
  12.0 17.6 %collective-permute-start.18 = (bf16[256,1024]{1,0:T(8,128)(2,1)S(1)}, bf16[256,1024]{1,0:T(8,128)(2,1)}, u32[]{:S(2)}, u32[]{:S(2)}) collective-permute-start(bf16[256,1024]{1,0:T(8,128)(2,1)S(1)} %get-tuple-element.147.refs_0_), channel_id=1, source_target_pairs={{0,8},{2,10},{4,12},{6,14},{8,16},{10,18},{12,20},{14,22},{16,24},... | collective-permute-start | bytes 1572872 | tf_op jit(solution)/shard_map/ppermute | solution.py:37
  23.6 17.3 %collective-permute-start.20 = (bf16[256,1024]{1,0:T(8,128)(2,1)S(1)}, bf16[256,1024]{1,0:T(8,128)(2,1)S(1)}, u32[]{:S(2)}, u32[]{:S(2)}) collective-permute-start(bf16[256,1024]{1,0:T(8,128)(2,1)S(1)} %get-tuple-element.145.refs_7_), channel_id=1, source_target_pairs={{0,2},{2,0},{4,6},{6,4},{8,10},{10,8},{12,14},{14,12},{16,18},{18,... | collective-permute-start | bytes 1572872 | tf_op jit(solution)/shard_map/ppermute | solution.py:32
  25.2 17.3 %collective-permute-start.21 = (bf16[256,1024]{1,0:T(8,128)(2,1)S(1)}, bf16[256,1024]{1,0:T(8,128)(2,1)S(1)}, u32[]{:S(2)}, u32[]{:S(2)}) collective-permute-start(bf16[256,1024]{1,0:T(8,128)(2,1)S(1)} %get-tuple-element.143.refs_8_), channel_id=1, source_target_pairs={{0,4},{2,6},{4,0},{6,2},{8,12},{10,14},{12,8},{14,10},{16,20},{18,... | collective-permute-start | bytes 1572872 | tf_op jit(solution)/shard_map/ppermute | solution.py:32
  26.7 17.2 %collective-permute-start.4 = (bf16[272,1024]{1,0:T(8,128)(2,1)}, bf16[272,1024]{1,0:T(8,128)(2,1)}, u32[]{:S(2)}, u32[]{:S(2)}) collective-permute-start(bf16[272,1024]{1,0:T(8,128)(2,1)} %collective-permute-done.refs_1_), channel_id=1, source_target_pairs={{8,16},{10,18},{12,20},{14,22},{16,24},{18,26},{20,28},{22,30},{9,... | collective-permute-start | bytes 1671176 | tf_op jit(solution)/shard_map/ppermute | solution.py:37
  29.6 19.4 %collective-permute-start.5 = (bf16[272,1024]{1,0:T(8,128)(2,1)}, bf16[272,1024]{1,0:T(8,128)(2,1)}, u32[]{:S(2)}, u32[]{:S(2)}) collective-permute-start(bf16[272,1024]{1,0:T(8,128)(2,1)} %collective-permute-done.1.refs_4_), channel_id=1, source_target_pairs={{8,0},{10,2},{12,4},{14,6},{16,8},{18,10},{20,12},{22,14},{9,1},{1... | collective-permute-start | bytes 1671176 | tf_op jit(solution)/shard_map/ppermute | solution.py:37
  43.9 25.2 %collective-permute-start.24 = (bf16[256,1024]{1,0:T(8,128)(2,1)S(1)}, bf16[256,1024]{1,0:T(8,128)(2,1)}, u32[]{:S(2)}, u32[]{:S(2)}) collective-permute-start(bf16[256,1024]{1,0:T(8,128)(2,1)S(1)} %get-tuple-element.143.refs_8_), channel_id=1, source_target_pairs={{0,2},{2,0},{4,6},{6,4},{8,10},{10,8},{12,14},{14,12},{16,18},{18,... | collective-permute-start | bytes 1572872 | tf_op jit(solution)/shard_map/ppermute | solution.py:32
  49.1 20.6 %collective-permute-start.25 = (bf16[256,1024]{1,0:T(8,128)(2,1)S(1)}, bf16[256,1024]{1,0:T(8,128)(2,1)}, u32[]{:S(2)}, u32[]{:S(2)}) collective-permute-start(bf16[256,1024]{1,0:T(8,128)(2,1)S(1)} %get-tuple-element.145.refs_7_), channel_id=1, source_target_pairs={{0,4},{2,6},{4,0},{6,2},{8,12},{10,14},{12,8},{14,10},{16,20},{18,... | collective-permute-start | bytes 1572872 | tf_op jit(solution)/shard_map/ppermute | solution.py:32
  50.6 17.1 %collective-permute-start.23 = (bf16[256,1024]{1,0:T(8,128)(2,1)}, bf16[256,1024]{1,0:T(8,128)(2,1)}, u32[]{:S(2)}, u32[]{:S(2)}) collective-permute-start(bf16[256,1024]{1,0:T(8,128)(2,1)} %copy-done), channel_id=1, source_target_pairs={{8,0},{10,2},{12,4},{14,6},{16,8},{18,10},{20,12},{22,14},{9,1},{1... | collective-permute-start | bytes 1572872 | tf_op jit(solution)/shard_map/ppermute | solution.py:37
  57.2 18.8 %collective-permute-start.9 = (bf16[272,1024]{1,0:T(8,128)(2,1)}, bf16[272,1024]{1,0:T(8,128)(2,1)}, u32[]{:S(2)}, u32[]{:S(2)}) collective-permute-start(bf16[272,1024]{1,0:T(8,128)(2,1)} %collective-permute-done.5.refs_5_), channel_id=1, source_target_pairs={{8,0},{10,2},{12,4},{14,6},{9,1},{11,3},{13,5},{15,7}} | collective-permute-start | bytes 1671176 | tf_op jit(solution)/shard_map/ppermute | solution.py:37
  69.7 24.4 %collective-permute-start.28 = (bf16[256,1024]{1,0:T(8,128)(2,1)}, bf16[256,1024]{1,0:T(8,128)(2,1)}, u32[]{:S(2)}, u32[]{:S(2)}) collective-permute-start(bf16[256,1024]{1,0:T(8,128)(2,1)} %copy-done.2), channel_id=1, source_target_pairs={{0,4},{2,6},{4,0},{6,2},{8,12},{10,14},{12,8},{14,10},{16,20},{18,... | collective-permute-start | bytes 1572872 | tf_op jit(solution)/shard_map/ppermute | solution.py:32
  71.2 22.9 %collective-permute-start.29 = (bf16[256,1024]{1,0:T(8,128)(2,1)}, bf16[256,1024]{1,0:T(8,128)(2,1)}, u32[]{:S(2)}, u32[]{:S(2)}) collective-permute-start(bf16[256,1024]{1,0:T(8,128)(2,1)} %copy-done.4), channel_id=1, source_target_pairs={{0,2},{2,0},{4,6},{6,4},{8,10},{10,8},{12,14},{14,12},{16,18},{18,... | collective-permute-start | bytes 1572872 | tf_op jit(solution)/shard_map/ppermute | solution.py:32
  76.0 17.3 %collective-permute-start.26 = (bf16[256,1024]{1,0:T(8,128)(2,1)}, bf16[256,1024]{1,0:T(8,128)(2,1)}, u32[]{:S(2)}, u32[]{:S(2)}) collective-permute-start(bf16[256,1024]{1,0:T(8,128)(2,1)} %collective-permute-done.22.refs_2_), channel_id=1, source_target_pairs={{16,24},{18,26},{20,28},{22,30},{17,25},{19,27},{21,29},{23,31}} | collective-permute-start | bytes 1572872 | tf_op jit(solution)/shard_map/ppermute | solution.py:37
  85.6 24.1 %collective-permute-start.12 = (bf16[1056,256]{1,0:T(8,128)(2,1)S(1)}, bf16[1056,256]{1,0:T(8,128)(2,1)S(1)}, u32[]{:S(2)}, u32[]{:S(2)}) collective-permute-start(bf16[1056,256]{1,0:T(8,128)(2,1)S(1)} %part.7.other_ref), channel_id=1, source_target_pairs={{0,8},{2,10},{4,12},{6,14},{1,9},{3,11},{5,13},{7,15}} | collective-permute-start | bytes 1622024 | tf_op jit(solution)/shard_map/ppermute | solution.py:37
  97.6 21.6 %collective-permute-start.30 = (bf16[1056,256]{1,0:T(8,128)(2,1)S(1)}, bf16[1056,256]{1,0:T(8,128)(2,1)S(1)}, u32[]{:S(2)}, u32[]{:S(2)}) collective-permute-start(bf16[1056,256]{1,0:T(8,128)(2,1)S(1)} %part.11.other_ref), channel_id=1, source_target_pairs={{0,8},{2,10},{4,12},{6,14},{1,9},{3,11},{5,13},{7,15}} | collective-permute-start | bytes 1622024 | tf_op jit(solution)/shard_map/ppermute | solution.py:37
  101.3 17.9 %collective-permute-start.31 = (bf16[1056,256]{1,0:T(8,128)(2,1)S(1)}, bf16[1056,256]{1,0:T(8,128)(2,1)S(1)}, u32[]{:S(2)}, u32[]{:S(2)}) collective-permute-start(bf16[1056,256]{1,0:T(8,128)(2,1)S(1)} %part.11.other_ref), channel_id=1, source_target_pairs={{24,16},{26,18},{28,20},{30,22},{25,17},{27,19},{29,21},{31,23}} | collective-permute-start | bytes 1622024 | tf_op jit(solution)/shard_map/ppermute | solution.py:37
  110.1 18.8 %collective-permute-start.14 = (bf16[1056,256]{1,0:T(8,128)(2,1)S(1)}, bf16[1056,256]{1,0:T(8,128)(2,1)S(1)}, u32[]{:S(2)}, u32[]{:S(2)}) collective-permute-start(bf16[1056,256]{1,0:T(8,128)(2,1)S(1)} %get-tuple-element.91), channel_id=1, source_target_pairs={{0,8},{2,10},{4,12},{6,14},{8,16},{10,18},{12,20},{14,22},{1,9},{3... | collective-permute-start | bytes 1622024 | tf_op jit(solution)/shard_map/ppermute | solution.py:37
  111.4 17.5 %collective-permute-start.15 = (bf16[1056,256]{1,0:T(8,128)(2,1)S(1)}, bf16[1056,256]{1,0:T(8,128)(2,1)S(1)}, u32[]{:S(2)}, u32[]{:S(2)}) collective-permute-start(bf16[1056,256]{1,0:T(8,128)(2,1)S(1)} %get-tuple-element.92), channel_id=1, source_target_pairs={{16,8},{18,10},{20,12},{22,14},{24,16},{26,18},{28,20},{30,22},{17... | collective-permute-start | bytes 1622024 | tf_op jit(solution)/shard_map/ppermute | solution.py:37
  119.7 19.3 %collective-permute-start.32 = (bf16[1056,256]{1,0:T(8,128)(2,1)S(1)}, bf16[1056,256]{1,0:T(8,128)(2,1)S(1)}, u32[]{:S(2)}, u32[]{:S(2)}) collective-permute-start(bf16[1056,256]{1,0:T(8,128)(2,1)S(1)} %get-tuple-element.126), channel_id=1, source_target_pairs={{0,8},{2,10},{4,12},{6,14},{8,16},{10,18},{12,20},{14,22},{1,9},{3... | collective-permute-start | bytes 1622024 | tf_op jit(solution)/shard_map/ppermute | solution.py:37
  121.0 18.0 %collective-permute-start.33 = (bf16[1056,256]{1,0:T(8,128)(2,1)S(1)}, bf16[1056,256]{1,0:T(8,128)(2,1)S(1)}, u32[]{:S(2)}, u32[]{:S(2)}) collective-permute-start(bf16[1056,256]{1,0:T(8,128)(2,1)S(1)} %get-tuple-element.127), channel_id=1, source_target_pairs={{16,8},{18,10},{20,12},{22,14},{24,16},{26,18},{28,20},{30,22},{17... | collective-permute-start | bytes 1622024 | tf_op jit(solution)/shard_map/ppermute | solution.py:37
  129.4 22.7 %collective-permute-start.16 = (bf16[1056,256]{1,0:T(8,128)(2,1)S(1)}, bf16[1056,256]{1,0:T(8,128)(2,1)S(1)}, u32[]{:S(2)}, u32[]{:S(2)}) collective-permute-start(bf16[1056,256]{1,0:T(8,128)(2,1)S(1)} %get-tuple-element.101), channel_id=1, source_target_pairs={{0,8},{2,10},{4,12},{6,14},{8,16},{10,18},{12,20},{14,22},{16,24},... | collective-permute-start | bytes 1622024 | tf_op jit(solution)/shard_map/ppermute | solution.py:37
  133.4 18.7 %collective-permute-start.17 = (bf16[1056,256]{1,0:T(8,128)(2,1)S(1)}, bf16[1056,256]{1,0:T(8,128)(2,1)S(1)}, u32[]{:S(2)}, u32[]{:S(2)}) collective-permute-start(bf16[1056,256]{1,0:T(8,128)(2,1)S(1)} %get-tuple-element.102), channel_id=1, source_target_pairs={{8,0},{10,2},{12,4},{14,6},{16,8},{18,10},{20,12},{22,14},{24,16},... | collective-permute-start | bytes 1622024 | tf_op jit(solution)/shard_map/ppermute | solution.py:37
  139.6 18.9 %collective-permute-start.34 = (bf16[1056,256]{1,0:T(8,128)(2,1)S(1)}, bf16[1056,256]{1,0:T(8,128)(2,1)S(1)}, u32[]{:S(2)}, u32[]{:S(2)}) collective-permute-start(bf16[1056,256]{1,0:T(8,128)(2,1)S(1)} %get-tuple-element.130), channel_id=1, source_target_pairs={{0,8},{2,10},{4,12},{6,14},{8,16},{10,18},{12,20},{14,22},{16,24},... | collective-permute-start | bytes 1622024 | tf_op jit(solution)/shard_map/ppermute | solution.py:37
  (24 other events, 292.6 us)
